TPU v7x, 32 devices: a whole 2x2x4 slice. The times are simulated.
32 devices in a mesh: dp: 4 (over x, core), seq: 4 (over z), tensor: 2 (over y).
Axes of the slice: x: 2, y: 2, z: 4, core: 2. Of those that a mesh axis runs over, the one named last changes fastest.
Arguments:
- memory_in: bfloat16 [8, 588, 1024], P(('dp', 'tensor'), 'seq'), may hold values from -6 to 6
- norm_gain: float32 [1024], replicated, may hold values from 0.1 to 1.9
- qkv_weight: bfloat16 [1024, 1536], replicated, may hold values from -1 to 1
- out_weight: bfloat16 [512, 1024], replicated, may hold values from -0.25 to 0.25
- key_weight: bfloat16 [1024, 1024], replicated, may hold values from -0.1875 to 0.1875
- value_weight: bfloat16 [1024, 1024], replicated, may hold values from -0.1875 to 0.1875
- shift_offsets: int32 [8, 2], P(('dp', 'tensor')), may hold values from 1 to 6
- row_order: int32 [8, 588], P('dp'), may hold values from 0 to 587, each once within a row
Outputs:
- keys: bfloat16 [8, 588, 1024], P('dp', 'tensor', 'seq')
- values: bfloat16 [8, 588, 1024], P('dp', 'tensor', 'seq')
All inputs are finite; a program needn't handle non-finite values.
Results may differ from a plain program's by a relative error of at most 0.008.
Values may be sent and summed in bfloat16 or wider, within the bound.
No kernel may reach another device: no remote copies, remote signals or barrier semaphores. Data moves between devices by JAX's collectives and lax.ppermute only.
A program may use at most 64 MiB of HBM per device.

v0:
```python
import jax
import jax.numpy as jnp
from jax import lax
from jax.sharding import PartitionSpec as P

HEADS = 16
HEAD_DIM = 32
GRID_H = 28
GRID_W = 21
WIN = 7


def shifted(block, axis, distance):
    devices = range(lax.axis_size(axis))
    route = [((i - distance) % len(devices), i) for i in devices]
    return lax.ppermute(block, axis, route)


def window_block(rolled, first_row, row_shift, col_shift, norm_gain, qkv_weight, out_weight):
    row_count = rolled.shape[0] // GRID_W
    attn_width = HEADS * HEAD_DIM
    win_rows = row_count // WIN
    win_cols = GRID_W // WIN
    x_float = rolled.astype(jnp.float32)
    row_mean = jnp.mean(x_float, axis=-1, keepdims=True)
    row_var = jnp.mean((x_float - row_mean) ** 2, axis=-1, keepdims=True)
    normed = ((x_float - row_mean) * lax.rsqrt(row_var + 1e-05) * norm_gain).astype(jnp.bfloat16)
    projected_qkv = jnp.dot(normed, qkv_weight, preferred_element_type=jnp.float32).astype(
        jnp.bfloat16
    )

    def windows(block):
        block = block.reshape(win_rows, WIN, win_cols, WIN, HEADS, HEAD_DIM)
        return block.transpose(0, 2, 4, 1, 3, 5).reshape(
            win_rows * win_cols, HEADS, WIN * WIN, HEAD_DIM
        )

    queries = windows(projected_qkv[:, :attn_width])
    keys_win = windows(projected_qkv[:, attn_width : 2 * attn_width])
    values_win = windows(projected_qkv[:, 2 * attn_width :])
    scores = jnp.einsum(
        "whqd,whkd->whqk", queries, keys_win, preferred_element_type=jnp.float32
    ) * HEAD_DIM ** (-0.5)
    row_ids = first_row + jnp.arange(row_count, dtype=jnp.int32)
    col_ids = jnp.arange(GRID_W, dtype=jnp.int32)
    wrap_row = (row_ids >= GRID_H - row_shift).astype(jnp.int32)
    wrap_col = (col_ids >= GRID_W - col_shift).astype(jnp.int32)
    labels = 2 * wrap_row[:, None] + wrap_col[None, :]
    labels = (
        labels.reshape(win_rows, WIN, win_cols, WIN)
        .transpose(0, 2, 1, 3)
        .reshape(win_rows * win_cols, WIN * WIN)
    )
    same_region = labels[:, :, None] == labels[:, None, :]
    scores = jnp.where(same_region[:, None], scores, -1000000000.0)
    weights = jax.nn.softmax(scores, axis=-1).astype(jnp.bfloat16)
    attended = jnp.einsum(
        "whqk,whkd->whqd", weights, values_win, preferred_element_type=jnp.float32
    ).astype(jnp.bfloat16)
    restored = attended.reshape(win_rows, win_cols, HEADS, WIN, WIN, HEAD_DIM)
    restored = restored.transpose(0, 3, 1, 4, 2, 5).reshape(row_count * GRID_W, attn_width)
    return (x_float + jnp.dot(restored, out_weight, preferred_element_type=jnp.float32)).astype(
        jnp.bfloat16
    )


def local(
    memory_in, norm_gain, qkv_weight, out_weight, key_weight, value_weight, shift_offsets, row_order
):
    page_count, band_rows, emb_width = memory_in.shape
    band_height = band_rows // GRID_W
    top_rows = memory_in[:, : (WIN - 1) * GRID_W]
    after_rows = shifted(top_rows, "seq", -1)
    extended = jnp.concatenate([memory_in, after_rows], axis=1)
    extended = extended.reshape(page_count, band_height + WIN - 1, GRID_W, emb_width)
    first_row = lax.axis_index("seq") * band_height

    def per_page(page_grid, shifts):
        rolled = lax.dynamic_slice_in_dim(page_grid, shifts[0], band_height, 0)
        rolled = jnp.roll(rolled, -shifts[1], axis=1).reshape(band_height * GRID_W, emb_width)
        return window_block(
            rolled, first_row, shifts[0], shifts[1], norm_gain, qkv_weight, out_weight
        )

    memory = jax.vmap(per_page)(extended, shift_offsets)
    n_seq = lax.axis_size("seq")
    n_tensor = lax.axis_size("tensor")
    kv_width = key_weight.shape[1]
    own_cols = kv_width // n_seq
    group_pages = n_tensor * page_count
    all_rows = row_order.shape[1]
    pos_dev = all_rows // n_tensor
    first_col = lax.axis_index("seq") * own_cols
    both_weight = jnp.concatenate(
        [
            lax.dynamic_slice_in_dim(key_weight, first_col, own_cols, 1),
            lax.dynamic_slice_in_dim(value_weight, first_col, own_cols, 1),
        ],
        axis=1,
    )
    own_order = lax.dynamic_slice_in_dim(row_order, lax.axis_index("tensor") * pos_dev, pos_dev, 1)
    page_ids = jnp.arange(group_pages, dtype=jnp.int32)
    tensor_pos = (page_ids // page_count)[:, None]
    page_pos = (page_ids % page_count)[:, None]
    band_ids = own_order // band_rows
    within = own_order % band_rows
    flat_index = (
        ((band_ids * n_tensor + tensor_pos) * page_count + page_pos) * band_rows + within
    ).reshape(-1)
    empty_rows = jnp.zeros((group_pages * pos_dev, emb_width), jnp.bfloat16)
    piece_flat = lax.all_gather(memory[None], ("seq", "tensor"), axis=0, tiled=True).reshape(
        -1, emb_width
    )
    inside = (flat_index >= 0) & (flat_index < piece_flat.shape[0])
    taken_rows = jnp.take(piece_flat, jnp.clip(flat_index, 0, piece_flat.shape[0] - 1), axis=0)
    picked = jnp.where(inside[:, None], taken_rows, empty_rows)
    projected = jnp.dot(picked, both_weight, preferred_element_type=jnp.float32)
    key_out = projected[:, :own_cols].astype(jnp.bfloat16).reshape(group_pages, pos_dev, own_cols)
    value_out = projected[:, own_cols:].astype(jnp.bfloat16).reshape(group_pages, pos_dev, own_cols)
    return (key_out, value_out)


def solution(mesh):
    placed = (
        P(("dp", "tensor"), "seq", None),
        P(),
        P(),
        P(),
        P(),
        P(),
        P(("dp", "tensor"), None),
        P("dp", None),
    )
    return jax.shard_map(
        local,
        mesh=mesh,
        in_specs=placed,
        out_specs=(P("dp", "tensor", "seq"), P("dp", "tensor", "seq")),
        check_vma=False,
    )
```

profile of v0, /device:TPU:0, one launch (start us, length us, event | category | flops | bytes accessed | tf_op | source)
XLA Modules:
  0.0 141.8 jit_solution(3748923475299018411)
XLA Ops:
  7.2 1.1 slice.28
  8.3 5.1 %collective-permute-start = (bf16[1,126,1024]{2,1,0:T(8,128)(2,1)S(1)}, bf16[1,126,1024]{2,1,0:T(8,128)(2,1)}, u32[]{:S(2)}, u32[]{:S(2)}) collective-permute-start(bf16[1,126,1024]{2,1,0:T(8,128)(2,1)S(1)} %slice.28), channel_id=1, source_target_pairs={{2,0},{4,2},{6,4},{0,6},{3,1},{5,3},{7,5},{1,7},{10,8},{12,10},{14... | collective-permute-start | bytes 774152 | tf_op jit(solution)/shard_map/ppermute | solution.py:16
  13.4 1.3 fusion.38
  19.0 2.0 %pad_maximum_fusion = bf16[1,273,1024]{2,1,0:T(8,128)(2,1)} fusion(bf16[1,126,1024]{2,1,0:T(8,128)(2,1)} %collective-permute-done, bf16[1,147,1024]{2,1,0:T(8,128)(2,1)} %param.8), kind=kLoop, calls=%fused_computation.34 | loop fusion | flops 1118208 | bytes 1118208 | tf_op jit(solution)/shard_map/concatenate | solution.py:74
  21.0 4.2 %reshape.389 = bf16[1,13,21,1024]{3,0,2,1:T(2,128)(2,1)} reshape(bf16[1,273,1024]{2,1,0:T(8,128)(2,1)} %pad_maximum_fusion) | data formatting | bytes 1118208 | tf_op jit(solution)/shard_map/reshape | solution.py:75
  25.2 1.7 %constant_dynamic-slice_fusion.2 = bf16[1,7,21,1024]{3,0,2,1:T(2,128)(2,1)S(1)} fusion(bf16[1,13,21,1024]{3,0,2,1:T(2,128)(2,1)} %reshape.389, s32[]{:T(128)} %bitcast.1), kind=kLoop, calls=%fused_computation.56 | loop fusion | bytes 602116 | tf_op jit(solution)/shard_map/vmap()/gather | solution.py:79
  26.9 4.2 %fusion.33 = (f32[7,21]{1,0:T(8,128)S(1)}, f32[7,21,1024]{2,1,0:T(8,128)}, f32[1,7,21,1024]{3,0,2,1:T(1,128)}) fusion(s32[]{:T(128)} %bitcast.3, bf16[1,7,21,1024]{3,0,2,1:T(2,128)(2,1)S(1)} %constant_dynamic-slice_fusion.2), kind=kLoop, calls=%fused_computation.62 | loop fusion | flops 451437 | bytes 1505872 | tf_op jit(solution)/shard_map/vmap()/reduce_sum | solution.py:25
  31.2 3.1 %fusion.21 = f32[147]{0:T(256)S(1)} fusion(f32[1,7,21,1024]{3,0,2,1:T(1,128)} %get-tuple-element.34, f32[147]{0:T(256)S(1)} %div.29), kind=kLoop, calls=%fused_computation.32 | loop fusion | flops 451437 | bytes 603288 | tf_op jit(solution)/shard_map/vmap()/reduce_sum | solution.py:26
  34.3 2.0 %reshape.373 = f32[147,1024]{1,0:T(8,128)} reshape(f32[7,21,1024]{2,1,0:T(8,128)} %get-tuple-element.31) | data formatting | bytes 1204224 | tf_op jit(solution)/shard_map/vmap()/convert_element_type | solution.py:24
  36.3 1.8 %fusion.1 = bf16[1,147,1536]{2,1,0:T(8,128)(2,1)S(1)} fusion(bf16[1024,1536]{1,0:T(8,128)(2,1)S(1)} %copy-done, f32[147,1024]{1,0:T(8,128)} %reshape.373, f32[1024]{0:T(1024)S(1)} %copy-done.1, f32[147]{0:T(256)S(1)} %add_rsqrt_fusion, f32[147]{0:T(256)S(1)} %div.29), kind=kOutput, calls=%fused_computation.3 | convolution fusion | flops 463249920 | bytes 4204696 | tf_op jit(solution)/shard_map/vmap()/dot_general | solution.py:28
  38.8 2.1 %reshape.306 = bf16[1,1,7,3,7,16,32]{6,5,4,3,2,1,0:T(8,128)(2,1)} reshape(bf16[1,147,512]{2,1,0:T(8,128)(2,1)} %get-tuple-element.37) | data formatting | bytes 301056 | tf_op jit(solution)/shard_map/vmap()/reshape | solution.py:33
  40.9 1.9 %copy.29 = bf16[1,1,7,3,7,16,32]{6,5,4,2,3,1,0:T(8,128)(2,1)} copy(bf16[1,1,7,3,7,16,32]{6,5,4,3,2,1,0:T(8,128)(2,1)} %reshape.306) | data formatting | bytes 301056 | tf_op jit(solution)/shard_map/vmap()/reshape | solution.py:33
  42.9 1.1 reshape.308
  44.0 1.1 copy.30
  45.1 1.6 %fusion.4 = f32[3,16,49,49]{2,3,1,0:T(8,128)S(1)} fusion(bf16[3,16,49,32]{3,1,2,0:T(8,128)(2,1)S(1)} %bitcast.39, bf16[3,16,49,32]{3,1,2,0:T(8,128)(2,1)} %bitcast.38, pred[3,49,49]{1,2,0:T(8,128)(4,1)S(1)} %broadcast_compare_fusion), kind=kOutput, calls=%fused_computation.7 | convolution fusion | flops 7606368 | bytes 769251 | tf_op jit(solution)/shard_map/vmap(whqd,whkd->whqk)/dot_general | solution.py:41
  46.7 1.1 copy-done.3
  47.8 1.0 fusion.39
  48.8 1.2 reshape.310
  49.9 1.9 %copy.33 = bf16[1,1,7,3,7,16,32]{6,5,4,2,3,1,0:T(8,128)(2,1)} copy(bf16[1,1,7,3,7,16,32]{6,5,4,3,2,1,0:T(8,128)(2,1)} %reshape.310) | data formatting | bytes 301056 | tf_op jit(solution)/shard_map/vmap()/reshape | solution.py:33
  51.9 2.6 %convolution_convert_fusion.2 = bf16[3,16,49,32]{2,3,1,0:T(8,128)(2,1)S(1)} fusion(bf16[3,16,49,32]{3,1,2,0:T(8,128)(2,1)} %bitcast.40, f32[3,16,49]{2,1,0:T(8,128)} %fusion.39, f32[3,16,49,49]{2,3,1,0:T(8,128)} %copy-done.3), kind=kOutput, calls=%fused_computation.11 | convolution fusion | flops 7799280 | bytes 771456 | tf_op jit(solution)/shard_map/vmap(whqk,whkd->whqd)/dot_general | solution.py:57
  54.4 1.3 copy.36
  55.8 1.9 %copy.37 = bf16[1,1,7,3,7,16,32]{6,5,4,3,2,1,0:T(8,128)(2,1)} copy(bf16[1,1,7,3,7,16,32]{6,5,4,2,3,1,0:T(8,128)(2,1)} %bitcast.37) | data formatting | bytes 301056 | tf_op jit(solution)/shard_map/vmap()/transpose | solution.py:61
  57.7 1.6 %reshape.313 = bf16[147,512]{1,0:T(8,128)(2,1)S(1)} reshape(bf16[1,1,7,3,7,16,32]{6,5,4,3,2,1,0:T(8,128)(2,1)} %copy.37) | data formatting | bytes 301056 | tf_op jit(solution)/shard_map/reshape.40
  59.3 2.5 %fusion.10 = bf16[1,147,1024]{2,1,0:T(8,128)(2,1)} fusion(f32[147,1024]{1,0:T(8,128)} %reshape.373, bf16[147,512]{1,0:T(8,128)(2,1)S(1)} %reshape.313, bf16[512,1024]{1,0:T(8,128)(2,1)} %param.11), kind=kOutput, calls=%fused_computation.19 | convolution fusion | flops 154441728 | bytes 2102272 | tf_op jit(solution)/shard_map/vmap()/dot_general | solution.py:62
  62.2 2.3 %constant_dynamic-slice_fusion = (bf16[1024,256]{1,0:T(8,128)(2,1)}, bf16[1024,256]{1,0:T(8,128)(2,1)}) fusion(bf16[1024,1024]{1,0:T(8,128)(2,1)} %param.13, s32[]{:T(128)S(6)} %select_n.85, bf16[1024,1024]{1,0:T(8,128)(2,1)} %param.12), kind=kLoop, calls=%fused_computation.54 | loop fusion | bytes 2097156 | tf_op jit(solution)/shard_map/dynamic_slice | solution.py:97
  64.5 52.8 %all-gather.4.cloned.1.call-done = bf16[8,147,1024]{2,1,0:T(8,128)(2,1)} async-done(((bf16[1,147,1024]{2,1,0:T(8,128)(2,1)}), bf16[8,147,1024]{2,1,0:T(8,128)(2,1)}) %all-gather.4.cloned.1.call-update) | async-done | bytes 2408464 | tf_op jit(solution)/shard_map/all_gather | solution.py:111
  117.3 3.8 %reshape.388 = bf16[1176,1024]{1,0:T(8,128)(2,1)} reshape(bf16[8,147,1024]{2,1,0:T(8,128)(2,1)} %all-gather.4.cloned.1.call-done) | data formatting | bytes 4816896
  121.2 6.6 %gather_fusion = bf16[588,1024]{1,0:T(8,128)(2,1)} fusion(bf16[1176,1024]{1,0:T(8,128)(2,1)} %reshape.388, s32[1024]{0:T(1024)S(1)} %pad_clamp_fusion), kind=kCustom, calls=%fused_computation | custom fusion | bytes 2410800 | tf_op jit(solution)/shard_map/jit(_take)/gather | solution.py:115
  127.8 2.4 %convolution_convert_fusion.1 = bf16[588,512]{1,0:T(8,128)(2,1)S(1)} fusion(bf16[588,1024]{1,0:T(8,128)(2,1)} %gather_fusion, pred[588]{0:T(1024)(128)(4,1)S(1)} %compare_and_fusion.1, pred[588]{0:T(1024)(128)(4,1)S(1)} %and.45, bf16[1024,256]{1,0:T(8,128)(2,1)} %get-tuple-element.42, bf16[1024,256]{1,0:T(8,128)(2,1)} %get-tuple-element.43), kind=kOutput, calls=%fused_computation.9 | convolution fusion | flops 620165120 | bytes 2856088 | tf_op jit(solution)/shard_map/dot_general | solution.py:117
  131.0 1.0 reshape.315
  132.1 0.9 copy.38
  133.0 1.0 reshape.316
  (29 shorter events, 3.4 us)
Async XLA Ops:
  7.2 29.2 %copy-start = (bf16[1024,1536]{1,0:T(8,128)(2,1)S(1)}, bf16[1024,1536]{1,0:T(8,128)(2,1)}, u32[]{:S(2)}) copy-start(bf16[1024,1536]{1,0:T(8,128)(2,1)} %param.10) | copy-start | bytes 9437188
  7.2 110.1 %all-gather.4.cloned.1.call-start = ((), (), s32[]{:S(2)}) async-start(), calls=%async_computation | async-start | bytes 2801664 | tf_op jit(solution)/shard_map/all_gather | solution.py:111
  8.3 10.7 %collective-permute-start = (bf16[1,126,1024]{2,1,0:T(8,128)(2,1)S(1)}, bf16[1,126,1024]{2,1,0:T(8,128)(2,1)}, u32[]{:S(2)}, u32[]{:S(2)}) collective-permute-start(bf16[1,126,1024]{2,1,0:T(8,128)(2,1)S(1)} %slice.28), channel_id=1, source_target_pairs={{2,0},{4,2},{6,4},{0,6},{3,1},{5,3},{7,5},{1,7},{10,8},{12,10},{14... | collective-permute-start | bytes 774152 | tf_op jit(solution)/shard_map/ppermute | solution.py:16
  31.1 5.2 %copy-start.1 = (f32[1024]{0:T(1024)S(1)}, f32[1024]{0:T(1024)}, u32[]{:S(2)}) copy-start(f32[1024]{0:T(1024)} %param.9) | copy-start | bytes 12292
  46.7 1.1 copy-start.3
  59.3 2.5 %copy-start.2 = (s32[2,588]{1,0:T(2,128)S(1)}, s32[2,588]{1,0:T(2,128)}, u32[]{:S(2)}) copy-start(s32[2,588]{1,0:T(2,128)} %param.15) | copy-start | bytes 14116
Sparse Core Ops, SparseCore 0:
  62.0 55.3 all-gather.3
where the time goes:
time: 143 us; the launch traced here: 142 us
  waiting for transfers between devices  52.8 us (37%)
  local copies, waits for them, and re-layouts  44.4 us (31%)
  between operations  18.1 us (13%)
  matrix products  10.8 us (8%)
  other arithmetic  10.5 us (7%)
  starting transfers between devices  5.14 us (4%)
    all_gather x1, waiting for transfers between devices, local(): lax.all_gather(memory[None], ('seq', 'tensor'), axis=0, tiled=True)  52.8 us
    reshape x6, local copies, waits for them, and re-layouts, windows(): block = block.reshape(win_rows, WIN, win_cols, WIN, HEADS, HEAD_DIM)  9.38 us
    unnamed x11, local copies, waits for them, and re-layouts  6.84 us
    gather x1, local copies, waits for them, and re-layouts, local(): jnp.take(piece_flat, jnp.clip(flat_index, 0, piece_flat.shape[0] - 1), ax...  6.59 us
    ppermute x1, starting transfers between devices, shifted(): return lax.ppermute(block, axis, route)  5.1 us
    reshape x1, local copies, waits for them, and re-layouts, local(): extended.reshape(page_count, band_height + WIN - 1, GRID_W, emb_width)  4.21 us
    reduce_sum x1, other arithmetic, window_block(): row_mean = jnp.mean(x_float, axis=-1, keepdims=True)  4.21 us
    reduce_sum x1, other arithmetic, window_block(): row_var = jnp.mean((x_float - row_mean) ** 2, axis=-1, keepdims=True)  3.09 us
  transfers between devices with their start and end apart: 2, of which 2 were waited for; matrix products, arithmetic and copies ran while one was open for 3% of the time, Pallas kernels for 0%

commit v1 on v0

v1 whole, which is shorter than its diff:
```python
import functools

import jax
import jax.numpy as jnp
from jax import lax
from jax.experimental import pallas as pl
from jax.experimental.pallas import tpu as pltpu
from jax.sharding import PartitionSpec as P

HEADS = 16
HEAD_DIM = 32
GRID_H = 28
GRID_W = 21
WIN = 7

GROUP = 8
VMEM_LIMIT = 48 * 1024 * 1024


def rotated(block, axis, distance):
    devices = lax.axis_size(axis)
    return lax.ppermute(block, axis, [(i, (i + distance) % devices) for i in range(devices)])


def dot(a, b):
    return jnp.dot(a, b, preferred_element_type=jnp.float32)


def one_hot(cond):
    return jnp.where(cond, 1.0, 0.0).astype(jnp.bfloat16)


def encode_kernel(
    n_seq, place, shifts, own_ref, halo_ref, gain_ref, qkv_ref, out_ref, key_ref, value_ref, *sent
):
    band_rows = own_ref.shape[0]
    halo_rows = halo_ref.shape[0]
    emb = own_ref.shape[1]
    rows = -(-band_rows // 16) * 16
    attn = HEADS * HEAD_DIM
    seq = place[0]
    row_shift, col_shift = shifts[0, 0], shifts[0, 1]

    cell = lax.broadcasted_iota(jnp.int32, (rows, 1), 0)
    cell_row = cell // GRID_W
    cell_col = cell - cell_row * GRID_W
    from_col = cell_col + col_shift
    from_col = jnp.where(from_col >= GRID_W, from_col - GRID_W, from_col)
    source = jnp.where(cell < band_rows, (cell_row + row_shift) * GRID_W + from_col, -1)
    take_own = one_hot(source == lax.broadcasted_iota(jnp.int32, (rows, band_rows), 1))
    take_halo = one_hot(source - band_rows == lax.broadcasted_iota(jnp.int32, (rows, halo_rows), 1))
    rolled = dot(take_own, own_ref[...]) + dot(take_halo, halo_ref[...])

    mean = jnp.mean(rolled, axis=-1, keepdims=True)
    centred = rolled - mean
    variance = jnp.mean(centred * centred, axis=-1, keepdims=True)
    normed = (centred * lax.rsqrt(variance + 1e-05) * gain_ref[...]).astype(jnp.bfloat16)
    qkv = dot(normed, qkv_ref[...]).astype(jnp.bfloat16)

    def marks(index):
        row = index // GRID_W
        col = index - row * GRID_W
        wrap_row = (seq * WIN + row >= GRID_H - row_shift).astype(jnp.int32)
        wrap_col = (col >= GRID_W - col_shift).astype(jnp.int32)
        return jnp.where(index < band_rows, (col // WIN) * 4 + 2 * wrap_row + wrap_col, -1)

    same = marks(cell) == marks(lax.broadcasted_iota(jnp.int32, (1, rows), 1))
    same = jnp.concatenate([same.astype(jnp.int32)] * GROUP, axis=0) != 0

    width = GROUP * HEAD_DIM
    lane_head = lax.broadcasted_iota(jnp.int32, (1, width), 1) // HEAD_DIM
    parts = []
    for g in range(HEADS // GROUP):
        at = g * width
        q = qkv[:, at : at + width]
        k = qkv[:, attn + at : attn + at + width]
        v = qkv[:, 2 * attn + at : 2 * attn + at + width]
        stacked = jnp.concatenate(
            [jnp.where(lane_head == h, q, jnp.zeros_like(q)) for h in range(GROUP)], axis=0
        )
        scores = lax.dot_general(
            stacked, k, (((1,), (1,)), ((), ())), preferred_element_type=jnp.float32
        )
        scores = jnp.where(same, scores * HEAD_DIM ** (-0.5), -1000000000.0)
        scores = jnp.exp(scores - jnp.max(scores, axis=-1, keepdims=True))
        total = jnp.sum(scores, axis=-1, keepdims=True)
        weights = (scores * (1.0 / total)).astype(jnp.bfloat16)
        mixed = dot(weights, v)
        part = jnp.zeros((rows, width), jnp.float32)
        for h in range(GROUP):
            part = jnp.where(lane_head == h, mixed[h * rows : (h + 1) * rows], part)
        parts.append(part.astype(jnp.bfloat16))
    attended = jnp.concatenate(parts, axis=1)
    memory = (rolled + dot(attended, out_ref[...])).astype(jnp.bfloat16)

    own_cols = key_ref.shape[1] // n_seq
    for d in range(n_seq):
        to = lax.rem(seq + d, n_seq)
        cols = pl.ds(pl.multiple_of(to * own_cols, own_cols), own_cols)
        sent[d][:, :own_cols] = dot(memory, key_ref[:, cols])[:band_rows].astype(jnp.bfloat16)
        sent[d][:, own_cols:] = dot(memory, value_ref[:, cols])[:band_rows].astype(jnp.bfloat16)


def select_kernel(n_seq, first, count, place, order_ref, *refs):
    held, outs = refs[:n_seq], refs[n_seq:]
    band_rows = held[0].shape[0]
    seq, tensor = place[0], place[1]
    n_tensor = order_ref.shape[0]
    pos = order_ref.shape[1]
    for i in range(count):
        order = order_ref[lax.rem(tensor + first + i, n_tensor)]
        total = None
        for d in range(n_seq):
            band = lax.rem(seq - d + n_seq, n_seq)
            pick = one_hot(
                order - band * band_rows == lax.broadcasted_iota(jnp.int32, (pos, band_rows), 1)
            )
            term = dot(pick, held[d][...])
            total = term if total is None else total + term
        outs[i][...] = total.astype(jnp.bfloat16)


def join_kernel(place, *refs):
    blocks, (key_out, value_out) = refs[:-2], refs[-2:]
    n_tensor = len(blocks)
    own_cols = key_out.shape[-1]
    for d in range(n_tensor):
        page = lax.rem(place[1] - d + n_tensor, n_tensor)
        key_out[page] = blocks[d][:, :own_cols]
        value_out[page] = blocks[d][:, own_cols:]


def call(kernel, out_shape, n_scalar, n_vmem, flops, moved):
    smem = pl.BlockSpec(memory_space=pltpu.SMEM)
    vmem = pl.BlockSpec(memory_space=pltpu.VMEM)
    return pl.pallas_call(
        kernel,
        out_shape=out_shape,
        in_specs=[smem] * n_scalar + [vmem] * n_vmem,
        out_specs=jax.tree.map(lambda _: vmem, out_shape),
        compiler_params=pltpu.CompilerParams(vmem_limit_bytes=VMEM_LIMIT),
        cost_estimate=pl.CostEstimate(flops=flops, bytes_accessed=moved, transcendentals=0),
    )


def local(
    memory_in, norm_gain, qkv_weight, out_weight, key_weight, value_weight, shift_offsets, row_order
):
    _, band_rows, emb = memory_in.shape
    n_seq = lax.axis_size("seq")
    n_tensor = lax.axis_size("tensor")
    own_cols = key_weight.shape[1] // n_seq
    pos = row_order.shape[1] // n_tensor
    place = jnp.stack([lax.axis_index("seq"), lax.axis_index("tensor")]).astype(jnp.int32)
    own = memory_in[0]
    halo = rotated(own[: (WIN - 1) * GRID_W], "seq", -1)
    order = lax.dynamic_index_in_dim(row_order, lax.axis_index("tensor"), 0, False)
    order = order.reshape(n_tensor, pos, 1)

    block = jax.ShapeDtypeStruct((band_rows, 2 * own_cols), jnp.bfloat16)
    sent = call(
        functools.partial(encode_kernel, n_seq), [block] * n_seq, 2, 7, 2_500_000_000, 10_000_000
    )(
        place, shift_offsets, own, halo, norm_gain.reshape(1, emb), qkv_weight, out_weight,
        key_weight, value_weight,
    )
    held = [rotated(sent[d], "seq", d) if d else sent[0] for d in range(n_seq)]

    piece = jax.ShapeDtypeStruct((pos, 2 * own_cols), jnp.bfloat16)
    away = call(
        functools.partial(select_kernel, n_seq, 1, n_tensor - 1),
        [piece] * (n_tensor - 1), 1, 1 + n_seq, 600_000_000, 1_000_000,
    )(place, order, *held)
    arrived = [rotated(away[d - 1], "tensor", d) for d in range(1, n_tensor)]
    kept = call(
        functools.partial(select_kernel, n_seq, 0, 1),
        [piece], 1, 1 + n_seq, 600_000_000, 1_000_000,
    )(place, order, *held)
    out = jax.ShapeDtypeStruct((n_tensor, pos, own_cols), jnp.bfloat16)
    key_out, value_out = call(join_kernel, [out, out], 1, n_tensor, 0, 2_000_000)(
        place, kept[0], *arrived
    )
    return key_out, value_out


def solution(mesh):
    placed = (
        P(("dp", "tensor"), "seq", None),
        P(),
        P(),
        P(),
        P(),
        P(),
        P(("dp", "tensor"), None),
        P("dp", None),
    )
    return jax.shard_map(
        local,
        mesh=mesh,
        in_specs=placed,
        out_specs=(P("dp", "tensor", "seq"), P("dp", "tensor", "seq")),
        check_vma=False,
    )
```

time: 143 us -> 51.7 us (0.36)
  the two profiles are of different devices: /device:TPU:0 before, /device:TPU:10 now
where the time goes in v1:
time: 51.7 us; the launch traced here: 51.4 us
  waiting for transfers between devices  24.9 us (48%)
  Pallas kernels  8.97 us (17%)
  starting transfers between devices  8.55 us (17%)
  local copies, waits for them, and re-layouts  8.22 us (16%)
  between operations  0.69 us (1%)
    ppermute x5, waiting for transfers between devices, rotated(): lax.ppermute(block, axis, [(i, (i + distance) % devices) for i in range(d...  24.9 us
    ppermute x5, starting transfers between devices, rotated(): lax.ppermute(block, axis, [(i, (i + distance) % devices) for i in range(d...  8.55 us
    pallas_call x1, Pallas kernels, local(): call(functools.partial(encode_kernel, n_seq), [block] * n_seq, 2, 7, 2500...  6.22 us
    unnamed x12, local copies, waits for them, and re-layouts  5.13 us
    pallas_call x2, local copies, waits for them, and re-layouts, local(): call(join_kernel, [out, out], 1, n_tensor, 0, 2000000)  1.9 us
    pallas_call x1, Pallas kernels, local(): call(functools.partial(select_kernel, n_seq, 0, 1), [piece], 1, 1 + n_seq...  1.08 us
    pallas_call x1, Pallas kernels, local(): call(functools.partial(select_kernel, n_seq, 1, n_tensor - 1), [piece] *...  1.08 us
  transfers between devices with their start and end apart: 5, of which 5 were waited for; matrix products, arithmetic and copies ran while one was open for 1% of the time, Pallas kernels for 2%

profile of v1, /device:TPU:10, one launch (start us, length us, event | category | flops | bytes accessed | tf_op | source)
XLA Modules:
  0.0 51.4 jit_solution(9704927163517905095)
XLA Ops:
  0.6 0.0 copy-start
  0.6 1.0 %slice_bitcast_fusion = bf16[126,1024]{1,0:T(8,128)(2,1)S(1)} fusion(bf16[1,147,1024]{2,1,0:T(8,128)(2,1)} %param.8), kind=kLoop, calls=%fused_computation | loop fusion | bytes 516096 | tf_op jit(solution)/shard_map/slice | solution.py:156
  1.6 0.5 collective-permute-start
  2.1 0.1 pad_add_fusion.place
  2.2 7.5 %collective-permute-done.halo_ref = bf16[126,1024]{1,0:T(8,128)(2,1)S(1)} collective-permute-done((bf16[126,1024]{1,0:T(8,128)(2,1)S(1)}, bf16[126,1024]{1,0:T(8,128)(2,1)S(1)}, u32[]{:S(2)}, u32[]{:S(2)}) %collective-permute-start) | collective-permute-done | bytes 258080 | tf_op jit(solution)/shard_map/ppermute | solution.py:22
  9.7 0.0 copy-start.1
  9.7 1.0 %copy-done.1 = bf16[1,147,1024]{2,1,0:T(8,128)(2,1)S(1)} copy-done((bf16[1,147,1024]{2,1,0:T(8,128)(2,1)S(1)}, bf16[1,147,1024]{2,1,0:T(8,128)(2,1)}, u32[]{:S(2)}) %copy-start.1) | copy-done | bytes 301080
  10.7 0.0 copy-start.2
  10.7 1.6 %copy-done.2 = bf16[1024,1024]{1,0:T(8,128)(2,1)S(1)} copy-done((bf16[1024,1024]{1,0:T(8,128)(2,1)S(1)}, bf16[1024,1024]{1,0:T(8,128)(2,1)}, u32[]{:S(2)}) %copy-start.2) | copy-done | bytes 2097176
  12.3 0.0 copy-start.3
  12.3 1.2 %copy-done.3 = bf16[512,1024]{1,0:T(8,128)(2,1)S(1)} copy-done((bf16[512,1024]{1,0:T(8,128)(2,1)S(1)}, bf16[512,1024]{1,0:T(8,128)(2,1)}, u32[]{:S(2)}) %copy-start.3) | copy-done | bytes 1048600
  13.5 0.0 copy-start.4
  13.5 0.7 %copy-done.4 = f32[1024]{0:T(1024)S(1)} copy-done((f32[1024]{0:T(1024)S(1)}, f32[1024]{0:T(1024)}, u32[]{:S(2)}) %copy-start.4) | copy-done | bytes 4120
  14.2 0.0 copy-start.5
  14.2 0.7 %copy-done.5 = s32[1,2]{1,0:T(1,128)S(1)} copy-done((s32[1,2]{1,0:T(1,128)S(1)}, s32[1,2]{1,0:T(1,128)}, u32[]{:S(2)}) %copy-start.5) | copy-done | bytes 32
  14.8 6.2 %shard_map.95 = (bf16[147,512]{1,0:T(8,128)(2,1)S(1)}, bf16[147,512]{1,0:T(8,128)(2,1)S(1)}, bf16[147,512]{1,0:T(8,128)(2,1)S(1)}, bf16[147,512]{1,0:T(8,128)(2,1)S(1)}) custom-call(s32[2]{0:T(128)S(1)} %pad_add_fusion.place, s32[1,2]{1,0:T(1,128)S(1)} %copy-done.5, bf16[147,1024]{1,0:T(8,128)(2,1)S(1)} %bitcast.6, ...), custom_call_target="tpu_custom_call" | custom-call | flops 2500000000 | bytes 10000000 | tf_op jit(solution)/shard_map/pallas_call | solution.py:161
  21.1 1.6 %collective-permute-start.1 = (bf16[147,512]{1,0:T(8,128)(2,1)S(1)}, bf16[147,512]{1,0:T(8,128)(2,1)S(1)}, u32[]{:S(2)}, u32[]{:S(2)}) collective-permute-start(bf16[147,512]{1,0:T(8,128)(2,1)S(1)} %get-tuple-element.7), channel_id=1, source_target_pairs={{0,2},{2,4},{4,6},{6,0},{1,3},{3,5},{5,7},{7,1},{8,10},{10,12},{12... | collective-permute-start | bytes 451592 | tf_op jit(solution)/shard_map/ppermute | solution.py:22
  22.7 2.9 %collective-permute-start.2 = (bf16[147,512]{1,0:T(8,128)(2,1)S(1)}, bf16[147,512]{1,0:T(8,128)(2,1)S(1)}, u32[]{:S(2)}, u32[]{:S(2)}) collective-permute-start(bf16[147,512]{1,0:T(8,128)(2,1)S(1)} %get-tuple-element.8), channel_id=1, source_target_pairs={{0,4},{2,6},{4,0},{6,2},{1,5},{3,7},{5,1},{7,3},{8,12},{10,14},{12... | collective-permute-start | bytes 451592 | tf_op jit(solution)/shard_map/ppermute | solution.py:22
  25.6 1.9 %collective-permute-start.3 = (bf16[147,512]{1,0:T(8,128)(2,1)S(1)}, bf16[147,512]{1,0:T(8,128)(2,1)S(1)}, u32[]{:S(2)}, u32[]{:S(2)}) collective-permute-start(bf16[147,512]{1,0:T(8,128)(2,1)S(1)} %get-tuple-element.9), channel_id=1, source_target_pairs={{0,6},{2,0},{4,2},{6,4},{1,7},{3,1},{5,3},{7,5},{8,14},{10,8},{12,... | collective-permute-start | bytes 451592 | tf_op jit(solution)/shard_map/ppermute | solution.py:22
  27.5 0.0 copy-done
  27.6 0.2 reshape.14.order_ref
  27.8 5.0 %collective-permute-done.1.refs_1_ = bf16[147,512]{1,0:T(8,128)(2,1)S(1)} collective-permute-done((bf16[147,512]{1,0:T(8,128)(2,1)S(1)}, bf16[147,512]{1,0:T(8,128)(2,1)S(1)}, u32[]{:S(2)}, u32[]{:S(2)}) %collective-permute-start.1) | collective-permute-done | bytes 150560 | tf_op jit(solution)/shard_map/ppermute | solution.py:22
  32.8 2.7 %collective-permute-done.2.refs_2_ = bf16[147,512]{1,0:T(8,128)(2,1)S(1)} collective-permute-done((bf16[147,512]{1,0:T(8,128)(2,1)S(1)}, bf16[147,512]{1,0:T(8,128)(2,1)S(1)}, u32[]{:S(2)}, u32[]{:S(2)}) %collective-permute-start.2) | collective-permute-done | bytes 150560 | tf_op jit(solution)/shard_map/ppermute | solution.py:22
  35.5 3.2 %collective-permute-done.3.refs_3_ = bf16[147,512]{1,0:T(8,128)(2,1)S(1)} collective-permute-done((bf16[147,512]{1,0:T(8,128)(2,1)S(1)}, bf16[147,512]{1,0:T(8,128)(2,1)S(1)}, u32[]{:S(2)}, u32[]{:S(2)}) %collective-permute-start.3) | collective-permute-done | bytes 150560 | tf_op jit(solution)/shard_map/ppermute | solution.py:22
  38.7 1.1 %shard_map.97 = bf16[294,512]{1,0:T(8,128)(2,1)S(1)} custom-call(s32[2]{0:T(128)S(1)} %pad_add_fusion.place, s32[2,294,1]{2,1,0:T(8,128)S(1)} %reshape.14.order_ref, bf16[147,512]{1,0:T(8,128)(2,1)S(1)} %get-tuple-element.6.refs_0_, bf16[147,512]{1,0:T(8,128)(2,1)S(1)} %collective-permute-done.1.refs_1_, ...), custom_call_target="tpu_custom_call" | custom-call | flops 600000000 | bytes 1000000 | tf_op jit(solution)/shard_map/pallas_call | solution.py:170
  39.8 1.6 %collective-permute-start.4 = (bf16[294,512]{1,0:T(8,128)(2,1)S(1)}, bf16[294,512]{1,0:T(8,128)(2,1)S(1)}, u32[]{:S(2)}, u32[]{:S(2)}) collective-permute-start(bf16[294,512]{1,0:T(8,128)(2,1)S(1)} %shard_map.97), channel_id=1, source_target_pairs={{0,1},{1,0},{2,3},{3,2},{4,5},{5,4},{6,7},{7,6},{8,9},{9,8},{10,11... | collective-permute-start | bytes 903176 | tf_op jit(solution)/shard_map/ppermute | solution.py:22
  41.3 1.1 %shard_map.96.refs_0_ = bf16[294,512]{1,0:T(8,128)(2,1)S(1)} custom-call(s32[2]{0:T(128)S(1)} %pad_add_fusion.place, s32[2,294,1]{2,1,0:T(8,128)S(1)} %reshape.14.order_ref, bf16[147,512]{1,0:T(8,128)(2,1)S(1)} %get-tuple-element.6.refs_0_, bf16[147,512]{1,0:T(8,128)(2,1)S(1)} %collective-permute-done.1.refs_1_, ...), custom_call_target="tpu_custom_call" | custom-call | flops 600000000 | bytes 1000000 | tf_op jit(solution)/shard_map/pallas_call | solution.py:175
  42.4 6.5 %collective-permute-done.4.refs_1_ = bf16[294,512]{1,0:T(8,128)(2,1)S(1)} collective-permute-done((bf16[294,512]{1,0:T(8,128)(2,1)S(1)}, bf16[294,512]{1,0:T(8,128)(2,1)S(1)}, u32[]{:S(2)}, u32[]{:S(2)}) %collective-permute-start.4) | collective-permute-done | bytes 301088 | tf_op jit(solution)/shard_map/ppermute | solution.py:22
  48.9 0.6 %shard_map.98 = (bf16[2,294,256]{2,1,0:T(8,128)(2,1)S(1)}, bf16[2,294,256]{2,1,0:T(8,128)(2,1)S(1)}) custom-call(s32[2]{0:T(128)S(1)} %pad_add_fusion.place, bf16[294,512]{1,0:T(8,128)(2,1)S(1)} %shard_map.96.refs_0_, bf16[294,512]{1,0:T(8,128)(2,1)S(1)} %collective-permute-done.4.refs_1_), custom_call_target="tpu_custom_call" | custom-call | bytes 2000000 | tf_op jit(solution)/shard_map/pallas_call | solution.py:180
  49.5 0.9 %copy.14 = bf16[2,294,256]{2,0,1:T(2,128)(2,1)} copy(bf16[2,294,256]{2,1,0:T(8,128)(2,1)S(1)} %get-tuple-element.12) | data formatting | bytes 602112 | tf_op jit(solution)/shard_map/pallas_call | solution.py:180
  50.5 0.9 %copy.15 = bf16[2,294,256]{2,0,1:T(2,128)(2,1)} copy(bf16[2,294,256]{2,1,0:T(8,128)(2,1)S(1)} %get-tuple-element.13) | data formatting | bytes 602112 | tf_op jit(solution)/shard_map/pallas_call | solution.py:180
  (1 shorter events, 0.0 us)
Async XLA Ops:
  0.6 26.9 %copy-start = (s32[2,588]{1,0:T(2,128)S(1)}, s32[2,588]{1,0:T(2,128)}, u32[]{:S(2)}) copy-start(s32[2,588]{1,0:T(2,128)} %param.15) | copy-start | bytes 14116
  1.6 8.1 %collective-permute-start = (bf16[126,1024]{1,0:T(8,128)(2,1)S(1)}, bf16[126,1024]{1,0:T(8,128)(2,1)S(1)}, u32[]{:S(2)}, u32[]{:S(2)}) collective-permute-start(bf16[126,1024]{1,0:T(8,128)(2,1)S(1)} %slice_bitcast_fusion), channel_id=1, source_target_pairs={{0,6},{2,0},{4,2},{6,4},{1,7},{3,1},{5,3},{7,5},{8,14},{10,8},{12,... | collective-permute-start | bytes 774152 | tf_op jit(solution)/shard_map/ppermute | solution.py:22
  9.7 1.0 %copy-start.1 = (bf16[1,147,1024]{2,1,0:T(8,128)(2,1)S(1)}, bf16[1,147,1024]{2,1,0:T(8,128)(2,1)}, u32[]{:S(2)}) copy-start(bf16[1,147,1024]{2,1,0:T(8,128)(2,1)} %param.8) | copy-start | bytes 903172
  10.7 1.6 %copy-start.2 = (bf16[1024,1024]{1,0:T(8,128)(2,1)S(1)}, bf16[1024,1024]{1,0:T(8,128)(2,1)}, u32[]{:S(2)}) copy-start(bf16[1024,1024]{1,0:T(8,128)(2,1)} %key_ref.1) | copy-start | bytes 6291460
  12.3 1.2 %copy-start.3 = (bf16[512,1024]{1,0:T(8,128)(2,1)S(1)}, bf16[512,1024]{1,0:T(8,128)(2,1)}, u32[]{:S(2)}) copy-start(bf16[512,1024]{1,0:T(8,128)(2,1)} %out_ref.1) | copy-start | bytes 3145732
  13.5 0.7 %copy-start.4 = (f32[1024]{0:T(1024)S(1)}, f32[1024]{0:T(1024)}, u32[]{:S(2)}) copy-start(f32[1024]{0:T(1024)} %param.9) | copy-start | bytes 12292
  14.2 0.7 %copy-start.5 = (s32[1,2]{1,0:T(1,128)S(1)}, s32[1,2]{1,0:T(1,128)}, u32[]{:S(2)}) copy-start(s32[1,2]{1,0:T(1,128)} %shifts.1) | copy-start | bytes 28
  21.1 11.7 %collective-permute-start.1 = (bf16[147,512]{1,0:T(8,128)(2,1)S(1)}, bf16[147,512]{1,0:T(8,128)(2,1)S(1)}, u32[]{:S(2)}, u32[]{:S(2)}) collective-permute-start(bf16[147,512]{1,0:T(8,128)(2,1)S(1)} %get-tuple-element.7), channel_id=1, source_target_pairs={{0,2},{2,4},{4,6},{6,0},{1,3},{3,5},{5,7},{7,1},{8,10},{10,12},{12... | collective-permute-start | bytes 451592 | tf_op jit(solution)/shard_map/ppermute | solution.py:22
  22.7 12.8 %collective-permute-start.2 = (bf16[147,512]{1,0:T(8,128)(2,1)S(1)}, bf16[147,512]{1,0:T(8,128)(2,1)S(1)}, u32[]{:S(2)}, u32[]{:S(2)}) collective-permute-start(bf16[147,512]{1,0:T(8,128)(2,1)S(1)} %get-tuple-element.8), channel_id=1, source_target_pairs={{0,4},{2,6},{4,0},{6,2},{1,5},{3,7},{5,1},{7,3},{8,12},{10,14},{12... | collective-permute-start | bytes 451592 | tf_op jit(solution)/shard_map/ppermute | solution.py:22
  25.6 13.1 %collective-permute-start.3 = (bf16[147,512]{1,0:T(8,128)(2,1)S(1)}, bf16[147,512]{1,0:T(8,128)(2,1)S(1)}, u32[]{:S(2)}, u32[]{:S(2)}) collective-permute-start(bf16[147,512]{1,0:T(8,128)(2,1)S(1)} %get-tuple-element.9), channel_id=1, source_target_pairs={{0,6},{2,0},{4,2},{6,4},{1,7},{3,1},{5,3},{7,5},{8,14},{10,8},{12,... | collective-permute-start | bytes 451592 | tf_op jit(solution)/shard_map/ppermute | solution.py:22
  39.8 9.2 %collective-permute-start.4 = (bf16[294,512]{1,0:T(8,128)(2,1)S(1)}, bf16[294,512]{1,0:T(8,128)(2,1)S(1)}, u32[]{:S(2)}, u32[]{:S(2)}) collective-permute-start(bf16[294,512]{1,0:T(8,128)(2,1)S(1)} %shard_map.97), channel_id=1, source_target_pairs={{0,1},{1,0},{2,3},{3,2},{4,5},{5,4},{6,7},{7,6},{8,9},{9,8},{10,11... | collective-permute-start | bytes 903176 | tf_op jit(solution)/shard_map/ppermute | solution.py:22

commit v2 on v1

v2 whole, which is shorter than its diff:
```python
import functools

import jax
import jax.numpy as jnp
from jax import lax
from jax.experimental import pallas as pl
from jax.experimental.pallas import tpu as pltpu
from jax.sharding import PartitionSpec as P

HEADS = 16
HEAD_DIM = 32
GRID_H = 28
GRID_W = 21
WIN = 7

GROUP = 8
VMEM_LIMIT = 32 * 1024 * 1024


def rotated(block, axis, distance):
    devices = lax.axis_size(axis)
    return lax.ppermute(block, axis, [(i, (i + distance) % devices) for i in range(devices)])


def dot(a, b):
    return jnp.dot(a, b, preferred_element_type=jnp.float32)


def one_hot(cond):
    return jnp.where(cond, 1.0, 0.0).astype(jnp.bfloat16)


def stage_kernel(n_weights, shifts, pages_ref, *refs):
    weights, rolled_ref, staged = refs[:n_weights], refs[n_weights], refs[n_weights + 1 : -2]
    own, arrived = refs[-2:]
    copies = [pltpu.make_async_copy(pages_ref.at[0], own, arrived.at[n_weights])]
    copies += [
        pltpu.make_async_copy(weights[i], staged[i], arrived.at[i]) for i in range(n_weights)
    ]
    for copy in copies:
        copy.start()
    band_rows = own.shape[0]
    rows = rolled_ref.shape[0]
    source = roll_source(rows, band_rows, shifts)
    take = one_hot(source == lax.broadcasted_iota(jnp.int32, (rows, band_rows), 1))
    copies[0].wait()
    rolled_ref[...] = dot(take, own[...]).astype(jnp.bfloat16)
    for copy in copies[1:]:
        copy.wait()


def roll_source(rows, band_rows, shifts):
    cell = lax.broadcasted_iota(jnp.int32, (rows, 1), 0)
    cell_row = cell // GRID_W
    from_col = cell - cell_row * GRID_W + shifts[0, 1]
    from_col = jnp.where(from_col >= GRID_W, from_col - GRID_W, from_col)
    return jnp.where(cell < band_rows, (cell_row + shifts[0, 0]) * GRID_W + from_col, -1)


def encode_kernel(
    n_seq, band_rows, place, shifts, rolled_ref, halo_ref, gain_ref, qkv_ref, out_ref, key_ref,
    memory_ref, *sent
):
    halo_rows = halo_ref.shape[0]
    rows = rolled_ref.shape[0]
    attn = HEADS * HEAD_DIM
    seq = place[0]
    row_shift, col_shift = shifts[0, 0], shifts[0, 1]

    source = roll_source(rows, band_rows, shifts) - band_rows
    take = one_hot(source == lax.broadcasted_iota(jnp.int32, (rows, halo_rows), 1))
    rolled = rolled_ref[...].astype(jnp.float32) + dot(take, halo_ref[...])

    mean = jnp.mean(rolled, axis=-1, keepdims=True)
    centred = rolled - mean
    variance = jnp.mean(centred * centred, axis=-1, keepdims=True)
    normed = (centred * lax.rsqrt(variance + 1e-05) * gain_ref[...]).astype(jnp.bfloat16)
    qkv = dot(normed, qkv_ref[...]).astype(jnp.bfloat16)

    def marks(index):
        row = index // GRID_W
        col = index - row * GRID_W
        wrap_row = (seq * WIN + row >= GRID_H - row_shift).astype(jnp.int32)
        wrap_col = (col >= GRID_W - col_shift).astype(jnp.int32)
        return jnp.where(index < band_rows, (col // WIN) * 4 + 2 * wrap_row + wrap_col, -1)

    same = marks(lax.broadcasted_iota(jnp.int32, (rows, 1), 0)) == marks(
        lax.broadcasted_iota(jnp.int32, (1, rows), 1)
    )
    same = jnp.concatenate([same.astype(jnp.int32)] * GROUP, axis=0) != 0

    width = GROUP * HEAD_DIM
    lane_head = lax.broadcasted_iota(jnp.int32, (1, width), 1) // HEAD_DIM
    parts = []
    for g in range(HEADS // GROUP):
        at = g * width
        q = qkv[:, at : at + width]
        k = qkv[:, attn + at : attn + at + width]
        v = qkv[:, 2 * attn + at : 2 * attn + at + width]
        stacked = jnp.concatenate(
            [jnp.where(lane_head == h, q, jnp.zeros_like(q)) for h in range(GROUP)], axis=0
        )
        scores = lax.dot_general(
            stacked, k, (((1,), (1,)), ((), ())), preferred_element_type=jnp.float32
        )
        scores = jnp.where(same, scores * HEAD_DIM ** (-0.5), -1000000000.0)
        scores = jnp.exp(scores - jnp.max(scores, axis=-1, keepdims=True))
        total = jnp.sum(scores, axis=-1, keepdims=True)
        weights = (scores * (1.0 / total)).astype(jnp.bfloat16)
        mixed = dot(weights, v)
        part = jnp.zeros((rows, width), jnp.float32)
        for h in range(GROUP):
            part = jnp.where(lane_head == h, mixed[h * rows : (h + 1) * rows], part)
        parts.append(part.astype(jnp.bfloat16))
    attended = jnp.concatenate(parts, axis=1)
    memory = (rolled + dot(attended, out_ref[...])).astype(jnp.bfloat16)
    memory_ref[...] = memory
    project(n_seq, seq, memory, key_ref, sent)


def project(n_seq, seq, memory, weight_ref, sent):
    own_cols = weight_ref.shape[1] // n_seq
    for d in range(n_seq):
        to = lax.rem(seq + d, n_seq)
        cols = pl.ds(pl.multiple_of(to * own_cols, own_cols), own_cols)
        block = dot(memory, weight_ref[:, cols])
        sent[d][...] = block[: sent[d].shape[0]].astype(jnp.bfloat16)


def value_kernel(n_seq, place, memory_ref, weight_ref, *sent):
    project(n_seq, place[0], memory_ref[...], weight_ref, sent)


def select_kernel(n_seq, first, count, place, order_ref, *refs):
    held, outs = refs[:n_seq], refs[n_seq:]
    band_rows = held[0].shape[0]
    seq, tensor = place[0], place[1]
    n_tensor = order_ref.shape[0]
    pos = order_ref.shape[1]
    for i in range(count):
        order = order_ref[lax.rem(tensor + first + i, n_tensor)]
        total = None
        for d in range(n_seq):
            band = lax.rem(seq - d + n_seq, n_seq)
            pick = one_hot(
                order - band * band_rows == lax.broadcasted_iota(jnp.int32, (pos, band_rows), 1)
            )
            term = dot(pick, held[d][...])
            total = term if total is None else total + term
        outs[i][...] = total.astype(jnp.bfloat16)


def call(kernel, out_shape, n_scalar, n_vmem, flops, moved, n_hbm=0, scratch=()):
    smem = pl.BlockSpec(memory_space=pltpu.SMEM)
    vmem = pl.BlockSpec(memory_space=pltpu.VMEM)
    hbm = pl.BlockSpec(memory_space=pltpu.HBM)
    return pl.pallas_call(
        kernel,
        out_shape=out_shape,
        in_specs=[smem] * n_scalar + [vmem] * n_vmem + [hbm] * n_hbm,
        out_specs=jax.tree.map(lambda _: vmem, out_shape),
        scratch_shapes=list(scratch),
        compiler_params=pltpu.CompilerParams(vmem_limit_bytes=VMEM_LIMIT),
        cost_estimate=pl.CostEstimate(flops=flops, bytes_accessed=moved, transcendentals=0),
    )


def local(
    memory_in, norm_gain, qkv_weight, out_weight, key_weight, value_weight, shift_offsets, row_order
):
    _, band_rows, emb = memory_in.shape
    n_seq = lax.axis_size("seq")
    n_tensor = lax.axis_size("tensor")
    own_cols = key_weight.shape[1] // n_seq
    pos = row_order.shape[1] // n_tensor
    rows = -(-band_rows // 16) * 16
    place = jnp.stack([lax.axis_index("seq"), lax.axis_index("tensor")]).astype(jnp.int32)
    halo = rotated(memory_in[0, : (WIN - 1) * GRID_W], "seq", -1)
    order = lax.dynamic_index_in_dim(row_order, lax.axis_index("tensor"), 0, False)
    order = order.reshape(n_tensor, pos, 1)

    weights = [qkv_weight, out_weight, key_weight, value_weight]
    rolled_own, *weights = call(
        functools.partial(stage_kernel, len(weights)),
        [jax.ShapeDtypeStruct((rows, emb), jnp.bfloat16)]
        + [jax.ShapeDtypeStruct(w.shape, w.dtype) for w in weights],
        1, 0, 50_000_000, 16_000_000, 1 + len(weights),
        [
            pltpu.VMEM((band_rows, emb), jnp.bfloat16),
            pltpu.SemaphoreType.DMA((1 + len(weights),)),
        ],
    )(shift_offsets, memory_in, *weights)

    block = jax.ShapeDtypeStruct((band_rows, own_cols), jnp.bfloat16)
    memory, *key_sent = call(
        functools.partial(encode_kernel, n_seq, band_rows),
        [jax.ShapeDtypeStruct((rows, emb), jnp.bfloat16)] + [block] * n_seq,
        2, 6, 1_600_000_000, 8_000_000,
    )(place, shift_offsets, rolled_own, halo, norm_gain.reshape(1, emb), *weights[:3])
    value_sent = call(
        functools.partial(value_kernel, n_seq), [block] * n_seq, 1, 2, 300_000_000, 2_000_000
    )(place, memory, weights[3])

    piece = jax.ShapeDtypeStruct((pos, own_cols), jnp.bfloat16)

    def gathered(sent):
        held = [rotated(sent[d], "seq", d) if d else sent[0] for d in range(n_seq)]
        away = call(
            functools.partial(select_kernel, n_seq, 1, n_tensor - 1),
            [piece] * (n_tensor - 1), 1, 1 + n_seq, 300_000_000, 1_000_000,
        )(place, order, *held)
        arrived = [rotated(away[d - 1], "tensor", d) for d in range(1, n_tensor)]
        kept = call(
            functools.partial(select_kernel, n_seq, 0, 1),
            [piece], 1, 1 + n_seq, 300_000_000, 1_000_000,
        )(place, order, *held)
        page = jnp.arange(n_tensor)[:, None, None]
        result = kept[0][None]
        for d in range(1, n_tensor):
            came = page == (lax.axis_index("tensor") - d) % n_tensor
            result = jnp.where(came, arrived[d - 1][None], result)
        return jnp.broadcast_to(result, (n_tensor, pos, own_cols))

    return gathered(key_sent), gathered(value_sent)


def solution(mesh):
    placed = (
        P(("dp", "tensor"), "seq", None),
        P(),
        P(),
        P(),
        P(),
        P(),
        P(("dp", "tensor"), None),
        P("dp", None),
    )
    return jax.shard_map(
        local,
        mesh=mesh,
        in_specs=placed,
        out_specs=(P("dp", "tensor", "seq"), P("dp", "tensor", "seq")),
        check_vma=False,
    )
```

time: 51.7 us -> 43.8 us (0.85)
  the two profiles are of different devices: /device:TPU:10 before, /device:TPU:0 now
where the time goes in v2:
time: 43.8 us; the launch traced here: 43.5 us
  starting transfers between devices  17.1 us (39%)
  Pallas kernels  10.1 us (23%)
  local copies, waits for them, and re-layouts  9.12 us (21%)
  waiting for transfers between devices  4.67 us (11%)
  other arithmetic  1.75 us (4%)
  between operations  0.76 us (2%)
    ppermute x9, starting transfers between devices, rotated(): lax.ppermute(block, axis, [(i, (i + distance) % devices) for i in range(d...  17.1 us
    unnamed x16, local copies, waits for them, and re-layouts  7.93 us
    ppermute x9, waiting for transfers between devices, rotated(): lax.ppermute(block, axis, [(i, (i + distance) % devices) for i in range(d...  4.67 us
    pallas_call x1, Pallas kernels, local(): call(functools.partial(encode_kernel, n_seq, band_rows), [jax.ShapeDtypeS...  3.78 us
    pallas_call x2, Pallas kernels, gathered(): call(functools.partial(select_kernel, n_seq, 1, n_tensor - 1), [piece] *...  1.87 us
    pallas_call x2, Pallas kernels, gathered(): call(functools.partial(select_kernel, n_seq, 0, 1), [piece], 1, 1 + n_seq...  1.85 us
    select_n x1, other arithmetic, gathered(): result = jnp.where(came, arrived[d - 1][None], result)  1.67 us
    pallas_call x1, Pallas kernels, local(): call(functools.partial(stage_kernel, len(weights)), [jax.ShapeDtypeStruct...  1.53 us
  transfers between devices with their start and end apart: 9, of which 2 were waited for; matrix products, arithmetic and copies ran while one was open for 1% of the time, Pallas kernels for 15%

profile of v2, /device:TPU:0, one launch (start us, length us, event | category | flops | bytes accessed | tf_op | source)
XLA Modules:
  0.0 43.5 jit_solution(6058816369986805638)
XLA Ops:
  0.6 0.0 copy-start
  0.6 1.0 %slice_bitcast_fusion = bf16[126,1024]{1,0:T(8,128)(2,1)S(1)} fusion(bf16[1,147,1024]{2,1,0:T(8,128)(2,1)} %pages_ref.1), kind=kLoop, calls=%fused_computation.2 | loop fusion | bytes 516096 | tf_op jit(solution)/shard_map/squeeze | solution.py:178
  1.6 5.1 %collective-permute-start = (bf16[126,1024]{1,0:T(8,128)(2,1)S(1)}, bf16[126,1024]{1,0:T(8,128)(2,1)S(1)}, u32[]{:S(2)}, u32[]{:S(2)}) collective-permute-start(bf16[126,1024]{1,0:T(8,128)(2,1)S(1)} %slice_bitcast_fusion), channel_id=1, source_target_pairs={{0,6},{2,0},{4,2},{6,4},{1,7},{3,1},{5,3},{7,5},{8,14},{10,8},{12,... | collective-permute-start | bytes 774152 | tf_op jit(solution)/shard_map/ppermute | solution.py:22
  6.7 1.9 %copy-done.1 = bf16[1024,1536]{1,0:T(8,128)(2,1)S(1)} copy-done((bf16[1024,1536]{1,0:T(8,128)(2,1)S(1)}, bf16[1024,1536]{1,0:T(8,128)(2,1)}, u32[]{:S(2)}) %copy-start.1) | copy-done | bytes 3145752
  8.6 1.6 %copy-done.2 = bf16[1024,1024]{1,0:T(8,128)(2,1)S(1)} copy-done((bf16[1024,1024]{1,0:T(8,128)(2,1)S(1)}, bf16[1024,1024]{1,0:T(8,128)(2,1)}, u32[]{:S(2)}) %copy-start.2) | copy-done | bytes 2097176
  10.2 1.6 %copy-done.3 = bf16[1024,1024]{1,0:T(8,128)(2,1)S(1)} copy-done((bf16[1024,1024]{1,0:T(8,128)(2,1)S(1)}, bf16[1024,1024]{1,0:T(8,128)(2,1)}, u32[]{:S(2)}) %copy-start.3) | copy-done | bytes 2097176
  11.8 1.0 %copy-done.4 = bf16[1,147,1024]{2,1,0:T(8,128)(2,1)S(1)} copy-done((bf16[1,147,1024]{2,1,0:T(8,128)(2,1)S(1)}, bf16[1,147,1024]{2,1,0:T(8,128)(2,1)}, u32[]{:S(2)}) %copy-start.4) | copy-done | bytes 301080
  12.8 1.2 %copy-done.5 = bf16[512,1024]{1,0:T(8,128)(2,1)S(1)} copy-done((bf16[512,1024]{1,0:T(8,128)(2,1)S(1)}, bf16[512,1024]{1,0:T(8,128)(2,1)}, u32[]{:S(2)}) %copy-start.5) | copy-done | bytes 1048600
  14.0 0.7 %copy-done.7 = s32[1,2]{1,0:T(1,128)S(1)} copy-done((s32[1,2]{1,0:T(1,128)S(1)}, s32[1,2]{1,0:T(1,128)}, u32[]{:S(2)}) %copy-start.7) | copy-done | bytes 32
  14.6 1.5 %shard_map.95 = (bf16[160,1024]{1,0:T(8,128)(2,1)S(1)}, bf16[1024,1536]{1,0:T(8,128)(2,1)S(1)}, bf16[512,1024]{1,0:T(8,128)(2,1)S(1)}, bf16[1024,1024]{1,0:T(8,128)(2,1)S(1)}, bf16[1024,1024]{1,0:T(8,128)(2,1)S(1)}) custom-call(s32[1,2]{1,0:T(1,128)S(1)} %copy-done.7, bf16[1,147,1024]{2,1,0:T(8,128)(2,1)S(1)} %copy-done.4, bf16[1024,1536]{1,0:T(8,128)(2,1)S(1)} %copy-done.1, ...), custom_call_target="tpu_custom_call" | custom-call | flops 50000000 | bytes 16000000 | tf_op jit(solution)/shard_map/pallas_call | solution.py:183
  16.2 0.1 pad_add_fusion.place
  16.3 0.0 collective-permute-done.halo_ref
  16.3 3.8 %shard_map.96 = (bf16[160,1024]{1,0:T(8,128)(2,1)S(1)}, bf16[147,256]{1,0:T(8,128)(2,1)S(1)}, bf16[147,256]{1,0:T(8,128)(2,1)S(1)}, bf16[147,256]{1,0:T(8,128)(2,1)S(1)}, bf16[147,256]{1,0:T(8,128)(2,1)S(1)}) custom-call(s32[2]{0:T(128)S(1)} %pad_add_fusion.place, s32[1,2]{1,0:T(1,128)S(1)} %copy-done.7, bf16[160,1024]{1,0:T(8,128)(2,1)S(1)} %get-tuple-element.16.rolled_ref, ...), custom_call_target="tpu_custom_call" | custom-call | flops 1600000000 | bytes 8000000 | tf_op jit(solution)/shard_map/pallas_call | solution.py:195
  20.1 0.1 collective-permute-start.1
  20.1 1.0 %collective-permute-start.2 = (bf16[147,256]{1,0:T(8,128)(2,1)S(1)}, bf16[147,256]{1,0:T(8,128)(2,1)S(1)}, u32[]{:S(2)}, u32[]{:S(2)}) collective-permute-start(bf16[147,256]{1,0:T(8,128)(2,1)S(1)} %get-tuple-element.22), channel_id=1, source_target_pairs={{0,4},{2,6},{4,0},{6,2},{1,5},{3,7},{5,1},{7,3},{8,12},{10,14},{12... | collective-permute-start | bytes 225800 | tf_op jit(solution)/shard_map/ppermute | solution.py:22
  21.1 2.8 %collective-permute-start.3 = (bf16[147,256]{1,0:T(8,128)(2,1)S(1)}, bf16[147,256]{1,0:T(8,128)(2,1)S(1)}, u32[]{:S(2)}, u32[]{:S(2)}) collective-permute-start(bf16[147,256]{1,0:T(8,128)(2,1)S(1)} %get-tuple-element.23), channel_id=1, source_target_pairs={{0,6},{2,0},{4,2},{6,4},{1,7},{3,1},{5,3},{7,5},{8,14},{10,8},{12,... | collective-permute-start | bytes 225800 | tf_op jit(solution)/shard_map/ppermute | solution.py:22
  23.9 1.1 %shard_map.99 = (bf16[147,256]{1,0:T(8,128)(2,1)S(1)}, bf16[147,256]{1,0:T(8,128)(2,1)S(1)}, bf16[147,256]{1,0:T(8,128)(2,1)S(1)}, bf16[147,256]{1,0:T(8,128)(2,1)S(1)}) custom-call(s32[2]{0:T(128)S(1)} %pad_add_fusion.place, bf16[160,1024]{1,0:T(8,128)(2,1)S(1)} %get-tuple-element.24.memory_ref, bf16[1024,1024]{1,0:T(8,128)(2,1)S(1)} %get-tuple-element.25.weight_ref), custom_call_target="tpu_custom_call" | custom-call | flops 300000000 | bytes 2000000 | tf_op jit(solution)/shard_map/pallas_call | solution.py:200
  25.0 0.6 %collective-permute-start.5 = (bf16[147,256]{1,0:T(8,128)(2,1)S(1)}, bf16[147,256]{1,0:T(8,128)(2,1)S(1)}, u32[]{:S(2)}, u32[]{:S(2)}) collective-permute-start(bf16[147,256]{1,0:T(8,128)(2,1)S(1)} %get-tuple-element.27), channel_id=1, source_target_pairs={{0,2},{2,4},{4,6},{6,0},{1,3},{3,5},{5,7},{7,1},{8,10},{10,12},{12... | collective-permute-start | bytes 225800 | tf_op jit(solution)/shard_map/ppermute | solution.py:22
  25.6 1.5 %collective-permute-start.6 = (bf16[147,256]{1,0:T(8,128)(2,1)S(1)}, bf16[147,256]{1,0:T(8,128)(2,1)S(1)}, u32[]{:S(2)}, u32[]{:S(2)}) collective-permute-start(bf16[147,256]{1,0:T(8,128)(2,1)S(1)} %get-tuple-element.28), channel_id=1, source_target_pairs={{0,4},{2,6},{4,0},{6,2},{1,5},{3,7},{5,1},{7,3},{8,12},{10,14},{12... | collective-permute-start | bytes 225800 | tf_op jit(solution)/shard_map/ppermute | solution.py:22
  27.2 0.0 collective-permute-done.1.refs_1_
  27.2 2.8 %collective-permute-start.7 = (bf16[147,256]{1,0:T(8,128)(2,1)S(1)}, bf16[147,256]{1,0:T(8,128)(2,1)S(1)}, u32[]{:S(2)}, u32[]{:S(2)}) collective-permute-start(bf16[147,256]{1,0:T(8,128)(2,1)S(1)} %get-tuple-element.29), channel_id=1, source_target_pairs={{0,6},{2,0},{4,2},{6,4},{1,7},{3,1},{5,3},{7,5},{8,14},{10,8},{12,... | collective-permute-start | bytes 225800 | tf_op jit(solution)/shard_map/ppermute | solution.py:22
  30.0 0.2 reshape.22.order_ref
  30.3 0.0 collective-permute-done.3.refs_3_
  30.3 0.9 %shard_map.97 = bf16[294,256]{1,0:T(8,128)(2,1)S(1)} custom-call(s32[2]{0:T(128)S(1)} %pad_add_fusion.place, s32[2,294,1]{2,1,0:T(8,128)S(1)} %reshape.22.order_ref, bf16[147,256]{1,0:T(8,128)(2,1)S(1)} %get-tuple-element.20.refs_0_, bf16[147,256]{1,0:T(8,128)(2,1)S(1)} %collective-permute-done.1.refs_1_, ...), custom_call_target="tpu_custom_call" | custom-call | flops 300000000 | bytes 1000000 | tf_op jit(solution)/shard_map/pallas_call | solution.py:208
  31.2 1.6 %collective-permute-start.4 = (bf16[294,256]{1,0:T(8,128)(2,1)S(1)}, bf16[294,256]{1,0:T(8,128)(2,1)S(1)}, u32[]{:S(2)}, u32[]{:S(2)}) collective-permute-start(bf16[294,256]{1,0:T(8,128)(2,1)S(1)} %shard_map.97), channel_id=1, source_target_pairs={{0,1},{1,0},{2,3},{3,2},{4,5},{5,4},{6,7},{7,6},{8,9},{9,8},{10,11... | collective-permute-start | bytes 451592 | tf_op jit(solution)/shard_map/ppermute | solution.py:22
  32.8 2.8 %collective-permute-done.6.refs_2_ = bf16[147,256]{1,0:T(8,128)(2,1)S(1)} collective-permute-done((bf16[147,256]{1,0:T(8,128)(2,1)S(1)}, bf16[147,256]{1,0:T(8,128)(2,1)S(1)}, u32[]{:S(2)}, u32[]{:S(2)}) %collective-permute-start.6) | collective-permute-done | bytes 75296 | tf_op jit(solution)/shard_map/ppermute | solution.py:22
  35.7 0.9 %shard_map.100 = bf16[294,256]{1,0:T(8,128)(2,1)S(1)} custom-call(s32[2]{0:T(128)S(1)} %pad_add_fusion.place, s32[2,294,1]{2,1,0:T(8,128)S(1)} %reshape.22.order_ref, bf16[147,256]{1,0:T(8,128)(2,1)S(1)} %get-tuple-element.26.refs_0_, bf16[147,256]{1,0:T(8,128)(2,1)S(1)} %collective-permute-done.5.refs_1_, ...), custom_call_target="tpu_custom_call" | custom-call | flops 300000000 | bytes 1000000 | tf_op jit(solution)/shard_map/pallas_call | solution.py:208
  36.6 1.6 %collective-permute-start.8 = (bf16[294,256]{1,0:T(8,128)(2,1)S(1)}, bf16[294,256]{1,0:T(8,128)(2,1)S(1)}, u32[]{:S(2)}, u32[]{:S(2)}) collective-permute-start(bf16[294,256]{1,0:T(8,128)(2,1)S(1)} %shard_map.100), channel_id=1, source_target_pairs={{0,1},{1,0},{2,3},{3,2},{4,5},{5,4},{6,7},{7,6},{8,9},{9,8},{10,11... | collective-permute-start | bytes 451592 | tf_op jit(solution)/shard_map/ppermute | solution.py:22
  38.2 0.9 %shard_map.98 = bf16[294,256]{1,0:T(8,128)(2,1)S(1)} custom-call(s32[2]{0:T(128)S(1)} %pad_add_fusion.place, s32[2,294,1]{2,1,0:T(8,128)S(1)} %reshape.22.order_ref, bf16[147,256]{1,0:T(8,128)(2,1)S(1)} %get-tuple-element.20.refs_0_, bf16[147,256]{1,0:T(8,128)(2,1)S(1)} %collective-permute-done.1.refs_1_, ...), custom_call_target="tpu_custom_call" | custom-call | flops 300000000 | bytes 1000000 | tf_op jit(solution)/shard_map/pallas_call | solution.py:213
  39.1 0.9 %shard_map.101 = bf16[294,256]{1,0:T(8,128)(2,1)S(1)} custom-call(s32[2]{0:T(128)S(1)} %pad_add_fusion.place, s32[2,294,1]{2,1,0:T(8,128)S(1)} %reshape.22.order_ref, bf16[147,256]{1,0:T(8,128)(2,1)S(1)} %get-tuple-element.26.refs_0_, bf16[147,256]{1,0:T(8,128)(2,1)S(1)} %collective-permute-done.5.refs_1_, ...), custom_call_target="tpu_custom_call" | custom-call | flops 300000000 | bytes 1000000 | tf_op jit(solution)/shard_map/pallas_call | solution.py:213
  40.1 1.8 %collective-permute-done.8 = bf16[294,256]{1,0:T(8,128)(2,1)S(1)} collective-permute-done((bf16[294,256]{1,0:T(8,128)(2,1)S(1)}, bf16[294,256]{1,0:T(8,128)(2,1)S(1)}, u32[]{:S(2)}, u32[]{:S(2)}) %collective-permute-start.8) | collective-permute-done | bytes 150560 | tf_op jit(solution)/shard_map/ppermute | solution.py:22
  41.8 1.7 %broadcast_select_fusion = (bf16[2,294,256]{2,0,1:T(2,128)(2,1)}, bf16[2,294,256]{2,0,1:T(2,128)(2,1)}) fusion(pred[2]{0:T(512)(128)(4,1)S(1)} %iota_compare_fusion, bf16[294,256]{1,0:T(8,128)(2,1)S(1)} %shard_map.101, bf16[294,256]{1,0:T(8,128)(2,1)S(1)} %collective-permute-done.8, bf16[294,256]{1,0:T(8,128)(2,1)S(1)} %shard_map.98, ...), kind=kLoop, calls=%fused_computation | loop fusion | flops 301056 | bytes 1204226 | tf_op jit(solution)/shard_map/jit(_where)/select_n | solution.py:221
  (15 shorter events, 0.0 us)
Async XLA Ops:
  0.6 29.4 %copy-start = (s32[2,588]{1,0:T(2,128)S(1)}, s32[2,588]{1,0:T(2,128)}, u32[]{:S(2)}) copy-start(s32[2,588]{1,0:T(2,128)} %param.15) | copy-start | bytes 14116
  1.6 14.6 %collective-permute-start = (bf16[126,1024]{1,0:T(8,128)(2,1)S(1)}, bf16[126,1024]{1,0:T(8,128)(2,1)S(1)}, u32[]{:S(2)}, u32[]{:S(2)}) collective-permute-start(bf16[126,1024]{1,0:T(8,128)(2,1)S(1)} %slice_bitcast_fusion), channel_id=1, source_target_pairs={{0,6},{2,0},{4,2},{6,4},{1,7},{3,1},{5,3},{7,5},{8,14},{10,8},{12,... | collective-permute-start | bytes 774152 | tf_op jit(solution)/shard_map/ppermute | solution.py:22
  6.7 1.9 %copy-start.1 = (bf16[1024,1536]{1,0:T(8,128)(2,1)S(1)}, bf16[1024,1536]{1,0:T(8,128)(2,1)}, u32[]{:S(2)}) copy-start(bf16[1024,1536]{1,0:T(8,128)(2,1)} %refs_0_.1) | copy-start | bytes 9437188
  8.6 1.6 %copy-start.2 = (bf16[1024,1024]{1,0:T(8,128)(2,1)S(1)}, bf16[1024,1024]{1,0:T(8,128)(2,1)}, u32[]{:S(2)}) copy-start(bf16[1024,1024]{1,0:T(8,128)(2,1)} %refs_2_.1) | copy-start | bytes 6291460
  10.2 1.6 %copy-start.3 = (bf16[1024,1024]{1,0:T(8,128)(2,1)S(1)}, bf16[1024,1024]{1,0:T(8,128)(2,1)}, u32[]{:S(2)}) copy-start(bf16[1024,1024]{1,0:T(8,128)(2,1)} %refs_3_.1) | copy-start | bytes 6291460
  11.8 1.0 %copy-start.4 = (bf16[1,147,1024]{2,1,0:T(8,128)(2,1)S(1)}, bf16[1,147,1024]{2,1,0:T(8,128)(2,1)}, u32[]{:S(2)}) copy-start(bf16[1,147,1024]{2,1,0:T(8,128)(2,1)} %pages_ref.1) | copy-start | bytes 903172
  12.8 1.2 %copy-start.5 = (bf16[512,1024]{1,0:T(8,128)(2,1)S(1)}, bf16[512,1024]{1,0:T(8,128)(2,1)}, u32[]{:S(2)}) copy-start(bf16[512,1024]{1,0:T(8,128)(2,1)} %refs_1_.1) | copy-start | bytes 3145732
  14.0 0.7 %copy-start.7 = (s32[1,2]{1,0:T(1,128)S(1)}, s32[1,2]{1,0:T(1,128)}, u32[]{:S(2)}) copy-start(s32[1,2]{1,0:T(1,128)} %shifts.3) | copy-start | bytes 28
  14.6 1.6 %copy-start.6 = (f32[1024]{0:T(1024)S(1)}, f32[1024]{0:T(1024)}, u32[]{:S(2)}) copy-start(f32[1024]{0:T(1024)} %param.9) | copy-start | bytes 12292
  20.1 7.1 %collective-permute-start.1 = (bf16[147,256]{1,0:T(8,128)(2,1)S(1)}, bf16[147,256]{1,0:T(8,128)(2,1)S(1)}, u32[]{:S(2)}, u32[]{:S(2)}) collective-permute-start(bf16[147,256]{1,0:T(8,128)(2,1)S(1)} %get-tuple-element.21), channel_id=1, source_target_pairs={{0,2},{2,4},{4,6},{6,0},{1,3},{3,5},{5,7},{7,1},{8,10},{10,12},{12... | collective-permute-start | bytes 225800 | tf_op jit(solution)/shard_map/ppermute | solution.py:22
  20.1 10.1 %collective-permute-start.2 = (bf16[147,256]{1,0:T(8,128)(2,1)S(1)}, bf16[147,256]{1,0:T(8,128)(2,1)S(1)}, u32[]{:S(2)}, u32[]{:S(2)}) collective-permute-start(bf16[147,256]{1,0:T(8,128)(2,1)S(1)} %get-tuple-element.22), channel_id=1, source_target_pairs={{0,4},{2,6},{4,0},{6,2},{1,5},{3,7},{5,1},{7,3},{8,12},{10,14},{12... | collective-permute-start | bytes 225800 | tf_op jit(solution)/shard_map/ppermute | solution.py:22
  21.1 9.2 %collective-permute-start.3 = (bf16[147,256]{1,0:T(8,128)(2,1)S(1)}, bf16[147,256]{1,0:T(8,128)(2,1)S(1)}, u32[]{:S(2)}, u32[]{:S(2)}) collective-permute-start(bf16[147,256]{1,0:T(8,128)(2,1)S(1)} %get-tuple-element.23), channel_id=1, source_target_pairs={{0,6},{2,0},{4,2},{6,4},{1,7},{3,1},{5,3},{7,5},{8,14},{10,8},{12,... | collective-permute-start | bytes 225800 | tf_op jit(solution)/shard_map/ppermute | solution.py:22
  25.0 7.8 %collective-permute-start.5 = (bf16[147,256]{1,0:T(8,128)(2,1)S(1)}, bf16[147,256]{1,0:T(8,128)(2,1)S(1)}, u32[]{:S(2)}, u32[]{:S(2)}) collective-permute-start(bf16[147,256]{1,0:T(8,128)(2,1)S(1)} %get-tuple-element.27), channel_id=1, source_target_pairs={{0,2},{2,4},{4,6},{6,0},{1,3},{3,5},{5,7},{7,1},{8,10},{10,12},{12... | collective-permute-start | bytes 225800 | tf_op jit(solution)/shard_map/ppermute | solution.py:22
  25.6 10.0 %collective-permute-start.6 = (bf16[147,256]{1,0:T(8,128)(2,1)S(1)}, bf16[147,256]{1,0:T(8,128)(2,1)S(1)}, u32[]{:S(2)}, u32[]{:S(2)}) collective-permute-start(bf16[147,256]{1,0:T(8,128)(2,1)S(1)} %get-tuple-element.28), channel_id=1, source_target_pairs={{0,4},{2,6},{4,0},{6,2},{1,5},{3,7},{5,1},{7,3},{8,12},{10,14},{12... | collective-permute-start | bytes 225800 | tf_op jit(solution)/shard_map/ppermute | solution.py:22
  27.2 8.5 %collective-permute-start.7 = (bf16[147,256]{1,0:T(8,128)(2,1)S(1)}, bf16[147,256]{1,0:T(8,128)(2,1)S(1)}, u32[]{:S(2)}, u32[]{:S(2)}) collective-permute-start(bf16[147,256]{1,0:T(8,128)(2,1)S(1)} %get-tuple-element.29), channel_id=1, source_target_pairs={{0,6},{2,0},{4,2},{6,4},{1,7},{3,1},{5,3},{7,5},{8,14},{10,8},{12,... | collective-permute-start | bytes 225800 | tf_op jit(solution)/shard_map/ppermute | solution.py:22
  31.2 8.8 %collective-permute-start.4 = (bf16[294,256]{1,0:T(8,128)(2,1)S(1)}, bf16[294,256]{1,0:T(8,128)(2,1)S(1)}, u32[]{:S(2)}, u32[]{:S(2)}) collective-permute-start(bf16[294,256]{1,0:T(8,128)(2,1)S(1)} %shard_map.97), channel_id=1, source_target_pairs={{0,1},{1,0},{2,3},{3,2},{4,5},{5,4},{6,7},{7,6},{8,9},{9,8},{10,11... | collective-permute-start | bytes 451592 | tf_op jit(solution)/shard_map/ppermute | solution.py:22
  36.6 5.3 %collective-permute-start.8 = (bf16[294,256]{1,0:T(8,128)(2,1)S(1)}, bf16[294,256]{1,0:T(8,128)(2,1)S(1)}, u32[]{:S(2)}, u32[]{:S(2)}) collective-permute-start(bf16[294,256]{1,0:T(8,128)(2,1)S(1)} %shard_map.100), channel_id=1, source_target_pairs={{0,1},{1,0},{2,3},{3,2},{4,5},{5,4},{6,7},{7,6},{8,9},{9,8},{10,11... | collective-permute-start | bytes 451592 | tf_op jit(solution)/shard_map/ppermute | solution.py:22

commit v3 on v2

--- a/solution.py
+++ b/solution.py
@@ -15,6 +15,7 @@
 
 GROUP = 8
 VMEM_LIMIT = 32 * 1024 * 1024
+ENCODE_LIMIT = 52 * 1024 * 1024
 
 
 def rotated(block, axis, distance):
@@ -30,44 +31,41 @@
     return jnp.where(cond, 1.0, 0.0).astype(jnp.bfloat16)
 
 
-def stage_kernel(n_weights, shifts, pages_ref, *refs):
-    weights, rolled_ref, staged = refs[:n_weights], refs[n_weights], refs[n_weights + 1 : -2]
-    own, arrived = refs[-2:]
-    copies = [pltpu.make_async_copy(pages_ref.at[0], own, arrived.at[n_weights])]
-    copies += [
-        pltpu.make_async_copy(weights[i], staged[i], arrived.at[i]) for i in range(n_weights)
-    ]
-    for copy in copies:
-        copy.start()
-    band_rows = own.shape[0]
+def stage_kernel(place, pages_ref, gain_ref, rolled_ref, gain_out):
+    gain_out[...] = gain_ref[...]
+    band_rows = pages_ref.shape[1]
     rows = rolled_ref.shape[0]
-    source = roll_source(rows, band_rows, shifts)
+    source = roll_source(rows, band_rows, place)
     take = one_hot(source == lax.broadcasted_iota(jnp.int32, (rows, band_rows), 1))
-    copies[0].wait()
-    rolled_ref[...] = dot(take, own[...]).astype(jnp.bfloat16)
-    for copy in copies[1:]:
-        copy.wait()
-
-
-def roll_source(rows, band_rows, shifts):
+    rolled_ref[...] = dot(take, pages_ref[0]).astype(jnp.bfloat16)
+
+
+def roll_source(rows, band_rows, place):
     cell = lax.broadcasted_iota(jnp.int32, (rows, 1), 0)
     cell_row = cell // GRID_W
-    from_col = cell - cell_row * GRID_W + shifts[0, 1]
+    from_col = cell - cell_row * GRID_W + place[3]
     from_col = jnp.where(from_col >= GRID_W, from_col - GRID_W, from_col)
-    return jnp.where(cell < band_rows, (cell_row + shifts[0, 0]) * GRID_W + from_col, -1)
+    return jnp.where(cell < band_rows, (cell_row + place[2]) * GRID_W + from_col, -1)
 
 
 def encode_kernel(
-    n_seq, band_rows, place, shifts, rolled_ref, halo_ref, gain_ref, qkv_ref, out_ref, key_ref,
-    memory_ref, *sent
+    n_seq, band_rows, place, rolled_ref, halo_ref, gain_ref, qkv_hbm, out_hbm, key_hbm,
+    memory_ref, *refs
 ):
+    sent, (qkv_ref, out_ref, key_ref, arrived) = refs[:n_seq], refs[n_seq:]
     halo_rows = halo_ref.shape[0]
     rows = rolled_ref.shape[0]
     attn = HEADS * HEAD_DIM
     seq = place[0]
-    row_shift, col_shift = shifts[0, 0], shifts[0, 1]
-
-    source = roll_source(rows, band_rows, shifts) - band_rows
+    thirds = [pl.ds(i * attn, attn) for i in range(3)]
+    pairs = [(qkv_hbm.at[:, third], qkv_ref.at[:, third]) for third in thirds]
+    pairs += [(out_hbm, out_ref), (key_hbm, key_ref)]
+    copies = [pltpu.make_async_copy(*pair, arrived.at[i]) for i, pair in enumerate(pairs)]
+    for copy in copies:
+        copy.start()
+    row_shift, col_shift = place[2], place[3]
+
+    source = roll_source(rows, band_rows, place) - band_rows
     take = one_hot(source == lax.broadcasted_iota(jnp.int32, (rows, halo_rows), 1))
     rolled = rolled_ref[...].astype(jnp.float32) + dot(take, halo_ref[...])
 
@@ -75,7 +73,11 @@
     centred = rolled - mean
     variance = jnp.mean(centred * centred, axis=-1, keepdims=True)
     normed = (centred * lax.rsqrt(variance + 1e-05) * gain_ref[...]).astype(jnp.bfloat16)
-    qkv = dot(normed, qkv_ref[...]).astype(jnp.bfloat16)
+    parts = []
+    for third, copy in zip(thirds, copies):
+        copy.wait()
+        parts.append(dot(normed, qkv_ref[:, third]).astype(jnp.bfloat16))
+    queries, keys, values = parts
 
     def marks(index):
         row = index // GRID_W
@@ -94,9 +96,7 @@
     parts = []
     for g in range(HEADS // GROUP):
         at = g * width
-        q = qkv[:, at : at + width]
-        k = qkv[:, attn + at : attn + at + width]
-        v = qkv[:, 2 * attn + at : 2 * attn + at + width]
+        q, k, v = (part[:, at : at + width] for part in (queries, keys, values))
         stacked = jnp.concatenate(
             [jnp.where(lane_head == h, q, jnp.zeros_like(q)) for h in range(GROUP)], axis=0
         )
@@ -113,8 +113,10 @@
             part = jnp.where(lane_head == h, mixed[h * rows : (h + 1) * rows], part)
         parts.append(part.astype(jnp.bfloat16))
     attended = jnp.concatenate(parts, axis=1)
+    copies[3].wait()
     memory = (rolled + dot(attended, out_ref[...])).astype(jnp.bfloat16)
     memory_ref[...] = memory
+    copies[4].wait()
     project(n_seq, seq, memory, key_ref, sent)
 
 
@@ -150,7 +152,7 @@
         outs[i][...] = total.astype(jnp.bfloat16)
 
 
-def call(kernel, out_shape, n_scalar, n_vmem, flops, moved, n_hbm=0, scratch=()):
+def call(kernel, out_shape, n_scalar, n_vmem, flops, moved, n_hbm=0, scratch=(), limit=VMEM_LIMIT):
     smem = pl.BlockSpec(memory_space=pltpu.SMEM)
     vmem = pl.BlockSpec(memory_space=pltpu.VMEM)
     hbm = pl.BlockSpec(memory_space=pltpu.HBM)
@@ -160,7 +162,7 @@
         in_specs=[smem] * n_scalar + [vmem] * n_vmem + [hbm] * n_hbm,
         out_specs=jax.tree.map(lambda _: vmem, out_shape),
         scratch_shapes=list(scratch),
-        compiler_params=pltpu.CompilerParams(vmem_limit_bytes=VMEM_LIMIT),
+        compiler_params=pltpu.CompilerParams(vmem_limit_bytes=limit),
         cost_estimate=pl.CostEstimate(flops=flops, bytes_accessed=moved, transcendentals=0),
     )
 
@@ -174,32 +176,33 @@
     own_cols = key_weight.shape[1] // n_seq
     pos = row_order.shape[1] // n_tensor
     rows = -(-band_rows // 16) * 16
-    place = jnp.stack([lax.axis_index("seq"), lax.axis_index("tensor")]).astype(jnp.int32)
+    place = jnp.stack(
+        [lax.axis_index("seq"), lax.axis_index("tensor"), shift_offsets[0, 0], shift_offsets[0, 1]]
+    )
     halo = rotated(memory_in[0, : (WIN - 1) * GRID_W], "seq", -1)
     order = lax.dynamic_index_in_dim(row_order, lax.axis_index("tensor"), 0, False)
     order = order.reshape(n_tensor, pos, 1)
 
-    weights = [qkv_weight, out_weight, key_weight, value_weight]
-    rolled_own, *weights = call(
-        functools.partial(stage_kernel, len(weights)),
-        [jax.ShapeDtypeStruct((rows, emb), jnp.bfloat16)]
-        + [jax.ShapeDtypeStruct(w.shape, w.dtype) for w in weights],
-        1, 0, 50_000_000, 16_000_000, 1 + len(weights),
+    rolled_own, gain = call(
+        stage_kernel,
         [
-            pltpu.VMEM((band_rows, emb), jnp.bfloat16),
-            pltpu.SemaphoreType.DMA((1 + len(weights),)),
+            jax.ShapeDtypeStruct((rows, emb), jnp.bfloat16),
+            jax.ShapeDtypeStruct((1, emb), jnp.float32),
         ],
-    )(shift_offsets, memory_in, *weights)
-
+        1, 2, 50_000_000, 1_000_000,
+    )(place, memory_in, norm_gain.reshape(1, emb))
+    weights = [qkv_weight, out_weight, key_weight]
     block = jax.ShapeDtypeStruct((band_rows, own_cols), jnp.bfloat16)
     memory, *key_sent = call(
         functools.partial(encode_kernel, n_seq, band_rows),
         [jax.ShapeDtypeStruct((rows, emb), jnp.bfloat16)] + [block] * n_seq,
-        2, 6, 1_600_000_000, 8_000_000,
-    )(place, shift_offsets, rolled_own, halo, norm_gain.reshape(1, emb), *weights[:3])
+        1, 3, 1_600_000_000, 8_000_000, len(weights),
+        [pltpu.VMEM(w.shape, w.dtype) for w in weights] + [pltpu.SemaphoreType.DMA((5,))],
+        ENCODE_LIMIT,
+    )(place, rolled_own, halo, gain, *weights)
     value_sent = call(
         functools.partial(value_kernel, n_seq), [block] * n_seq, 1, 2, 300_000_000, 2_000_000
-    )(place, memory, weights[3])
+    )(place, memory, value_weight)
 
     piece = jax.ShapeDtypeStruct((pos, own_cols), jnp.bfloat16)
 
@@ -214,14 +217,18 @@
             functools.partial(select_kernel, n_seq, 0, 1),
             [piece], 1, 1 + n_seq, 300_000_000, 1_000_000,
         )(place, order, *held)
+        return [*kept, *arrived]
+
+    def by_page(blocks):
         page = jnp.arange(n_tensor)[:, None, None]
-        result = kept[0][None]
+        result = blocks[0][None]
         for d in range(1, n_tensor):
             came = page == (lax.axis_index("tensor") - d) % n_tensor
-            result = jnp.where(came, arrived[d - 1][None], result)
+            result = jnp.where(came, blocks[d][None], result)
         return jnp.broadcast_to(result, (n_tensor, pos, own_cols))
 
-    return gathered(key_sent), gathered(value_sent)
+    key_out, value_blocks = lax.optimization_barrier((by_page(gathered(key_sent)), gathered(value_sent)))
+    return key_out, by_page(value_blocks)
 
 
 def solution(mesh):

time: 43.8 us -> 41.8 us (0.954)
  local copies, waits for them, and re-layouts: 9.12 us -> 4.2 us
  other arithmetic: 1.75 us -> 3.65 us
  Pallas kernels: 10.1 us -> 11.2 us
  starting transfers between devices: 17.1 us -> 17.7 us
  waiting for transfers between devices: 4.67 us -> 4.08 us
    unnamed x16 -> x8, local copies, waits for them, and re-layouts: 7.93 us -> 1.67 us
    pallas_call x1, Pallas kernels: 3.78 us -> 5.61 us  [local(): call(functools.partial(encode_kernel, n_seq, band_rows), [jax.ShapeDtypeS...]
    slice x0 -> x1, local copies, waits for them, and re-layouts: none -> 1.35 us  [local(): shift_offsets[0, 0]]
    another operation x1, other arithmetic: 0.08 us -> 1.35 us  [local(): jnp.stack([lax.axis_index('seq'), lax.axis_index('tensor'), shift_offsets...]
    pallas_call x1, Pallas kernels: 1.53 us -> 0.79 us  [local(): call(stage_kernel, [jax.ShapeDtypeStruct((rows, emb), jnp.bfloat16), jax....]
    select_n x1 -> x2, other arithmetic: 1.67 us -> 2.29 us  [by_page(): result = jnp.where(came, blocks[d][None], result)]
    ppermute x9, waiting for transfers between devices: 4.67 us -> 4.08 us  [rotated(): lax.ppermute(block, axis, [(i, (i + distance) % devices) for i in range(d...]
    ppermute x9, starting transfers between devices: 17.1 us -> 17.7 us  [rotated(): lax.ppermute(block, axis, [(i, (i + distance) % devices) for i in range(d...]
  transfers between devices with their start and end apart: 9 -> 9, of which waited for: 2 -> 5; matrix products, arithmetic and copies ran while one was open for 1% -> 10% of each run, Pallas kernels for 15% -> 13%
where the time goes in v3:
time: 41.8 us; the launch traced here: 41.6 us
  starting transfers between devices  17.7 us (42%)
  Pallas kernels  11.2 us (27%)
  local copies, waits for them, and re-layouts  4.2 us (10%)
  waiting for transfers between devices  4.08 us (10%)
  other arithmetic  3.65 us (9%)
  between operations  0.74 us (2%)
    ppermute x9, starting transfers between devices, rotated(): lax.ppermute(block, axis, [(i, (i + distance) % devices) for i in range(d...  17.7 us
    pallas_call x1, Pallas kernels, local(): call(functools.partial(encode_kernel, n_seq, band_rows), [jax.ShapeDtypeS...  5.61 us
    ppermute x9, waiting for transfers between devices, rotated(): lax.ppermute(block, axis, [(i, (i + distance) % devices) for i in range(d...  4.08 us
    select_n x2, other arithmetic, by_page(): result = jnp.where(came, blocks[d][None], result)  2.29 us
    pallas_call x2, Pallas kernels, gathered(): call(functools.partial(select_kernel, n_seq, 1, n_tensor - 1), [piece] *...  1.87 us
    pallas_call x2, Pallas kernels, gathered(): call(functools.partial(select_kernel, n_seq, 0, 1), [piece], 1, 1 + n_seq...  1.85 us
    unnamed x8, local copies, waits for them, and re-layouts  1.67 us
    another operation x1, other arithmetic, local(): jnp.stack([lax.axis_index('seq'), lax.axis_index('tensor'), shift_offsets...  1.35 us
  transfers between devices with their start and end apart: 9, of which 5 were waited for; matrix products, arithmetic and copies ran while one was open for 10% of the time, Pallas kernels for 13%

profile of v3, /device:TPU:0, one launch (start us, length us, event | category | flops | bytes accessed | tf_op | source)
XLA Modules:
  0.0 41.6 jit_solution(10565688597418398723)
XLA Ops:
  0.6 0.0 copy-start
  0.6 1.0 %slice_bitcast_fusion = bf16[126,1024]{1,0:T(8,128)(2,1)S(1)} fusion(bf16[1,147,1024]{2,1,0:T(8,128)(2,1)} %pages_ref.1), kind=kLoop, calls=%fused_computation.2 | loop fusion | bytes 516096 | tf_op jit(solution)/shard_map/squeeze | solution.py:182
  1.6 5.1 %collective-permute-start = (bf16[126,1024]{1,0:T(8,128)(2,1)S(1)}, bf16[126,1024]{1,0:T(8,128)(2,1)S(1)}, u32[]{:S(2)}, u32[]{:S(2)}) collective-permute-start(bf16[126,1024]{1,0:T(8,128)(2,1)S(1)} %slice_bitcast_fusion), channel_id=1, source_target_pairs={{0,6},{2,0},{4,2},{6,4},{1,7},{3,1},{5,3},{7,5},{8,14},{10,8},{12,... | collective-permute-start | bytes 774152 | tf_op jit(solution)/shard_map/ppermute | solution.py:23
  6.7 1.3 %fusion = (s32[1,1]{1,0:T(1,128)}, s32[1,1]{1,0:T(1,128)}) fusion(s32[1,2]{1,0:T(1,128)} %param.14), kind=kLoop, calls=%fused_computation.6 | loop fusion | bytes 16 | tf_op jit(solution)/shard_map/slice | solution.py:180
  8.1 1.4 %pad_add_fusion.place = s32[4]{0:T(128)S(1)} fusion(s32[1]{0:T(128)} %bitcast.3, s32[1]{0:T(128)} %bitcast.2, s32[1]{0:T(128)} %bitcast.1, s32[1]{0:T(128)} %bitcast), kind=kLoop, calls=%fused_computation.4 | loop fusion | flops 12 | bytes 32 | tf_op jit(solution)/shard_map/stack | solution.py:179
  9.4 1.0 %copy-done.2 = bf16[1,147,1024]{2,1,0:T(8,128)(2,1)S(1)} copy-done((bf16[1,147,1024]{2,1,0:T(8,128)(2,1)S(1)}, bf16[1,147,1024]{2,1,0:T(8,128)(2,1)}, u32[]{:S(2)}) %copy-start.2) | copy-done | bytes 301080
  10.4 0.7 %copy-done.3 = f32[1024]{0:T(1024)S(1)} copy-done((f32[1024]{0:T(1024)S(1)}, f32[1024]{0:T(1024)}, u32[]{:S(2)}) %copy-start.3) | copy-done | bytes 4120
  11.1 0.8 %shard_map.95 = (bf16[160,1024]{1,0:T(8,128)(2,1)S(1)}, f32[1,1024]{1,0:T(1,128)S(1)}) custom-call(s32[4]{0:T(128)S(1)} %pad_add_fusion.place, bf16[1,147,1024]{2,1,0:T(8,128)(2,1)S(1)} %copy-done.2, f32[1,1024]{1,0:T(1,128)S(1)} %bitcast.7), custom_call_target="tpu_custom_call" | custom-call | flops 50000000 | bytes 1000000 | tf_op jit(solution)/shard_map/pallas_call | solution.py:186
  11.9 0.4 collective-permute-done.halo_ref
  12.3 5.6 %shard_map.96 = (bf16[160,1024]{1,0:T(8,128)(2,1)S(1)}, bf16[147,256]{1,0:T(8,128)(2,1)S(1)}, bf16[147,256]{1,0:T(8,128)(2,1)S(1)}, bf16[147,256]{1,0:T(8,128)(2,1)S(1)}, bf16[147,256]{1,0:T(8,128)(2,1)S(1)}) custom-call(s32[4]{0:T(128)S(1)} %pad_add_fusion.place, bf16[160,1024]{1,0:T(8,128)(2,1)S(1)} %get-tuple-element.16.rolled_ref, ...), custom_call_target="tpu_custom_call" | custom-call | flops 1600000000 | bytes 8000000 | tf_op jit(solution)/shard_map/pallas_call | solution.py:196
  17.9 0.5 %collective-permute-start.1 = (bf16[147,256]{1,0:T(8,128)(2,1)S(1)}, bf16[147,256]{1,0:T(8,128)(2,1)S(1)}, u32[]{:S(2)}, u32[]{:S(2)}) collective-permute-start(bf16[147,256]{1,0:T(8,128)(2,1)S(1)} %get-tuple-element.19), channel_id=1, source_target_pairs={{0,2},{2,4},{4,6},{6,0},{1,3},{3,5},{5,7},{7,1},{8,10},{10,12},{12... | collective-permute-start | bytes 225800 | tf_op jit(solution)/shard_map/ppermute | solution.py:23
  18.4 4.4 %collective-permute-start.2 = (bf16[147,256]{1,0:T(8,128)(2,1)S(1)}, bf16[147,256]{1,0:T(8,128)(2,1)S(1)}, u32[]{:S(2)}, u32[]{:S(2)}) collective-permute-start(bf16[147,256]{1,0:T(8,128)(2,1)S(1)} %get-tuple-element.20), channel_id=1, source_target_pairs={{0,4},{2,6},{4,0},{6,2},{1,5},{3,7},{5,1},{7,3},{8,12},{10,14},{12... | collective-permute-start | bytes 225800 | tf_op jit(solution)/shard_map/ppermute | solution.py:23
  22.8 0.0 collective-permute-start.3
  22.8 0.2 reshape.22.order_ref
  23.1 1.1 %shard_map.99 = (bf16[147,256]{1,0:T(8,128)(2,1)S(1)}, bf16[147,256]{1,0:T(8,128)(2,1)S(1)}, bf16[147,256]{1,0:T(8,128)(2,1)S(1)}, bf16[147,256]{1,0:T(8,128)(2,1)S(1)}) custom-call(s32[4]{0:T(128)S(1)} %pad_add_fusion.place, bf16[160,1024]{1,0:T(8,128)(2,1)S(1)} %get-tuple-element.22.memory_ref, bf16[1024,1024]{1,0:T(8,128)(2,1)S(1)} %copy-done.1), custom_call_target="tpu_custom_call" | custom-call | flops 300000000 | bytes 2000000 | tf_op jit(solution)/shard_map/pallas_call | solution.py:203
  24.1 2.1 %collective-permute-start.5 = (bf16[147,256]{1,0:T(8,128)(2,1)S(1)}, bf16[147,256]{1,0:T(8,128)(2,1)S(1)}, u32[]{:S(2)}, u32[]{:S(2)}) collective-permute-start(bf16[147,256]{1,0:T(8,128)(2,1)S(1)} %get-tuple-element.24), channel_id=1, source_target_pairs={{0,2},{2,4},{4,6},{6,0},{1,3},{3,5},{5,7},{7,1},{8,10},{10,12},{12... | collective-permute-start | bytes 225800 | tf_op jit(solution)/shard_map/ppermute | solution.py:23
  26.2 0.0 collective-permute-start.6
  26.2 2.4 %collective-permute-start.7 = (bf16[147,256]{1,0:T(8,128)(2,1)S(1)}, bf16[147,256]{1,0:T(8,128)(2,1)S(1)}, u32[]{:S(2)}, u32[]{:S(2)}) collective-permute-start(bf16[147,256]{1,0:T(8,128)(2,1)S(1)} %get-tuple-element.26), channel_id=1, source_target_pairs={{0,6},{2,0},{4,2},{6,4},{1,7},{3,1},{5,3},{7,5},{8,14},{10,8},{12,... | collective-permute-start | bytes 225800 | tf_op jit(solution)/shard_map/ppermute | solution.py:23
  28.7 0.5 %collective-permute-done.2.refs_2_ = bf16[147,256]{1,0:T(8,128)(2,1)S(1)} collective-permute-done((bf16[147,256]{1,0:T(8,128)(2,1)S(1)}, bf16[147,256]{1,0:T(8,128)(2,1)S(1)}, u32[]{:S(2)}, u32[]{:S(2)}) %collective-permute-start.2) | collective-permute-done | bytes 75296 | tf_op jit(solution)/shard_map/ppermute | solution.py:23
  29.2 0.1 collective-permute-done.3.refs_3_
  29.4 0.9 %shard_map.97 = bf16[294,256]{1,0:T(8,128)(2,1)S(1)} custom-call(s32[4]{0:T(128)S(1)} %pad_add_fusion.place, s32[2,294,1]{2,1,0:T(8,128)S(1)} %reshape.22.order_ref, bf16[147,256]{1,0:T(8,128)(2,1)S(1)} %get-tuple-element.18.refs_0_, bf16[147,256]{1,0:T(8,128)(2,1)S(1)} %collective-permute-done.1.refs_1_, ...), custom_call_target="tpu_custom_call" | custom-call | flops 300000000 | bytes 1000000 | tf_op jit(solution)/shard_map/pallas_call | solution.py:211
  30.3 1.6 %collective-permute-start.4 = (bf16[294,256]{1,0:T(8,128)(2,1)S(1)}, bf16[294,256]{1,0:T(8,128)(2,1)S(1)}, u32[]{:S(2)}, u32[]{:S(2)}) collective-permute-start(bf16[294,256]{1,0:T(8,128)(2,1)S(1)} %shard_map.97), channel_id=1, source_target_pairs={{0,1},{1,0},{2,3},{3,2},{4,5},{5,4},{6,7},{7,6},{8,9},{9,8},{10,11... | collective-permute-start | bytes 451592 | tf_op jit(solution)/shard_map/ppermute | solution.py:23
  31.9 0.0 collective-permute-done.5.refs_1_
  31.9 2.3 %collective-permute-done.6.refs_2_ = bf16[147,256]{1,0:T(8,128)(2,1)S(1)} collective-permute-done((bf16[147,256]{1,0:T(8,128)(2,1)S(1)}, bf16[147,256]{1,0:T(8,128)(2,1)S(1)}, u32[]{:S(2)}, u32[]{:S(2)}) %collective-permute-start.6) | collective-permute-done | bytes 75296 | tf_op jit(solution)/shard_map/ppermute | solution.py:23
  34.2 0.0 collective-permute-done.7.refs_3_
  34.2 0.9 %shard_map.101 = bf16[294,256]{1,0:T(8,128)(2,1)S(1)} custom-call(s32[4]{0:T(128)S(1)} %pad_add_fusion.place, s32[2,294,1]{2,1,0:T(8,128)S(1)} %reshape.22.order_ref, bf16[147,256]{1,0:T(8,128)(2,1)S(1)} %get-tuple-element.23.refs_0_, bf16[147,256]{1,0:T(8,128)(2,1)S(1)} %collective-permute-done.5.refs_1_, ...), custom_call_target="tpu_custom_call" | custom-call | flops 300000000 | bytes 1000000 | tf_op jit(solution)/shard_map/pallas_call | solution.py:211
  35.2 1.6 %collective-permute-start.8 = (bf16[294,256]{1,0:T(8,128)(2,1)S(1)}, bf16[294,256]{1,0:T(8,128)(2,1)S(1)}, u32[]{:S(2)}, u32[]{:S(2)}) collective-permute-start(bf16[294,256]{1,0:T(8,128)(2,1)S(1)} %shard_map.101), channel_id=1, source_target_pairs={{0,1},{1,0},{2,3},{3,2},{4,5},{5,4},{6,7},{7,6},{8,9},{9,8},{10,11... | collective-permute-start | bytes 451592 | tf_op jit(solution)/shard_map/ppermute | solution.py:23
  36.7 0.9 %shard_map.100 = bf16[294,256]{1,0:T(8,128)(2,1)S(1)} custom-call(s32[4]{0:T(128)S(1)} %pad_add_fusion.place, s32[2,294,1]{2,1,0:T(8,128)S(1)} %reshape.22.order_ref, bf16[147,256]{1,0:T(8,128)(2,1)S(1)} %get-tuple-element.23.refs_0_, bf16[147,256]{1,0:T(8,128)(2,1)S(1)} %collective-permute-done.5.refs_1_, ...), custom_call_target="tpu_custom_call" | custom-call | flops 300000000 | bytes 1000000 | tf_op jit(solution)/shard_map/pallas_call | solution.py:216
  37.7 0.9 %shard_map.98 = bf16[294,256]{1,0:T(8,128)(2,1)S(1)} custom-call(s32[4]{0:T(128)S(1)} %pad_add_fusion.place, s32[2,294,1]{2,1,0:T(8,128)S(1)} %reshape.22.order_ref, bf16[147,256]{1,0:T(8,128)(2,1)S(1)} %get-tuple-element.18.refs_0_, bf16[147,256]{1,0:T(8,128)(2,1)S(1)} %collective-permute-done.1.refs_1_, ...), custom_call_target="tpu_custom_call" | custom-call | flops 300000000 | bytes 1000000 | tf_op jit(solution)/shard_map/pallas_call | solution.py:216
  38.6 1.1 %broadcast_select_fusion.1 = bf16[2,294,256]{2,0,1:T(2,128)(2,1)} fusion(pred[2]{0:T(512)(128)(4,1)S(1)} %iota_compare_fusion, bf16[294,256]{1,0:T(8,128)(2,1)S(1)} %shard_map.98, bf16[294,256]{1,0:T(8,128)(2,1)S(1)} %collective-permute-done.4), kind=kLoop, calls=%fused_computation.1 | loop fusion | flops 150528 | bytes 602114 | tf_op jit(solution)/shard_map/jit(_where)/select_n | solution.py:227
  39.8 0.6 %collective-permute-done.8 = bf16[294,256]{1,0:T(8,128)(2,1)S(1)} collective-permute-done((bf16[294,256]{1,0:T(8,128)(2,1)S(1)}, bf16[294,256]{1,0:T(8,128)(2,1)S(1)}, u32[]{:S(2)}, u32[]{:S(2)}) %collective-permute-start.8) | collective-permute-done | bytes 150560 | tf_op jit(solution)/shard_map/ppermute | solution.py:23
  40.4 1.1 %broadcast_select_fusion = bf16[2,294,256]{2,0,1:T(2,128)(2,1)} fusion(pred[2]{0:T(512)(128)(4,1)S(1)} %iota_compare_fusion, bf16[294,256]{1,0:T(8,128)(2,1)S(1)} %shard_map.100, bf16[294,256]{1,0:T(8,128)(2,1)S(1)} %collective-permute-done.8), kind=kLoop, calls=%fused_computation | loop fusion | flops 150528 | bytes 602114 | tf_op jit(solution)/shard_map/jit(_where)/select_n | solution.py:227
  (9 shorter events, 0.0 us)
Async XLA Ops:
  0.6 22.2 %copy-start = (s32[2,588]{1,0:T(2,128)S(1)}, s32[2,588]{1,0:T(2,128)}, u32[]{:S(2)}) copy-start(s32[2,588]{1,0:T(2,128)} %param.15) | copy-start | bytes 14116
  1.6 10.7 %collective-permute-start = (bf16[126,1024]{1,0:T(8,128)(2,1)S(1)}, bf16[126,1024]{1,0:T(8,128)(2,1)S(1)}, u32[]{:S(2)}, u32[]{:S(2)}) collective-permute-start(bf16[126,1024]{1,0:T(8,128)(2,1)S(1)} %slice_bitcast_fusion), channel_id=1, source_target_pairs={{0,6},{2,0},{4,2},{6,4},{1,7},{3,1},{5,3},{7,5},{8,14},{10,8},{12,... | collective-permute-start | bytes 774152 | tf_op jit(solution)/shard_map/ppermute | solution.py:23
  9.4 1.0 %copy-start.2 = (bf16[1,147,1024]{2,1,0:T(8,128)(2,1)S(1)}, bf16[1,147,1024]{2,1,0:T(8,128)(2,1)}, u32[]{:S(2)}) copy-start(bf16[1,147,1024]{2,1,0:T(8,128)(2,1)} %pages_ref.1) | copy-start | bytes 903172
  10.4 0.7 %copy-start.3 = (f32[1024]{0:T(1024)S(1)}, f32[1024]{0:T(1024)}, u32[]{:S(2)}) copy-start(f32[1024]{0:T(1024)} %param.9) | copy-start | bytes 12292
  12.3 10.8 %copy-start.1 = (bf16[1024,1024]{1,0:T(8,128)(2,1)S(1)}, bf16[1024,1024]{1,0:T(8,128)(2,1)}, u32[]{:S(2)}) copy-start(bf16[1024,1024]{1,0:T(8,128)(2,1)} %weight_ref.1) | copy-start | bytes 6291460
  17.9 8.3 %collective-permute-start.1 = (bf16[147,256]{1,0:T(8,128)(2,1)S(1)}, bf16[147,256]{1,0:T(8,128)(2,1)S(1)}, u32[]{:S(2)}, u32[]{:S(2)}) collective-permute-start(bf16[147,256]{1,0:T(8,128)(2,1)S(1)} %get-tuple-element.19), channel_id=1, source_target_pairs={{0,2},{2,4},{4,6},{6,0},{1,3},{3,5},{5,7},{7,1},{8,10},{10,12},{12... | collective-permute-start | bytes 225800 | tf_op jit(solution)/shard_map/ppermute | solution.py:23
  18.4 10.8 %collective-permute-start.2 = (bf16[147,256]{1,0:T(8,128)(2,1)S(1)}, bf16[147,256]{1,0:T(8,128)(2,1)S(1)}, u32[]{:S(2)}, u32[]{:S(2)}) collective-permute-start(bf16[147,256]{1,0:T(8,128)(2,1)S(1)} %get-tuple-element.20), channel_id=1, source_target_pairs={{0,4},{2,6},{4,0},{6,2},{1,5},{3,7},{5,1},{7,3},{8,12},{10,14},{12... | collective-permute-start | bytes 225800 | tf_op jit(solution)/shard_map/ppermute | solution.py:23
  22.8 6.5 %collective-permute-start.3 = (bf16[147,256]{1,0:T(8,128)(2,1)S(1)}, bf16[147,256]{1,0:T(8,128)(2,1)S(1)}, u32[]{:S(2)}, u32[]{:S(2)}) collective-permute-start(bf16[147,256]{1,0:T(8,128)(2,1)S(1)} %get-tuple-element.21), channel_id=1, source_target_pairs={{0,6},{2,0},{4,2},{6,4},{1,7},{3,1},{5,3},{7,5},{8,14},{10,8},{12,... | collective-permute-start | bytes 225800 | tf_op jit(solution)/shard_map/ppermute | solution.py:23
  24.1 7.7 %collective-permute-start.5 = (bf16[147,256]{1,0:T(8,128)(2,1)S(1)}, bf16[147,256]{1,0:T(8,128)(2,1)S(1)}, u32[]{:S(2)}, u32[]{:S(2)}) collective-permute-start(bf16[147,256]{1,0:T(8,128)(2,1)S(1)} %get-tuple-element.24), channel_id=1, source_target_pairs={{0,2},{2,4},{4,6},{6,0},{1,3},{3,5},{5,7},{7,1},{8,10},{10,12},{12... | collective-permute-start | bytes 225800 | tf_op jit(solution)/shard_map/ppermute | solution.py:23
  26.2 8.0 %collective-permute-start.6 = (bf16[147,256]{1,0:T(8,128)(2,1)S(1)}, bf16[147,256]{1,0:T(8,128)(2,1)S(1)}, u32[]{:S(2)}, u32[]{:S(2)}) collective-permute-start(bf16[147,256]{1,0:T(8,128)(2,1)S(1)} %get-tuple-element.25), channel_id=1, source_target_pairs={{0,4},{2,6},{4,0},{6,2},{1,5},{3,7},{5,1},{7,3},{8,12},{10,14},{12... | collective-permute-start | bytes 225800 | tf_op jit(solution)/shard_map/ppermute | solution.py:23
  26.2 8.0 %collective-permute-start.7 = (bf16[147,256]{1,0:T(8,128)(2,1)S(1)}, bf16[147,256]{1,0:T(8,128)(2,1)S(1)}, u32[]{:S(2)}, u32[]{:S(2)}) collective-permute-start(bf16[147,256]{1,0:T(8,128)(2,1)S(1)} %get-tuple-element.26), channel_id=1, source_target_pairs={{0,6},{2,0},{4,2},{6,4},{1,7},{3,1},{5,3},{7,5},{8,14},{10,8},{12,... | collective-permute-start | bytes 225800 | tf_op jit(solution)/shard_map/ppermute | solution.py:23
  30.3 8.3 %collective-permute-start.4 = (bf16[294,256]{1,0:T(8,128)(2,1)S(1)}, bf16[294,256]{1,0:T(8,128)(2,1)S(1)}, u32[]{:S(2)}, u32[]{:S(2)}) collective-permute-start(bf16[294,256]{1,0:T(8,128)(2,1)S(1)} %shard_map.97), channel_id=1, source_target_pairs={{0,1},{1,0},{2,3},{3,2},{4,5},{5,4},{6,7},{7,6},{8,9},{9,8},{10,11... | collective-permute-start | bytes 451592 | tf_op jit(solution)/shard_map/ppermute | solution.py:23
  35.2 5.3 %collective-permute-start.8 = (bf16[294,256]{1,0:T(8,128)(2,1)S(1)}, bf16[294,256]{1,0:T(8,128)(2,1)S(1)}, u32[]{:S(2)}, u32[]{:S(2)}) collective-permute-start(bf16[294,256]{1,0:T(8,128)(2,1)S(1)} %shard_map.101), channel_id=1, source_target_pairs={{0,1},{1,0},{2,3},{3,2},{4,5},{5,4},{6,7},{7,6},{8,9},{9,8},{10,11... | collective-permute-start | bytes 451592 | tf_op jit(solution)/shard_map/ppermute | solution.py:23

commit v4 on v3

--- a/solution.py
+++ b/solution.py
@@ -15,7 +15,12 @@
 
 GROUP = 8
 VMEM_LIMIT = 32 * 1024 * 1024
+STAGE_LIMIT = 48 * 1024 * 1024
 ENCODE_LIMIT = 52 * 1024 * 1024
+
+SMEM = pl.BlockSpec(memory_space=pltpu.SMEM)
+VMEM = pl.BlockSpec(memory_space=pltpu.VMEM)
+HBM = pl.BlockSpec(memory_space=pltpu.HBM)
 
 
 def rotated(block, axis, distance):
@@ -31,41 +36,45 @@
     return jnp.where(cond, 1.0, 0.0).astype(jnp.bfloat16)
 
 
-def stage_kernel(place, pages_ref, gain_ref, rolled_ref, gain_out):
+def stage_kernel(shifts, pages_ref, gain_ref, weight_hbm, rolled_ref, gain_out, weight_ref, arrived):
+    copy = pltpu.make_async_copy(weight_hbm, weight_ref, arrived)
+    copy.start()
     gain_out[...] = gain_ref[...]
     band_rows = pages_ref.shape[1]
     rows = rolled_ref.shape[0]
-    source = roll_source(rows, band_rows, place)
+    source = roll_source(rows, band_rows, shifts)
     take = one_hot(source == lax.broadcasted_iota(jnp.int32, (rows, band_rows), 1))
     rolled_ref[...] = dot(take, pages_ref[0]).astype(jnp.bfloat16)
-
-
-def roll_source(rows, band_rows, place):
+    copy.wait()
+
+
+def roll_source(rows, band_rows, shifts):
     cell = lax.broadcasted_iota(jnp.int32, (rows, 1), 0)
     cell_row = cell // GRID_W
-    from_col = cell - cell_row * GRID_W + place[3]
+    from_col = cell - cell_row * GRID_W + shifts[0, 1]
     from_col = jnp.where(from_col >= GRID_W, from_col - GRID_W, from_col)
-    return jnp.where(cell < band_rows, (cell_row + place[2]) * GRID_W + from_col, -1)
+    return jnp.where(cell < band_rows, (cell_row + shifts[0, 0]) * GRID_W + from_col, -1)
 
 
 def encode_kernel(
-    n_seq, band_rows, place, rolled_ref, halo_ref, gain_ref, qkv_hbm, out_hbm, key_hbm,
-    memory_ref, *refs
+    n_seq, band_rows, place, shifts, rolled_ref, halo_ref, gain_ref, qkv_ref, *refs
 ):
-    sent, (qkv_ref, out_ref, key_ref, arrived) = refs[:n_seq], refs[n_seq:]
+    in_hbm, refs = refs[:3], refs[3:]
+    key_sent, value_sent, refs = refs[:n_seq], refs[n_seq : 2 * n_seq], refs[2 * n_seq :]
+    on_chip, arrived = refs[:3], refs[3]
+    out_ref, key_ref, value_ref = on_chip
+    copies = [
+        pltpu.make_async_copy(in_hbm[i], on_chip[i], arrived.at[i]) for i in range(len(on_chip))
+    ]
+    for copy in copies:
+        copy.start()
     halo_rows = halo_ref.shape[0]
     rows = rolled_ref.shape[0]
     attn = HEADS * HEAD_DIM
     seq = place[0]
-    thirds = [pl.ds(i * attn, attn) for i in range(3)]
-    pairs = [(qkv_hbm.at[:, third], qkv_ref.at[:, third]) for third in thirds]
-    pairs += [(out_hbm, out_ref), (key_hbm, key_ref)]
-    copies = [pltpu.make_async_copy(*pair, arrived.at[i]) for i, pair in enumerate(pairs)]
-    for copy in copies:
-        copy.start()
-    row_shift, col_shift = place[2], place[3]
-
-    source = roll_source(rows, band_rows, place) - band_rows
+    row_shift, col_shift = shifts[0, 0], shifts[0, 1]
+
+    source = roll_source(rows, band_rows, shifts) - band_rows
     take = one_hot(source == lax.broadcasted_iota(jnp.int32, (rows, halo_rows), 1))
     rolled = rolled_ref[...].astype(jnp.float32) + dot(take, halo_ref[...])
 
@@ -73,11 +82,8 @@
     centred = rolled - mean
     variance = jnp.mean(centred * centred, axis=-1, keepdims=True)
     normed = (centred * lax.rsqrt(variance + 1e-05) * gain_ref[...]).astype(jnp.bfloat16)
-    parts = []
-    for third, copy in zip(thirds, copies):
-        copy.wait()
-        parts.append(dot(normed, qkv_ref[:, third]).astype(jnp.bfloat16))
-    queries, keys, values = parts
+    qkv = dot(normed, qkv_ref[...]).astype(jnp.bfloat16)
+    queries, keys, values = (qkv[:, i * attn : (i + 1) * attn] for i in range(3))
 
     def marks(index):
         row = index // GRID_W
@@ -113,11 +119,12 @@
             part = jnp.where(lane_head == h, mixed[h * rows : (h + 1) * rows], part)
         parts.append(part.astype(jnp.bfloat16))
     attended = jnp.concatenate(parts, axis=1)
-    copies[3].wait()
+    copies[0].wait()
     memory = (rolled + dot(attended, out_ref[...])).astype(jnp.bfloat16)
-    memory_ref[...] = memory
-    copies[4].wait()
-    project(n_seq, seq, memory, key_ref, sent)
+    copies[1].wait()
+    project(n_seq, seq, memory, key_ref, key_sent)
+    copies[2].wait()
+    project(n_seq, seq, memory, value_ref, value_sent)
 
 
 def project(n_seq, seq, memory, weight_ref, sent):
@@ -127,10 +134,6 @@
         cols = pl.ds(pl.multiple_of(to * own_cols, own_cols), own_cols)
         block = dot(memory, weight_ref[:, cols])
         sent[d][...] = block[: sent[d].shape[0]].astype(jnp.bfloat16)
-
-
-def value_kernel(n_seq, place, memory_ref, weight_ref, *sent):
-    project(n_seq, place[0], memory_ref[...], weight_ref, sent)
 
 
 def select_kernel(n_seq, first, count, place, order_ref, *refs):
@@ -153,14 +156,11 @@
 
 
 def call(kernel, out_shape, n_scalar, n_vmem, flops, moved, n_hbm=0, scratch=(), limit=VMEM_LIMIT):
-    smem = pl.BlockSpec(memory_space=pltpu.SMEM)
-    vmem = pl.BlockSpec(memory_space=pltpu.VMEM)
-    hbm = pl.BlockSpec(memory_space=pltpu.HBM)
     return pl.pallas_call(
         kernel,
         out_shape=out_shape,
-        in_specs=[smem] * n_scalar + [vmem] * n_vmem + [hbm] * n_hbm,
-        out_specs=jax.tree.map(lambda _: vmem, out_shape),
+        in_specs=[SMEM] * n_scalar + [VMEM] * n_vmem + [HBM] * n_hbm,
+        out_specs=jax.tree.map(lambda _: VMEM, out_shape),
         scratch_shapes=list(scratch),
         compiler_params=pltpu.CompilerParams(vmem_limit_bytes=limit),
         cost_estimate=pl.CostEstimate(flops=flops, bytes_accessed=moved, transcendentals=0),
@@ -176,33 +176,30 @@
     own_cols = key_weight.shape[1] // n_seq
     pos = row_order.shape[1] // n_tensor
     rows = -(-band_rows // 16) * 16
-    place = jnp.stack(
-        [lax.axis_index("seq"), lax.axis_index("tensor"), shift_offsets[0, 0], shift_offsets[0, 1]]
-    )
+    place = jnp.stack([lax.axis_index("seq"), lax.axis_index("tensor")]).astype(jnp.int32)
     halo = rotated(memory_in[0, : (WIN - 1) * GRID_W], "seq", -1)
     order = lax.dynamic_index_in_dim(row_order, lax.axis_index("tensor"), 0, False)
     order = order.reshape(n_tensor, pos, 1)
 
-    rolled_own, gain = call(
+    rolled_own, gain, qkv_on_chip = call(
         stage_kernel,
         [
             jax.ShapeDtypeStruct((rows, emb), jnp.bfloat16),
             jax.ShapeDtypeStruct((1, emb), jnp.float32),
+            jax.ShapeDtypeStruct(qkv_weight.shape, qkv_weight.dtype),
         ],
-        1, 2, 50_000_000, 1_000_000,
-    )(place, memory_in, norm_gain.reshape(1, emb))
-    weights = [qkv_weight, out_weight, key_weight]
+        1, 2, 50_000_000, 4_000_000, 1, [pltpu.SemaphoreType.DMA], STAGE_LIMIT,
+    )(shift_offsets, memory_in, norm_gain.reshape(1, emb), qkv_weight)
+    weights = [out_weight, key_weight, value_weight]
     block = jax.ShapeDtypeStruct((band_rows, own_cols), jnp.bfloat16)
-    memory, *key_sent = call(
-        functools.partial(encode_kernel, n_seq, band_rows),
-        [jax.ShapeDtypeStruct((rows, emb), jnp.bfloat16)] + [block] * n_seq,
-        1, 3, 1_600_000_000, 8_000_000, len(weights),
-        [pltpu.VMEM(w.shape, w.dtype) for w in weights] + [pltpu.SemaphoreType.DMA((5,))],
+    sent = call(
+        functools.partial(encode_kernel, n_seq, band_rows), [block] * (2 * n_seq),
+        2, 4, 2_000_000_000, 10_000_000, len(weights),
+        [pltpu.VMEM(w.shape, w.dtype) for w in weights]
+        + [pltpu.SemaphoreType.DMA((len(weights),))],
         ENCODE_LIMIT,
-    )(place, rolled_own, halo, gain, *weights)
-    value_sent = call(
-        functools.partial(value_kernel, n_seq), [block] * n_seq, 1, 2, 300_000_000, 2_000_000
-    )(place, memory, value_weight)
+    )(place, shift_offsets, rolled_own, halo, gain, qkv_on_chip, *weights)
+    key_sent, value_sent = sent[:n_seq], sent[n_seq:]
 
     piece = jax.ShapeDtypeStruct((pos, own_cols), jnp.bfloat16)
 

time: 41.8 us -> 42.6 us (1.019)
  other arithmetic: 3.65 us -> 2.37 us
  local copies, waits for them, and re-layouts: 4.2 us -> 5.14 us
  Pallas kernels: 11.2 us -> 12.1 us
    unnamed x8 -> x12, local copies, waits for them, and re-layouts: 1.67 us -> 3.95 us
    pallas_call x1, Pallas kernels: 0.79 us -> 2.44 us  [local(): call(stage_kernel, [jax.ShapeDtypeStruct((rows, emb), jnp.bfloat16), jax....]
    slice x1 -> x0, local copies, waits for them, and re-layouts: 1.35 us -> none  [local(): shift_offsets[0, 0]]
    another operation x1, other arithmetic: 1.35 us -> 0.07 us  [local(): jnp.stack([lax.axis_index('seq'), lax.axis_index('tensor')])]
    pallas_call x2 -> x1, Pallas kernels: 6.69 us -> 5.95 us  [local(): call(functools.partial(encode_kernel, n_seq, band_rows), [block] * (2 * n...]
  transfers between devices with their start and end apart: 9 -> 9, of which waited for: 5 -> 4; matrix products, arithmetic and copies ran while one was open for 10% -> 3% of each run, Pallas kernels for 13% -> 15%
where the time goes in v4:
time: 42.6 us; the launch traced here: 42.4 us
  starting transfers between devices  17.5 us (41%)
  Pallas kernels  12.1 us (28%)
  local copies, waits for them, and re-layouts  5.14 us (12%)
  waiting for transfers between devices  4.49 us (11%)
  other arithmetic  2.37 us (6%)
  between operations  0.75 us (2%)
    ppermute x9, starting transfers between devices, rotated(): lax.ppermute(block, axis, [(i, (i + distance) % devices) for i in range(d...  17.5 us
    pallas_call x1, Pallas kernels, local(): call(functools.partial(encode_kernel, n_seq, band_rows), [block] * (2 * n...  5.95 us
    ppermute x9, waiting for transfers between devices, rotated(): lax.ppermute(block, axis, [(i, (i + distance) % devices) for i in range(d...  4.49 us
    unnamed x12, local copies, waits for them, and re-layouts  3.95 us
    pallas_call x1, Pallas kernels, local(): call(stage_kernel, [jax.ShapeDtypeStruct((rows, emb), jnp.bfloat16), jax....  2.44 us
    select_n x2, other arithmetic, by_page(): result = jnp.where(came, blocks[d][None], result)  2.29 us
    pallas_call x2, Pallas kernels, gathered(): call(functools.partial(select_kernel, n_seq, 1, n_tensor - 1), [piece] *...  1.88 us
    pallas_call x2, Pallas kernels, gathered(): call(functools.partial(select_kernel, n_seq, 0, 1), [piece], 1, 1 + n_seq...  1.87 us
  transfers between devices with their start and end apart: 9, of which 4 were waited for; matrix products, arithmetic and copies ran while one was open for 3% of the time, Pallas kernels for 15%

profile of v4, /device:TPU:0, one launch (start us, length us, event | category | flops | bytes accessed | tf_op | source)
XLA Modules:
  0.0 42.4 jit_solution(492410543776091341)
XLA Ops:
  0.6 0.0 copy-start
  0.6 0.0 copy-start.5
  0.7 1.0 %slice_bitcast_fusion = bf16[126,1024]{1,0:T(8,128)(2,1)S(1)} fusion(bf16[1,147,1024]{2,1,0:T(8,128)(2,1)} %pages_ref.1), kind=kLoop, calls=%fused_computation.2 | loop fusion | bytes 516096 | tf_op jit(solution)/shard_map/squeeze | solution.py:180
  1.6 5.1 %collective-permute-start = (bf16[126,1024]{1,0:T(8,128)(2,1)S(1)}, bf16[126,1024]{1,0:T(8,128)(2,1)S(1)}, u32[]{:S(2)}, u32[]{:S(2)}) collective-permute-start(bf16[126,1024]{1,0:T(8,128)(2,1)S(1)} %slice_bitcast_fusion), channel_id=1, source_target_pairs={{0,6},{2,0},{4,2},{6,4},{1,7},{3,1},{5,3},{7,5},{8,14},{10,8},{12,... | collective-permute-start | bytes 774152 | tf_op jit(solution)/shard_map/ppermute | solution.py:28
  6.7 1.0 %copy-done.2 = bf16[1,147,1024]{2,1,0:T(8,128)(2,1)S(1)} copy-done((bf16[1,147,1024]{2,1,0:T(8,128)(2,1)S(1)}, bf16[1,147,1024]{2,1,0:T(8,128)(2,1)}, u32[]{:S(2)}) %copy-start.2) | copy-done | bytes 301080
  7.7 0.7 %copy-done.3 = f32[1024]{0:T(1024)S(1)} copy-done((f32[1024]{0:T(1024)S(1)}, f32[1024]{0:T(1024)}, u32[]{:S(2)}) %copy-start.3) | copy-done | bytes 4120
  8.4 0.7 %copy-done.4 = s32[1,2]{1,0:T(1,128)S(1)} copy-done((s32[1,2]{1,0:T(1,128)S(1)}, s32[1,2]{1,0:T(1,128)}, u32[]{:S(2)}) %copy-start.4) | copy-done | bytes 32
  9.1 2.4 %shard_map.95 = (bf16[160,1024]{1,0:T(8,128)(2,1)S(1)}, f32[1,1024]{1,0:T(1,128)S(1)}, bf16[1024,1536]{1,0:T(8,128)(2,1)S(1)}) custom-call(s32[1,2]{1,0:T(1,128)S(1)} %copy-done.4, bf16[1,147,1024]{2,1,0:T(8,128)(2,1)S(1)} %copy-done.2, f32[1,1024]{1,0:T(1,128)S(1)} %bitcast.5, bf16[1024,1536]{1,0:T(8,128)(2,1)} %weight_hbm.1), custom_call_target="tpu_custom_call" | custom-call | flops 50000000 | bytes 4000000 | tf_op jit(solution)/shard_map/pallas_call | solution.py:184
  11.5 1.6 %copy-done.1 = bf16[1024,1536]{1,0:T(8,128)(2,1)} copy-done((bf16[1024,1536]{1,0:T(8,128)(2,1)}, bf16[1024,1536]{1,0:T(8,128)(2,1)S(1)}, u32[]{:S(2)}) %copy-start.1) | copy-done | bytes 3145752
  13.1 0.1 pad_add_fusion.place
  13.2 6.0 %shard_map.96 = (bf16[147,256]{1,0:T(8,128)(2,1)S(1)}, bf16[147,256]{1,0:T(8,128)(2,1)S(1)}, bf16[147,256]{1,0:T(8,128)(2,1)S(1)}, bf16[147,256]{1,0:T(8,128)(2,...) custom-call(s32[2]{0:T(128)S(1)} %pad_add_fusion.place, ...), custom_call_target="tpu_custom_call" | custom-call | flops 2000000000 | bytes 10000000 | tf_op jit(solution)/shard_map/pallas_call | solution.py:195
  19.2 0.1 collective-permute-start.1
  19.2 3.9 %collective-permute-start.2 = (bf16[147,256]{1,0:T(8,128)(2,1)S(1)}, bf16[147,256]{1,0:T(8,128)(2,1)S(1)}, u32[]{:S(2)}, u32[]{:S(2)}) collective-permute-start(bf16[147,256]{1,0:T(8,128)(2,1)S(1)} %get-tuple-element.21), channel_id=1, source_target_pairs={{0,4},{2,6},{4,0},{6,2},{1,5},{3,7},{5,1},{7,3},{8,12},{10,14},{12... | collective-permute-start | bytes 225800 | tf_op jit(solution)/shard_map/ppermute | solution.py:28
  23.2 0.0 collective-permute-start.3
  23.2 0.2 reshape.22.order_ref
  23.4 2.1 %collective-permute-start.5 = (bf16[147,256]{1,0:T(8,128)(2,1)S(1)}, bf16[147,256]{1,0:T(8,128)(2,1)S(1)}, u32[]{:S(2)}, u32[]{:S(2)}) collective-permute-start(bf16[147,256]{1,0:T(8,128)(2,1)S(1)} %get-tuple-element.24), channel_id=1, source_target_pairs={{0,2},{2,4},{4,6},{6,0},{1,3},{3,5},{5,7},{7,1},{8,10},{10,12},{12... | collective-permute-start | bytes 225800 | tf_op jit(solution)/shard_map/ppermute | solution.py:28
  25.5 0.0 collective-permute-start.6
  25.5 0.8 %collective-permute-done.1.refs_1_ = bf16[147,256]{1,0:T(8,128)(2,1)S(1)} collective-permute-done((bf16[147,256]{1,0:T(8,128)(2,1)S(1)}, bf16[147,256]{1,0:T(8,128)(2,1)S(1)}, u32[]{:S(2)}, u32[]{:S(2)}) %collective-permute-start.1) | collective-permute-done | bytes 75296 | tf_op jit(solution)/shard_map/ppermute | solution.py:28
  26.3 3.1 %collective-permute-start.7 = (bf16[147,256]{1,0:T(8,128)(2,1)S(1)}, bf16[147,256]{1,0:T(8,128)(2,1)S(1)}, u32[]{:S(2)}, u32[]{:S(2)}) collective-permute-start(bf16[147,256]{1,0:T(8,128)(2,1)S(1)} %get-tuple-element.26), channel_id=1, source_target_pairs={{0,6},{2,0},{4,2},{6,4},{1,7},{3,1},{5,3},{7,5},{8,14},{10,8},{12,... | collective-permute-start | bytes 225800 | tf_op jit(solution)/shard_map/ppermute | solution.py:28
  29.4 0.9 %collective-permute-done.2.refs_2_ = bf16[147,256]{1,0:T(8,128)(2,1)S(1)} collective-permute-done((bf16[147,256]{1,0:T(8,128)(2,1)S(1)}, bf16[147,256]{1,0:T(8,128)(2,1)S(1)}, u32[]{:S(2)}, u32[]{:S(2)}) %collective-permute-start.2) | collective-permute-done | bytes 75296 | tf_op jit(solution)/shard_map/ppermute | solution.py:28
  30.4 0.0 collective-permute-done.3.refs_3_
  30.4 0.9 %shard_map.97 = bf16[294,256]{1,0:T(8,128)(2,1)S(1)} custom-call(s32[2]{0:T(128)S(1)} %pad_add_fusion.place, s32[2,294,1]{2,1,0:T(8,128)S(1)} %reshape.22.order_ref, bf16[147,256]{1,0:T(8,128)(2,1)S(1)} %get-tuple-element.19.refs_0_, bf16[147,256]{1,0:T(8,128)(2,1)S(1)} %collective-permute-done.1.refs_1_, ...), custom_call_target="tpu_custom_call" | custom-call | flops 300000000 | bytes 1000000 | tf_op jit(solution)/shard_map/pallas_call | solution.py:208
  31.3 1.6 %collective-permute-start.4 = (bf16[294,256]{1,0:T(8,128)(2,1)S(1)}, bf16[294,256]{1,0:T(8,128)(2,1)S(1)}, u32[]{:S(2)}, u32[]{:S(2)}) collective-permute-start(bf16[294,256]{1,0:T(8,128)(2,1)S(1)} %shard_map.97), channel_id=1, source_target_pairs={{0,1},{1,0},{2,3},{3,2},{4,5},{5,4},{6,7},{7,6},{8,9},{9,8},{10,11... | collective-permute-start | bytes 451592 | tf_op jit(solution)/shard_map/ppermute | solution.py:28
  32.9 2.1 %collective-permute-done.6.refs_2_ = bf16[147,256]{1,0:T(8,128)(2,1)S(1)} collective-permute-done((bf16[147,256]{1,0:T(8,128)(2,1)S(1)}, bf16[147,256]{1,0:T(8,128)(2,1)S(1)}, u32[]{:S(2)}, u32[]{:S(2)}) %collective-permute-start.6) | collective-permute-done | bytes 75296 | tf_op jit(solution)/shard_map/ppermute | solution.py:28
  35.0 0.0 collective-permute-done.7.refs_3_
  35.0 0.9 %shard_map.100 = bf16[294,256]{1,0:T(8,128)(2,1)S(1)} custom-call(s32[2]{0:T(128)S(1)} %pad_add_fusion.place, s32[2,294,1]{2,1,0:T(8,128)S(1)} %reshape.22.order_ref, bf16[147,256]{1,0:T(8,128)(2,1)S(1)} %get-tuple-element.23.refs_0_, bf16[147,256]{1,0:T(8,128)(2,1)S(1)} %collective-permute-done.5.refs_1_, ...), custom_call_target="tpu_custom_call" | custom-call | flops 300000000 | bytes 1000000 | tf_op jit(solution)/shard_map/pallas_call | solution.py:208
  36.0 1.6 %collective-permute-start.8 = (bf16[294,256]{1,0:T(8,128)(2,1)S(1)}, bf16[294,256]{1,0:T(8,128)(2,1)S(1)}, u32[]{:S(2)}, u32[]{:S(2)}) collective-permute-start(bf16[294,256]{1,0:T(8,128)(2,1)S(1)} %shard_map.100), channel_id=1, source_target_pairs={{0,1},{1,0},{2,3},{3,2},{4,5},{5,4},{6,7},{7,6},{8,9},{9,8},{10,11... | collective-permute-start | bytes 451592 | tf_op jit(solution)/shard_map/ppermute | solution.py:28
  37.5 0.9 %shard_map.99 = bf16[294,256]{1,0:T(8,128)(2,1)S(1)} custom-call(s32[2]{0:T(128)S(1)} %pad_add_fusion.place, s32[2,294,1]{2,1,0:T(8,128)S(1)} %reshape.22.order_ref, bf16[147,256]{1,0:T(8,128)(2,1)S(1)} %get-tuple-element.23.refs_0_, bf16[147,256]{1,0:T(8,128)(2,1)S(1)} %collective-permute-done.5.refs_1_, ...), custom_call_target="tpu_custom_call" | custom-call | flops 300000000 | bytes 1000000 | tf_op jit(solution)/shard_map/pallas_call | solution.py:213
  38.5 0.9 %shard_map.98 = bf16[294,256]{1,0:T(8,128)(2,1)S(1)} custom-call(s32[2]{0:T(128)S(1)} %pad_add_fusion.place, s32[2,294,1]{2,1,0:T(8,128)S(1)} %reshape.22.order_ref, bf16[147,256]{1,0:T(8,128)(2,1)S(1)} %get-tuple-element.19.refs_0_, bf16[147,256]{1,0:T(8,128)(2,1)S(1)} %collective-permute-done.1.refs_1_, ...), custom_call_target="tpu_custom_call" | custom-call | flops 300000000 | bytes 1000000 | tf_op jit(solution)/shard_map/pallas_call | solution.py:213
  39.4 1.1 %broadcast_select_fusion.1 = bf16[2,294,256]{2,0,1:T(2,128)(2,1)} fusion(pred[2]{0:T(512)(128)(4,1)S(1)} %iota_compare_fusion, bf16[294,256]{1,0:T(8,128)(2,1)S(1)} %shard_map.98, bf16[294,256]{1,0:T(8,128)(2,1)S(1)} %collective-permute-done.4), kind=kLoop, calls=%fused_computation.1 | loop fusion | flops 150528 | bytes 602114 | tf_op jit(solution)/shard_map/jit(_where)/select_n | solution.py:224
  40.6 0.6 %collective-permute-done.8 = bf16[294,256]{1,0:T(8,128)(2,1)S(1)} collective-permute-done((bf16[294,256]{1,0:T(8,128)(2,1)S(1)}, bf16[294,256]{1,0:T(8,128)(2,1)S(1)}, u32[]{:S(2)}, u32[]{:S(2)}) %collective-permute-start.8) | collective-permute-done | bytes 150560 | tf_op jit(solution)/shard_map/ppermute | solution.py:28
  41.2 1.1 %broadcast_select_fusion = bf16[2,294,256]{2,0,1:T(2,128)(2,1)} fusion(pred[2]{0:T(512)(128)(4,1)S(1)} %iota_compare_fusion, bf16[294,256]{1,0:T(8,128)(2,1)S(1)} %shard_map.99, bf16[294,256]{1,0:T(8,128)(2,1)S(1)} %collective-permute-done.8), kind=kLoop, calls=%fused_computation | loop fusion | flops 150528 | bytes 602114 | tf_op jit(solution)/shard_map/jit(_where)/select_n | solution.py:224
  (11 shorter events, 0.0 us)
Async XLA Ops:
  0.6 22.5 %copy-start = (s32[2,588]{1,0:T(2,128)S(1)}, s32[2,588]{1,0:T(2,128)}, u32[]{:S(2)}) copy-start(s32[2,588]{1,0:T(2,128)} %param.15) | copy-start | bytes 14116
  0.6 12.6 %copy-start.5 = (s32[1,2]{1,0:T(1,128)S(1)}, s32[1,2]{1,0:T(1,128)}, u32[]{:S(2)}) copy-start(s32[1,2]{1,0:T(1,128)} %shifts.3) | copy-start | bytes 28
  1.6 11.6 %collective-permute-start = (bf16[126,1024]{1,0:T(8,128)(2,1)S(1)}, bf16[126,1024]{1,0:T(8,128)(2,1)S(1)}, u32[]{:S(2)}, u32[]{:S(2)}) collective-permute-start(bf16[126,1024]{1,0:T(8,128)(2,1)S(1)} %slice_bitcast_fusion), channel_id=1, source_target_pairs={{0,6},{2,0},{4,2},{6,4},{1,7},{3,1},{5,3},{7,5},{8,14},{10,8},{12,... | collective-permute-start | bytes 774152 | tf_op jit(solution)/shard_map/ppermute | solution.py:28
  6.7 1.0 %copy-start.2 = (bf16[1,147,1024]{2,1,0:T(8,128)(2,1)S(1)}, bf16[1,147,1024]{2,1,0:T(8,128)(2,1)}, u32[]{:S(2)}) copy-start(bf16[1,147,1024]{2,1,0:T(8,128)(2,1)} %pages_ref.1) | copy-start | bytes 903172
  7.7 0.7 %copy-start.3 = (f32[1024]{0:T(1024)S(1)}, f32[1024]{0:T(1024)}, u32[]{:S(2)}) copy-start(f32[1024]{0:T(1024)} %param.9) | copy-start | bytes 12292
  8.4 0.7 %copy-start.4 = (s32[1,2]{1,0:T(1,128)S(1)}, s32[1,2]{1,0:T(1,128)}, u32[]{:S(2)}) copy-start(s32[1,2]{1,0:T(1,128)} %shifts.3) | copy-start | bytes 28
  11.5 1.6 %copy-start.1 = (bf16[1024,1536]{1,0:T(8,128)(2,1)}, bf16[1024,1536]{1,0:T(8,128)(2,1)S(1)}, u32[]{:S(2)}) copy-start(bf16[1024,1536]{1,0:T(8,128)(2,1)S(1)} %get-tuple-element.18.qkv_ref) | copy-start | bytes 9437188
  19.2 7.2 %collective-permute-start.1 = (bf16[147,256]{1,0:T(8,128)(2,1)S(1)}, bf16[147,256]{1,0:T(8,128)(2,1)S(1)}, u32[]{:S(2)}, u32[]{:S(2)}) collective-permute-start(bf16[147,256]{1,0:T(8,128)(2,1)S(1)} %get-tuple-element.20), channel_id=1, source_target_pairs={{0,2},{2,4},{4,6},{6,0},{1,3},{3,5},{5,7},{7,1},{8,10},{10,12},{12... | collective-permute-start | bytes 225800 | tf_op jit(solution)/shard_map/ppermute | solution.py:28
  19.2 11.1 %collective-permute-start.2 = (bf16[147,256]{1,0:T(8,128)(2,1)S(1)}, bf16[147,256]{1,0:T(8,128)(2,1)S(1)}, u32[]{:S(2)}, u32[]{:S(2)}) collective-permute-start(bf16[147,256]{1,0:T(8,128)(2,1)S(1)} %get-tuple-element.21), channel_id=1, source_target_pairs={{0,4},{2,6},{4,0},{6,2},{1,5},{3,7},{5,1},{7,3},{8,12},{10,14},{12... | collective-permute-start | bytes 225800 | tf_op jit(solution)/shard_map/ppermute | solution.py:28
  23.2 7.2 %collective-permute-start.3 = (bf16[147,256]{1,0:T(8,128)(2,1)S(1)}, bf16[147,256]{1,0:T(8,128)(2,1)S(1)}, u32[]{:S(2)}, u32[]{:S(2)}) collective-permute-start(bf16[147,256]{1,0:T(8,128)(2,1)S(1)} %get-tuple-element.22), channel_id=1, source_target_pairs={{0,6},{2,0},{4,2},{6,4},{1,7},{3,1},{5,3},{7,5},{8,14},{10,8},{12,... | collective-permute-start | bytes 225800 | tf_op jit(solution)/shard_map/ppermute | solution.py:28
  23.4 9.5 %collective-permute-start.5 = (bf16[147,256]{1,0:T(8,128)(2,1)S(1)}, bf16[147,256]{1,0:T(8,128)(2,1)S(1)}, u32[]{:S(2)}, u32[]{:S(2)}) collective-permute-start(bf16[147,256]{1,0:T(8,128)(2,1)S(1)} %get-tuple-element.24), channel_id=1, source_target_pairs={{0,2},{2,4},{4,6},{6,0},{1,3},{3,5},{5,7},{7,1},{8,10},{10,12},{12... | collective-permute-start | bytes 225800 | tf_op jit(solution)/shard_map/ppermute | solution.py:28
  25.5 9.5 %collective-permute-start.6 = (bf16[147,256]{1,0:T(8,128)(2,1)S(1)}, bf16[147,256]{1,0:T(8,128)(2,1)S(1)}, u32[]{:S(2)}, u32[]{:S(2)}) collective-permute-start(bf16[147,256]{1,0:T(8,128)(2,1)S(1)} %get-tuple-element.25), channel_id=1, source_target_pairs={{0,4},{2,6},{4,0},{6,2},{1,5},{3,7},{5,1},{7,3},{8,12},{10,14},{12... | collective-permute-start | bytes 225800 | tf_op jit(solution)/shard_map/ppermute | solution.py:28
  26.3 8.7 %collective-permute-start.7 = (bf16[147,256]{1,0:T(8,128)(2,1)S(1)}, bf16[147,256]{1,0:T(8,128)(2,1)S(1)}, u32[]{:S(2)}, u32[]{:S(2)}) collective-permute-start(bf16[147,256]{1,0:T(8,128)(2,1)S(1)} %get-tuple-element.26), channel_id=1, source_target_pairs={{0,6},{2,0},{4,2},{6,4},{1,7},{3,1},{5,3},{7,5},{8,14},{10,8},{12,... | collective-permute-start | bytes 225800 | tf_op jit(solution)/shard_map/ppermute | solution.py:28
  31.3 8.1 %collective-permute-start.4 = (bf16[294,256]{1,0:T(8,128)(2,1)S(1)}, bf16[294,256]{1,0:T(8,128)(2,1)S(1)}, u32[]{:S(2)}, u32[]{:S(2)}) collective-permute-start(bf16[294,256]{1,0:T(8,128)(2,1)S(1)} %shard_map.97), channel_id=1, source_target_pairs={{0,1},{1,0},{2,3},{3,2},{4,5},{5,4},{6,7},{7,6},{8,9},{9,8},{10,11... | collective-permute-start | bytes 451592 | tf_op jit(solution)/shard_map/ppermute | solution.py:28
  36.0 5.3 %collective-permute-start.8 = (bf16[294,256]{1,0:T(8,128)(2,1)S(1)}, bf16[294,256]{1,0:T(8,128)(2,1)S(1)}, u32[]{:S(2)}, u32[]{:S(2)}) collective-permute-start(bf16[294,256]{1,0:T(8,128)(2,1)S(1)} %shard_map.100), channel_id=1, source_target_pairs={{0,1},{1,0},{2,3},{3,2},{4,5},{5,4},{6,7},{7,6},{8,9},{9,8},{10,11... | collective-permute-start | bytes 451592 | tf_op jit(solution)/shard_map/ppermute | solution.py:28

commit v5 on v4

v5 whole, which is shorter than its diff:
```python
import functools

import jax
import jax.numpy as jnp
from jax import lax
from jax.experimental import pallas as pl
from jax.experimental.pallas import tpu as pltpu
from jax.sharding import PartitionSpec as P

HEADS = 16
HEAD_DIM = 32
GRID_H = 28
GRID_W = 21
WIN = 7

GROUP = 8
VMEM_LIMIT = 24 * 1024 * 1024

SMEM = pl.BlockSpec(memory_space=pltpu.SMEM)
VMEM = pl.BlockSpec(memory_space=pltpu.VMEM)
HBM = pl.BlockSpec(memory_space=pltpu.HBM)


def rotated(block, axis, distance):
    devices = lax.axis_size(axis)
    return lax.ppermute(block, axis, [(i, (i + distance) % devices) for i in range(devices)])


def paired(n):
    return n & (n - 1) == 0


def target(place, d, n):
    return place ^ d if paired(n) else lax.rem(place + d, n)


def origin(place, d, n):
    return place ^ d if paired(n) else lax.rem(place - d + n, n)


def exchanged(block, axis, d):
    n = lax.axis_size(axis)
    pairs = [(i, i ^ d if paired(n) else (i + d) % n) for i in range(n)]
    return lax.ppermute(block, axis, pairs)


def band_of(seq, n_seq):
    return lax.rem(seq + n_seq - 1, n_seq)


def dot(a, b):
    return jnp.dot(a, b, preferred_element_type=jnp.float32)


def one_hot(cond):
    return jnp.where(cond, 1.0, 0.0).astype(jnp.bfloat16)


def stage_kernel(n_seq, place, shifts_hbm, pages_hbm, gain_hbm, *refs):
    weights, refs = refs[:4], refs[4:]
    rolled_ref, take_ref, same_ref, gain_ref, *staged = refs[:8]
    shifts, own, arrived = refs[8:]
    pairs = [(shifts_hbm, shifts), (pages_hbm.at[0], own), (gain_hbm, gain_ref)]
    pairs += list(zip(weights, staged))
    copies = [pltpu.make_async_copy(*pair, arrived.at[i]) for i, pair in enumerate(pairs)]
    for copy in copies:
        copy.start()
    band_rows = own.shape[0]
    rows, halo_rows = take_ref.shape
    copies[0].wait()
    row_shift, col_shift = shifts[0, 0], shifts[0, 1]

    cell = lax.broadcasted_iota(jnp.int32, (rows, 1), 0)
    cell_row = cell // GRID_W
    from_col = cell - cell_row * GRID_W + col_shift
    from_col = jnp.where(from_col >= GRID_W, from_col - GRID_W, from_col)
    skipped = band_rows - halo_rows
    source = jnp.where(cell < band_rows, (cell_row + row_shift) * GRID_W + from_col - skipped, -1)
    take_ref[...] = one_hot(source == lax.broadcasted_iota(jnp.int32, (rows, halo_rows), 1))
    take_own = one_hot(
        source - halo_rows == lax.broadcasted_iota(jnp.int32, (rows, band_rows), 1)
    )

    band = band_of(place[0], n_seq)

    def marks(index):
        row = index // GRID_W
        col = index - row * GRID_W
        wrap_row = (band * WIN + row >= GRID_H - row_shift).astype(jnp.int32)
        wrap_col = (col >= GRID_W - col_shift).astype(jnp.int32)
        return jnp.where(index < band_rows, (col // WIN) * 4 + 2 * wrap_row + wrap_col, -1)

    same = marks(cell) == marks(lax.broadcasted_iota(jnp.int32, (1, rows), 1))
    same_ref[...] = same.astype(jnp.int32)
    copies[1].wait()
    rolled_ref[...] = dot(take_own, own[...]).astype(jnp.bfloat16)
    for copy in copies[2:]:
        copy.wait()


def encode_kernel(
    n_seq, place, rolled_ref, halo_ref, take_ref, same_ref, gain_ref, qkv_ref, out_ref, key_ref,
    value_ref, *sent
):
    rows = rolled_ref.shape[0]
    attn = HEADS * HEAD_DIM
    seq = place[0]
    rolled = rolled_ref[...].astype(jnp.float32) + dot(take_ref[...], halo_ref[...])

    mean = jnp.mean(rolled, axis=-1, keepdims=True)
    centred = rolled - mean
    variance = jnp.mean(centred * centred, axis=-1, keepdims=True)
    normed = (centred * lax.rsqrt(variance + 1e-05) * gain_ref[...]).astype(jnp.bfloat16)
    qkv = dot(normed, qkv_ref[...]).astype(jnp.bfloat16)
    queries, keys, values = (qkv[:, i * attn : (i + 1) * attn] for i in range(3))

    same = jnp.concatenate([same_ref[...]] * GROUP, axis=0) != 0
    width = GROUP * HEAD_DIM
    lane_head = lax.broadcasted_iota(jnp.int32, (1, width), 1) // HEAD_DIM
    parts = []
    for g in range(HEADS // GROUP):
        at = g * width
        q, k, v = (part[:, at : at + width] for part in (queries, keys, values))
        stacked = jnp.concatenate(
            [jnp.where(lane_head == h, q, jnp.zeros_like(q)) for h in range(GROUP)], axis=0
        )
        scores = lax.dot_general(
            stacked, k, (((1,), (1,)), ((), ())), preferred_element_type=jnp.float32
        )
        scores = jnp.where(same, scores * HEAD_DIM ** (-0.5), -1000000000.0)
        scores = jnp.exp(scores - jnp.max(scores, axis=-1, keepdims=True))
        total = jnp.sum(scores, axis=-1, keepdims=True)
        weights = (scores * (1.0 / total)).astype(jnp.bfloat16)
        mixed = dot(weights, v)
        part = jnp.zeros((rows, width), jnp.float32)
        for h in range(GROUP):
            part = jnp.where(lane_head == h, mixed[h * rows : (h + 1) * rows], part)
        parts.append(part.astype(jnp.bfloat16))
    attended = jnp.concatenate(parts, axis=1)
    memory = (rolled + dot(attended, out_ref[...])).astype(jnp.bfloat16)

    own_cols = key_ref.shape[1] // n_seq
    for weight_ref, blocks in ((key_ref, sent[:n_seq]), (value_ref, sent[n_seq:])):
        for d in range(n_seq):
            cols = pl.ds(pl.multiple_of(target(seq, d, n_seq) * own_cols, own_cols), own_cols)
            block = dot(memory, weight_ref[:, cols])
            blocks[d][...] = block[: blocks[d].shape[0]].astype(jnp.bfloat16)


def select_kernel(rounds, first, count, place, order_ref, *refs):
    n_seq = len(rounds)
    held, outs = refs[:n_seq], refs[n_seq:]
    band_rows = held[0].shape[0]
    seq, tensor = place[0], place[1]
    n_tensor = order_ref.shape[0]
    pos = order_ref.shape[1]
    for i in range(count):
        order = order_ref[lax.rem(tensor + first + i, n_tensor)]
        total = None
        for d, block in zip(rounds, held):
            band = band_of(origin(seq, d, n_seq), n_seq)
            pick = one_hot(
                order - band * band_rows == lax.broadcasted_iota(jnp.int32, (pos, band_rows), 1)
            )
            term = dot(pick, block[...])
            total = term if total is None else total + term
        outs[i][...] = total.astype(jnp.bfloat16)


def call(kernel, out_shape, n_scalar, n_vmem, flops, moved, n_hbm=0, scratch=()):
    return pl.pallas_call(
        kernel,
        out_shape=out_shape,
        in_specs=[SMEM] * n_scalar + [VMEM] * n_vmem + [HBM] * n_hbm,
        out_specs=jax.tree.map(lambda _: VMEM, out_shape),
        scratch_shapes=list(scratch),
        compiler_params=pltpu.CompilerParams(vmem_limit_bytes=VMEM_LIMIT),
        cost_estimate=pl.CostEstimate(flops=flops, bytes_accessed=moved, transcendentals=0),
    )


def local(
    memory_in, norm_gain, qkv_weight, out_weight, key_weight, value_weight, shift_offsets, row_order
):
    _, band_rows, emb = memory_in.shape
    n_seq = lax.axis_size("seq")
    n_tensor = lax.axis_size("tensor")
    own_cols = key_weight.shape[1] // n_seq
    pos = row_order.shape[1] // n_tensor
    rows = -(-band_rows // 16) * 16
    place = jnp.stack([lax.axis_index("seq"), lax.axis_index("tensor")]).astype(jnp.int32)
    halo = rotated(memory_in[0, GRID_W :], "seq", 1)
    order = lax.dynamic_index_in_dim(row_order, lax.axis_index("tensor"), 0, False)
    order = order.reshape(n_tensor, pos, 1)

    weights = [qkv_weight, out_weight, key_weight, value_weight]
    off_chip = [shift_offsets, memory_in, norm_gain.reshape(1, emb), *weights]
    staged = call(
        functools.partial(stage_kernel, n_seq),
        [
            jax.ShapeDtypeStruct((rows, emb), jnp.bfloat16),
            jax.ShapeDtypeStruct((rows, halo.shape[0]), jnp.bfloat16),
            jax.ShapeDtypeStruct((rows, rows), jnp.int32),
            jax.ShapeDtypeStruct((1, emb), jnp.float32),
        ]
        + [jax.ShapeDtypeStruct(w.shape, w.dtype) for w in weights],
        1, 0, 50_000_000, 8_000_000, len(off_chip),
        [
            pltpu.SMEM(shift_offsets.shape, jnp.int32),
            pltpu.VMEM((band_rows, emb), jnp.bfloat16),
            pltpu.SemaphoreType.DMA((len(off_chip),)),
        ],
    )(place, *(pltpu.with_memory_space_constraint(x, pltpu.HBM) for x in off_chip))
    block = jax.ShapeDtypeStruct((band_rows, own_cols), jnp.bfloat16)
    sent = call(
        functools.partial(encode_kernel, n_seq), [block] * (2 * n_seq),
        1, 9, 2_000_000_000, 10_000_000,
    )(place, staged[0], halo, *staged[1:])

    rounds = [*range(2, n_seq), 1]
    key_held = [sent[0]] + [exchanged(sent[d], "seq", d) for d in rounds]
    value_held = [sent[n_seq]] + [exchanged(sent[n_seq + d], "seq", d) for d in rounds]

    piece = jax.ShapeDtypeStruct((pos, own_cols), jnp.bfloat16)

    def gathered(held):
        away = call(
            functools.partial(select_kernel, [0, *rounds], 1, n_tensor - 1),
            [piece] * (n_tensor - 1), 1, 1 + n_seq, 300_000_000, 1_000_000,
        )(place, order, *held)
        arrived = [rotated(away[d - 1], "tensor", d) for d in range(1, n_tensor)]
        kept = call(
            functools.partial(select_kernel, [0, *rounds], 0, 1),
            [piece], 1, 1 + n_seq, 300_000_000, 1_000_000,
        )(place, order, *held)
        return [*kept, *arrived]

    def by_page(blocks):
        page = jnp.arange(n_tensor)[:, None, None]
        result = blocks[0][None]
        for d in range(1, n_tensor):
            came = page == (lax.axis_index("tensor") - d) % n_tensor
            result = jnp.where(came, blocks[d][None], result)
        return jnp.broadcast_to(result, (n_tensor, pos, own_cols))

    key_out, value_blocks = lax.optimization_barrier(
        (by_page(gathered(key_held)), gathered(value_held))
    )
    return key_out, by_page(value_blocks)


def solution(mesh):
    placed = (
        P(("dp", "tensor"), "seq", None),
        P(),
        P(),
        P(),
        P(),
        P(),
        P(("dp", "tensor"), None),
        P("dp", None),
    )
    return jax.shard_map(
        local,
        mesh=mesh,
        in_specs=placed,
        out_specs=(P("dp", "tensor", "seq"), P("dp", "tensor", "seq")),
        check_vma=False,
    )
```

time: 42.6 us -> 39.8 us (0.934)
  waiting for transfers between devices: 4.49 us -> 10.6 us
  starting transfers between devices: 17.5 us -> 12.7 us
  local copies, waits for them, and re-layouts: 5.14 us -> 1.25 us
    ppermute x9 -> x3, starting transfers between devices: 17.5 us -> 6.15 us  [rotated(): lax.ppermute(block, axis, [(i, (i + distance) % devices) for i in range(d...]
    ppermute x0 -> x6, starting transfers between devices: none -> 6.59 us  [exchanged(): return lax.ppermute(block, axis, pairs)]
    ppermute x0 -> x6, waiting for transfers between devices: none -> 5.83 us  [exchanged(): return lax.ppermute(block, axis, pairs)]
    unnamed x12 -> x2, local copies, waits for them, and re-layouts: 3.95 us -> 0.01 us
    ppermute x9 -> x3, waiting for transfers between devices: 4.49 us -> 4.8 us  [rotated(): lax.ppermute(block, axis, [(i, (i + distance) % devices) for i in range(d...]
  transfers between devices with their start and end apart: 9 -> 9, of which waited for: 4 -> 5; matrix products, arithmetic and copies ran while one was open for 3% -> 4% of each run, Pallas kernels for 15% -> 20%
where the time goes in v5:
time: 39.8 us; the launch traced here: 39.7 us
  starting transfers between devices  12.7 us (32%)
  Pallas kernels  12 us (30%)
  waiting for transfers between devices  10.6 us (27%)
  other arithmetic  2.37 us (6%)
  local copies, waits for them, and re-layouts  1.25 us (3%)
  between operations  0.73 us (2%)
    ppermute x6, starting transfers between devices, exchanged(): return lax.ppermute(block, axis, pairs)  6.59 us
    ppermute x3, starting transfers between devices, rotated(): lax.ppermute(block, axis, [(i, (i + distance) % devices) for i in range(d...  6.15 us
    ppermute x6, waiting for transfers between devices, exchanged(): return lax.ppermute(block, axis, pairs)  5.83 us
    ppermute x3, waiting for transfers between devices, rotated(): lax.ppermute(block, axis, [(i, (i + distance) % devices) for i in range(d...  4.8 us
    pallas_call x1, Pallas kernels, local(): call(functools.partial(stage_kernel, n_seq), [jax.ShapeDtypeStruct((rows,...  4.19 us
    pallas_call x1, Pallas kernels, local(): call(functools.partial(encode_kernel, n_seq), [block] * (2 * n_seq), 1, 9...  4.04 us
    select_n x2, other arithmetic, by_page(): result = jnp.where(came, blocks[d][None], result)  2.29 us
    pallas_call x2, Pallas kernels, gathered(): call(functools.partial(select_kernel, [0, *rounds], 1, n_tensor - 1), [pi...  1.87 us
  transfers between devices with their start and end apart: 9, of which 5 were waited for; matrix products, arithmetic and copies ran while one was open for 4% of the time, Pallas kernels for 20%

profile of v5, /device:TPU:0, one launch (start us, length us, event | category | flops | bytes accessed | tf_op | source)
XLA Modules:
  0.0 39.7 jit_solution(4819046885766725754)
XLA Ops:
  0.6 0.0 copy-start
  0.6 1.0 %slice_bitcast_fusion = bf16[126,1024]{1,0:T(8,128)(2,1)S(1)} fusion(bf16[1,147,1024]{2,1,0:T(8,128)(2,1)} %pages_hbm.1), kind=kLoop, calls=%fused_computation.2 | loop fusion | bytes 516096 | tf_op jit(solution)/shard_map/squeeze | solution.py:192
  1.7 3.1 %collective-permute-start = (bf16[126,1024]{1,0:T(8,128)(2,1)S(1)}, bf16[126,1024]{1,0:T(8,128)(2,1)S(1)}, u32[]{:S(2)}, u32[]{:S(2)}) collective-permute-start(bf16[126,1024]{1,0:T(8,128)(2,1)S(1)} %slice_bitcast_fusion), channel_id=1, source_target_pairs={{0,2},{2,4},{4,6},{6,0},{1,3},{3,5},{5,7},{7,1},{8,10},{10,12},{12... | collective-permute-start | bytes 774152 | tf_op jit(solution)/shard_map/ppermute | solution.py:26
  4.8 0.1 pad_add_fusion.place
  4.8 4.2 %shard_map.95 = (bf16[160,1024]{1,0:T(8,128)(2,1)S(1)}, bf16[160,126]{1,0:T(8,128)(2,1)S(1)}, s32[160,160]{1,0:T(8,128)S(1)}, f32[1,1024]{1,0:T(1,128)S(1)}, bf1...) custom-call(s32[2]{0:T(128)S(1)} %pad_add_fusion.place, ...), custom_call_target="tpu_custom_call" | custom-call | flops 50000000 | bytes 8000000 | tf_op jit(solution)/shard_map/pallas_call | solution.py:198
  9.0 4.1 %collective-permute-done.halo_ref = bf16[126,1024]{1,0:T(8,128)(2,1)S(1)} collective-permute-done((bf16[126,1024]{1,0:T(8,128)(2,1)S(1)}, bf16[126,1024]{1,0:T(8,128)(2,1)S(1)}, u32[]{:S(2)}, u32[]{:S(2)}) %collective-permute-start) | collective-permute-done | bytes 258080 | tf_op jit(solution)/shard_map/ppermute | solution.py:26
  13.1 4.0 %shard_map.96 = (bf16[147,256]{1,0:T(8,128)(2,1)S(1)}, bf16[147,256]{1,0:T(8,128)(2,1)S(1)}, bf16[147,256]{1,0:T(8,128)(2,1)S(1)}, bf16[147,256]{1,0:T(8,128)(2,...) custom-call(s32[2]{0:T(128)S(1)} %pad_add_fusion.place, ...), custom_call_target="tpu_custom_call" | custom-call | flops 2000000000 | bytes 10000000 | tf_op jit(solution)/shard_map/pallas_call | solution.py:215
  17.1 0.8 %collective-permute-start.1 = (bf16[147,256]{1,0:T(8,128)(2,1)S(1)}, bf16[147,256]{1,0:T(8,128)(2,1)S(1)}, u32[]{:S(2)}, u32[]{:S(2)}) collective-permute-start(bf16[147,256]{1,0:T(8,128)(2,1)S(1)} %get-tuple-element.30), channel_id=1, source_target_pairs={{0,4},{2,6},{4,0},{6,2},{1,5},{3,7},{5,1},{7,3},{8,12},{10,14},{12... | collective-permute-start | bytes 225800 | tf_op jit(solution)/shard_map/ppermute | solution.py:44
  17.9 1.3 %collective-permute-start.2 = (bf16[147,256]{1,0:T(8,128)(2,1)S(1)}, bf16[147,256]{1,0:T(8,128)(2,1)S(1)}, u32[]{:S(2)}, u32[]{:S(2)}) collective-permute-start(bf16[147,256]{1,0:T(8,128)(2,1)S(1)} %get-tuple-element.31), channel_id=1, source_target_pairs={{0,6},{2,4},{4,2},{6,0},{1,7},{3,5},{5,3},{7,1},{8,14},{10,12},{12... | collective-permute-start | bytes 225800 | tf_op jit(solution)/shard_map/ppermute | solution.py:44
  19.3 1.4 %collective-permute-start.3 = (bf16[147,256]{1,0:T(8,128)(2,1)S(1)}, bf16[147,256]{1,0:T(8,128)(2,1)S(1)}, u32[]{:S(2)}, u32[]{:S(2)}) collective-permute-start(bf16[147,256]{1,0:T(8,128)(2,1)S(1)} %get-tuple-element.32), channel_id=1, source_target_pairs={{0,2},{2,0},{4,6},{6,4},{1,3},{3,1},{5,7},{7,5},{8,10},{10,8},{12,... | collective-permute-start | bytes 225800 | tf_op jit(solution)/shard_map/ppermute | solution.py:44
  20.7 0.0 copy-done
  20.7 0.2 reshape.22.order_ref
  20.9 1.7 %collective-permute-start.5 = (bf16[147,256]{1,0:T(8,128)(2,1)S(1)}, bf16[147,256]{1,0:T(8,128)(2,1)S(1)}, u32[]{:S(2)}, u32[]{:S(2)}) collective-permute-start(bf16[147,256]{1,0:T(8,128)(2,1)S(1)} %get-tuple-element.34), channel_id=1, source_target_pairs={{0,4},{2,6},{4,0},{6,2},{1,5},{3,7},{5,1},{7,3},{8,12},{10,14},{12... | collective-permute-start | bytes 225800 | tf_op jit(solution)/shard_map/ppermute | solution.py:44
  22.6 1.3 %collective-permute-start.6 = (bf16[147,256]{1,0:T(8,128)(2,1)S(1)}, bf16[147,256]{1,0:T(8,128)(2,1)S(1)}, u32[]{:S(2)}, u32[]{:S(2)}) collective-permute-start(bf16[147,256]{1,0:T(8,128)(2,1)S(1)} %get-tuple-element.35), channel_id=1, source_target_pairs={{0,6},{2,4},{4,2},{6,0},{1,7},{3,5},{5,3},{7,1},{8,14},{10,12},{12... | collective-permute-start | bytes 225800 | tf_op jit(solution)/shard_map/ppermute | solution.py:44
  24.0 3.7 %collective-permute-done.1.refs_1_ = bf16[147,256]{1,0:T(8,128)(2,1)S(1)} collective-permute-done((bf16[147,256]{1,0:T(8,128)(2,1)S(1)}, bf16[147,256]{1,0:T(8,128)(2,1)S(1)}, u32[]{:S(2)}, u32[]{:S(2)}) %collective-permute-start.1) | collective-permute-done | bytes 75296 | tf_op jit(solution)/shard_map/ppermute | solution.py:44
  27.6 0.0 collective-permute-start.7
  27.6 0.0 collective-permute-done.2.refs_2_
  27.6 0.0 collective-permute-done.3.refs_3_
  27.6 0.9 %shard_map.97 = bf16[294,256]{1,0:T(8,128)(2,1)S(1)} custom-call(s32[2]{0:T(128)S(1)} %pad_add_fusion.place, s32[2,294,1]{2,1,0:T(8,128)S(1)} %reshape.22.order_ref, bf16[147,256]{1,0:T(8,128)(2,1)S(1)} %get-tuple-element.29.refs_0_, bf16[147,256]{1,0:T(8,128)(2,1)S(1)} %collective-permute-done.1.refs_1_, ...), custom_call_target="tpu_custom_call" | custom-call | flops 300000000 | bytes 1000000 | tf_op jit(solution)/shard_map/pallas_call | solution.py:227
  28.6 1.6 %collective-permute-start.4 = (bf16[294,256]{1,0:T(8,128)(2,1)S(1)}, bf16[294,256]{1,0:T(8,128)(2,1)S(1)}, u32[]{:S(2)}, u32[]{:S(2)}) collective-permute-start(bf16[294,256]{1,0:T(8,128)(2,1)S(1)} %shard_map.97), channel_id=1, source_target_pairs={{0,1},{1,0},{2,3},{3,2},{4,5},{5,4},{6,7},{7,6},{8,9},{9,8},{10,11... | collective-permute-start | bytes 451592 | tf_op jit(solution)/shard_map/ppermute | solution.py:26
  30.2 1.6 %collective-permute-done.5.refs_1_ = bf16[147,256]{1,0:T(8,128)(2,1)S(1)} collective-permute-done((bf16[147,256]{1,0:T(8,128)(2,1)S(1)}, bf16[147,256]{1,0:T(8,128)(2,1)S(1)}, u32[]{:S(2)}, u32[]{:S(2)}) %collective-permute-start.5) | collective-permute-done | bytes 75296 | tf_op jit(solution)/shard_map/ppermute | solution.py:44
  31.7 0.0 collective-permute-done.6.refs_2_
  31.8 0.6 %collective-permute-done.7.refs_3_ = bf16[147,256]{1,0:T(8,128)(2,1)S(1)} collective-permute-done((bf16[147,256]{1,0:T(8,128)(2,1)S(1)}, bf16[147,256]{1,0:T(8,128)(2,1)S(1)}, u32[]{:S(2)}, u32[]{:S(2)}) %collective-permute-start.7) | collective-permute-done | bytes 75296 | tf_op jit(solution)/shard_map/ppermute | solution.py:44
  32.3 0.9 %shard_map.100 = bf16[294,256]{1,0:T(8,128)(2,1)S(1)} custom-call(s32[2]{0:T(128)S(1)} %pad_add_fusion.place, s32[2,294,1]{2,1,0:T(8,128)S(1)} %reshape.22.order_ref, bf16[147,256]{1,0:T(8,128)(2,1)S(1)} %get-tuple-element.33.refs_0_, bf16[147,256]{1,0:T(8,128)(2,1)S(1)} %collective-permute-done.5.refs_1_, ...), custom_call_target="tpu_custom_call" | custom-call | flops 300000000 | bytes 1000000 | tf_op jit(solution)/shard_map/pallas_call | solution.py:227
  33.3 1.5 %collective-permute-start.8 = (bf16[294,256]{1,0:T(8,128)(2,1)S(1)}, bf16[294,256]{1,0:T(8,128)(2,1)S(1)}, u32[]{:S(2)}, u32[]{:S(2)}) collective-permute-start(bf16[294,256]{1,0:T(8,128)(2,1)S(1)} %shard_map.100), channel_id=1, source_target_pairs={{0,1},{1,0},{2,3},{3,2},{4,5},{5,4},{6,7},{7,6},{8,9},{9,8},{10,11... | collective-permute-start | bytes 451592 | tf_op jit(solution)/shard_map/ppermute | solution.py:26
  34.8 0.9 %shard_map.99 = bf16[294,256]{1,0:T(8,128)(2,1)S(1)} custom-call(s32[2]{0:T(128)S(1)} %pad_add_fusion.place, s32[2,294,1]{2,1,0:T(8,128)S(1)} %reshape.22.order_ref, bf16[147,256]{1,0:T(8,128)(2,1)S(1)} %get-tuple-element.33.refs_0_, bf16[147,256]{1,0:T(8,128)(2,1)S(1)} %collective-permute-done.5.refs_1_, ...), custom_call_target="tpu_custom_call" | custom-call | flops 300000000 | bytes 1000000 | tf_op jit(solution)/shard_map/pallas_call | solution.py:232
  35.7 0.9 %shard_map.98 = bf16[294,256]{1,0:T(8,128)(2,1)S(1)} custom-call(s32[2]{0:T(128)S(1)} %pad_add_fusion.place, s32[2,294,1]{2,1,0:T(8,128)S(1)} %reshape.22.order_ref, bf16[147,256]{1,0:T(8,128)(2,1)S(1)} %get-tuple-element.29.refs_0_, bf16[147,256]{1,0:T(8,128)(2,1)S(1)} %collective-permute-done.1.refs_1_, ...), custom_call_target="tpu_custom_call" | custom-call | flops 300000000 | bytes 1000000 | tf_op jit(solution)/shard_map/pallas_call | solution.py:232
  36.6 0.0 collective-permute-done.4
  36.7 1.1 %broadcast_select_fusion.1 = bf16[2,294,256]{2,0,1:T(2,128)(2,1)} fusion(pred[2]{0:T(512)(128)(4,1)S(1)} %iota_compare_fusion, bf16[294,256]{1,0:T(8,128)(2,1)S(1)} %shard_map.98, bf16[294,256]{1,0:T(8,128)(2,1)S(1)} %collective-permute-done.4), kind=kLoop, calls=%fused_computation.1 | loop fusion | flops 150528 | bytes 602114 | tf_op jit(solution)/shard_map/jit(_where)/select_n | solution.py:243
  37.8 0.7 %collective-permute-done.8 = bf16[294,256]{1,0:T(8,128)(2,1)S(1)} collective-permute-done((bf16[294,256]{1,0:T(8,128)(2,1)S(1)}, bf16[294,256]{1,0:T(8,128)(2,1)S(1)}, u32[]{:S(2)}, u32[]{:S(2)}) %collective-permute-start.8) | collective-permute-done | bytes 150560 | tf_op jit(solution)/shard_map/ppermute | solution.py:26
  38.5 1.1 %broadcast_select_fusion = bf16[2,294,256]{2,0,1:T(2,128)(2,1)} fusion(pred[2]{0:T(512)(128)(4,1)S(1)} %iota_compare_fusion, bf16[294,256]{1,0:T(8,128)(2,1)S(1)} %shard_map.99, bf16[294,256]{1,0:T(8,128)(2,1)S(1)} %collective-permute-done.8), kind=kLoop, calls=%fused_computation | loop fusion | flops 150528 | bytes 602114 | tf_op jit(solution)/shard_map/jit(_where)/select_n | solution.py:243
  (2 shorter events, 0.0 us)
Async XLA Ops:
  0.6 20.1 %copy-start = (s32[2,588]{1,0:T(2,128)S(1)}, s32[2,588]{1,0:T(2,128)}, u32[]{:S(2)}) copy-start(s32[2,588]{1,0:T(2,128)} %param.15) | copy-start | bytes 14116
  1.7 11.4 %collective-permute-start = (bf16[126,1024]{1,0:T(8,128)(2,1)S(1)}, bf16[126,1024]{1,0:T(8,128)(2,1)S(1)}, u32[]{:S(2)}, u32[]{:S(2)}) collective-permute-start(bf16[126,1024]{1,0:T(8,128)(2,1)S(1)} %slice_bitcast_fusion), channel_id=1, source_target_pairs={{0,2},{2,4},{4,6},{6,0},{1,3},{3,5},{5,7},{7,1},{8,10},{10,12},{12... | collective-permute-start | bytes 774152 | tf_op jit(solution)/shard_map/ppermute | solution.py:26
  17.1 10.5 %collective-permute-start.1 = (bf16[147,256]{1,0:T(8,128)(2,1)S(1)}, bf16[147,256]{1,0:T(8,128)(2,1)S(1)}, u32[]{:S(2)}, u32[]{:S(2)}) collective-permute-start(bf16[147,256]{1,0:T(8,128)(2,1)S(1)} %get-tuple-element.30), channel_id=1, source_target_pairs={{0,4},{2,6},{4,0},{6,2},{1,5},{3,7},{5,1},{7,3},{8,12},{10,14},{12... | collective-permute-start | bytes 225800 | tf_op jit(solution)/shard_map/ppermute | solution.py:44
  17.9 9.7 %collective-permute-start.2 = (bf16[147,256]{1,0:T(8,128)(2,1)S(1)}, bf16[147,256]{1,0:T(8,128)(2,1)S(1)}, u32[]{:S(2)}, u32[]{:S(2)}) collective-permute-start(bf16[147,256]{1,0:T(8,128)(2,1)S(1)} %get-tuple-element.31), channel_id=1, source_target_pairs={{0,6},{2,4},{4,2},{6,0},{1,7},{3,5},{5,3},{7,1},{8,14},{10,12},{12... | collective-permute-start | bytes 225800 | tf_op jit(solution)/shard_map/ppermute | solution.py:44
  19.3 8.4 %collective-permute-start.3 = (bf16[147,256]{1,0:T(8,128)(2,1)S(1)}, bf16[147,256]{1,0:T(8,128)(2,1)S(1)}, u32[]{:S(2)}, u32[]{:S(2)}) collective-permute-start(bf16[147,256]{1,0:T(8,128)(2,1)S(1)} %get-tuple-element.32), channel_id=1, source_target_pairs={{0,2},{2,0},{4,6},{6,4},{1,3},{3,1},{5,7},{7,5},{8,10},{10,8},{12,... | collective-permute-start | bytes 225800 | tf_op jit(solution)/shard_map/ppermute | solution.py:44
  20.9 10.8 %collective-permute-start.5 = (bf16[147,256]{1,0:T(8,128)(2,1)S(1)}, bf16[147,256]{1,0:T(8,128)(2,1)S(1)}, u32[]{:S(2)}, u32[]{:S(2)}) collective-permute-start(bf16[147,256]{1,0:T(8,128)(2,1)S(1)} %get-tuple-element.34), channel_id=1, source_target_pairs={{0,4},{2,6},{4,0},{6,2},{1,5},{3,7},{5,1},{7,3},{8,12},{10,14},{12... | collective-permute-start | bytes 225800 | tf_op jit(solution)/shard_map/ppermute | solution.py:44
  22.6 9.1 %collective-permute-start.6 = (bf16[147,256]{1,0:T(8,128)(2,1)S(1)}, bf16[147,256]{1,0:T(8,128)(2,1)S(1)}, u32[]{:S(2)}, u32[]{:S(2)}) collective-permute-start(bf16[147,256]{1,0:T(8,128)(2,1)S(1)} %get-tuple-element.35), channel_id=1, source_target_pairs={{0,6},{2,4},{4,2},{6,0},{1,7},{3,5},{5,3},{7,1},{8,14},{10,12},{12... | collective-permute-start | bytes 225800 | tf_op jit(solution)/shard_map/ppermute | solution.py:44
  27.6 4.7 %collective-permute-start.7 = (bf16[147,256]{1,0:T(8,128)(2,1)S(1)}, bf16[147,256]{1,0:T(8,128)(2,1)S(1)}, u32[]{:S(2)}, u32[]{:S(2)}) collective-permute-start(bf16[147,256]{1,0:T(8,128)(2,1)S(1)} %get-tuple-element.36), channel_id=1, source_target_pairs={{0,2},{2,0},{4,6},{6,4},{1,3},{3,1},{5,7},{7,5},{8,10},{10,8},{12,... | collective-permute-start | bytes 225800 | tf_op jit(solution)/shard_map/ppermute | solution.py:44
  28.6 8.1 %collective-permute-start.4 = (bf16[294,256]{1,0:T(8,128)(2,1)S(1)}, bf16[294,256]{1,0:T(8,128)(2,1)S(1)}, u32[]{:S(2)}, u32[]{:S(2)}) collective-permute-start(bf16[294,256]{1,0:T(8,128)(2,1)S(1)} %shard_map.97), channel_id=1, source_target_pairs={{0,1},{1,0},{2,3},{3,2},{4,5},{5,4},{6,7},{7,6},{8,9},{9,8},{10,11... | collective-permute-start | bytes 451592 | tf_op jit(solution)/shard_map/ppermute | solution.py:26
  33.3 5.3 %collective-permute-start.8 = (bf16[294,256]{1,0:T(8,128)(2,1)S(1)}, bf16[294,256]{1,0:T(8,128)(2,1)S(1)}, u32[]{:S(2)}, u32[]{:S(2)}) collective-permute-start(bf16[294,256]{1,0:T(8,128)(2,1)S(1)} %shard_map.100), channel_id=1, source_target_pairs={{0,1},{1,0},{2,3},{3,2},{4,5},{5,4},{6,7},{7,6},{8,9},{9,8},{10,11... | collective-permute-start | bytes 451592 | tf_op jit(solution)/shard_map/ppermute | solution.py:26

commit v6 on v5

--- a/solution.py
+++ b/solution.py
@@ -56,10 +56,10 @@
     return jnp.where(cond, 1.0, 0.0).astype(jnp.bfloat16)
 
 
-def stage_kernel(n_seq, place, shifts_hbm, pages_hbm, gain_hbm, *refs):
+def stage_kernel(rounds, place, order_ref, shifts_hbm, pages_hbm, gain_hbm, *refs):
     weights, refs = refs[:4], refs[4:]
-    rolled_ref, take_ref, same_ref, gain_ref, *staged = refs[:8]
-    shifts, own, arrived = refs[8:]
+    rolled_ref, take_ref, same_ref, picks_ref, gain_ref, *staged = refs[:9]
+    shifts, own, arrived = refs[9:]
     pairs = [(shifts_hbm, shifts), (pages_hbm.at[0], own), (gain_hbm, gain_ref)]
     pairs += list(zip(weights, staged))
     copies = [pltpu.make_async_copy(*pair, arrived.at[i]) for i, pair in enumerate(pairs)]
@@ -67,6 +67,15 @@
         copy.start()
     band_rows = own.shape[0]
     rows, halo_rows = take_ref.shape
+    n_seq = len(rounds)
+    n_tensor, pos, _ = order_ref.shape
+    for i in range(n_tensor):
+        order = order_ref[lax.rem(place[1] + i, n_tensor)]
+        for r, d in enumerate(rounds):
+            local = order - band_of(origin(place[0], d, n_seq), n_seq) * band_rows
+            picks_ref[i, r] = one_hot(
+                local == lax.broadcasted_iota(jnp.int32, (pos, band_rows), 1)
+            )
     copies[0].wait()
     row_shift, col_shift = shifts[0, 0], shifts[0, 1]
 
@@ -99,12 +108,11 @@
 
 
 def encode_kernel(
-    n_seq, place, rolled_ref, halo_ref, take_ref, same_ref, gain_ref, qkv_ref, out_ref, key_ref,
+    blocks, place, rolled_ref, halo_ref, take_ref, same_ref, gain_ref, qkv_ref, out_ref, key_ref,
     value_ref, *sent
 ):
     rows = rolled_ref.shape[0]
     attn = HEADS * HEAD_DIM
-    seq = place[0]
     rolled = rolled_ref[...].astype(jnp.float32) + dot(take_ref[...], halo_ref[...])
 
     mean = jnp.mean(rolled, axis=-1, keepdims=True)
@@ -138,33 +146,19 @@
         parts.append(part.astype(jnp.bfloat16))
     attended = jnp.concatenate(parts, axis=1)
     memory = (rolled + dot(attended, out_ref[...])).astype(jnp.bfloat16)
-
-    own_cols = key_ref.shape[1] // n_seq
-    for weight_ref, blocks in ((key_ref, sent[:n_seq]), (value_ref, sent[n_seq:])):
-        for d in range(n_seq):
-            cols = pl.ds(pl.multiple_of(target(seq, d, n_seq) * own_cols, own_cols), own_cols)
-            block = dot(memory, weight_ref[:, cols])
-            blocks[d][...] = block[: blocks[d].shape[0]].astype(jnp.bfloat16)
-
-
-def select_kernel(rounds, first, count, place, order_ref, *refs):
-    n_seq = len(rounds)
+    own_cols = sent[0].shape[1]
+    for (is_value, d), block_ref in zip(blocks, sent):
+        at = target(place[0], d, key_ref.shape[1] // own_cols) * own_cols
+        weight_ref = value_ref if is_value else key_ref
+        block = dot(memory, weight_ref[:, pl.ds(pl.multiple_of(at, own_cols), own_cols)])
+        block_ref[...] = block[: block_ref.shape[0]].astype(jnp.bfloat16)
+
+
+def select_kernel(n_seq, first, picks_ref, *refs):
     held, outs = refs[:n_seq], refs[n_seq:]
-    band_rows = held[0].shape[0]
-    seq, tensor = place[0], place[1]
-    n_tensor = order_ref.shape[0]
-    pos = order_ref.shape[1]
-    for i in range(count):
-        order = order_ref[lax.rem(tensor + first + i, n_tensor)]
-        total = None
-        for d, block in zip(rounds, held):
-            band = band_of(origin(seq, d, n_seq), n_seq)
-            pick = one_hot(
-                order - band * band_rows == lax.broadcasted_iota(jnp.int32, (pos, band_rows), 1)
-            )
-            term = dot(pick, block[...])
-            total = term if total is None else total + term
-        outs[i][...] = total.astype(jnp.bfloat16)
+    for i, out in enumerate(outs):
+        terms = [dot(picks_ref[first + i, r], held[r][...]) for r in range(n_seq)]
+        out[...] = sum(terms[1:], terms[0]).astype(jnp.bfloat16)
 
 
 def call(kernel, out_shape, n_scalar, n_vmem, flops, moved, n_hbm=0, scratch=()):
@@ -193,47 +187,46 @@
     order = lax.dynamic_index_in_dim(row_order, lax.axis_index("tensor"), 0, False)
     order = order.reshape(n_tensor, pos, 1)
 
+    rounds = [*range(2, n_seq), 1, 0]
     weights = [qkv_weight, out_weight, key_weight, value_weight]
     off_chip = [shift_offsets, memory_in, norm_gain.reshape(1, emb), *weights]
-    staged = call(
-        functools.partial(stage_kernel, n_seq),
+    rolled_own, take, same, picks, gain, qkv_chip, out_chip, key_chip, value_chip = call(
+        functools.partial(stage_kernel, rounds),
         [
             jax.ShapeDtypeStruct((rows, emb), jnp.bfloat16),
             jax.ShapeDtypeStruct((rows, halo.shape[0]), jnp.bfloat16),
             jax.ShapeDtypeStruct((rows, rows), jnp.int32),
+            jax.ShapeDtypeStruct((n_tensor, n_seq, pos, band_rows), jnp.bfloat16),
             jax.ShapeDtypeStruct((1, emb), jnp.float32),
         ]
         + [jax.ShapeDtypeStruct(w.shape, w.dtype) for w in weights],
-        1, 0, 50_000_000, 8_000_000, len(off_chip),
+        1, 1, 50_000_000, 8_000_000, len(off_chip),
         [
             pltpu.SMEM(shift_offsets.shape, jnp.int32),
             pltpu.VMEM((band_rows, emb), jnp.bfloat16),
             pltpu.SemaphoreType.DMA((len(off_chip),)),
         ],
-    )(place, *(pltpu.with_memory_space_constraint(x, pltpu.HBM) for x in off_chip))
+    )(place, order, *(pltpu.with_memory_space_constraint(x, pltpu.HBM) for x in off_chip))
+
     block = jax.ShapeDtypeStruct((band_rows, own_cols), jnp.bfloat16)
+    blocks = [(is_value, d) for is_value in (False, True) for d in rounds]
     sent = call(
-        functools.partial(encode_kernel, n_seq), [block] * (2 * n_seq),
+        functools.partial(encode_kernel, blocks), [block] * len(blocks),
         1, 9, 2_000_000_000, 10_000_000,
-    )(place, staged[0], halo, *staged[1:])
-
-    rounds = [*range(2, n_seq), 1]
-    key_held = [sent[0]] + [exchanged(sent[d], "seq", d) for d in rounds]
-    value_held = [sent[n_seq]] + [exchanged(sent[n_seq + d], "seq", d) for d in rounds]
-
-    piece = jax.ShapeDtypeStruct((pos, own_cols), jnp.bfloat16)
-
-    def gathered(held):
-        away = call(
-            functools.partial(select_kernel, [0, *rounds], 1, n_tensor - 1),
-            [piece] * (n_tensor - 1), 1, 1 + n_seq, 300_000_000, 1_000_000,
-        )(place, order, *held)
+    )(place, rolled_own, halo, take, same, gain, qkv_chip, out_chip, key_chip, value_chip)
+    held = [exchanged(b, "seq", d) if d else b for (_, d), b in zip(blocks, sent)]
+
+    def selected(group, first, count):
+        return call(
+            functools.partial(select_kernel, n_seq, first),
+            [jax.ShapeDtypeStruct((pos, own_cols), jnp.bfloat16)] * count,
+            0, 1 + n_seq, 300_000_000, 1_000_000,
+        )(picks, *held[group * n_seq : (group + 1) * n_seq])
+
+    def gathered(group):
+        away = selected(group, 1, n_tensor - 1)
         arrived = [rotated(away[d - 1], "tensor", d) for d in range(1, n_tensor)]
-        kept = call(
-            functools.partial(select_kernel, [0, *rounds], 0, 1),
-            [piece], 1, 1 + n_seq, 300_000_000, 1_000_000,
-        )(place, order, *held)
-        return [*kept, *arrived]
+        return [*selected(group, 0, 1), *arrived]
 
     def by_page(blocks):
         page = jnp.arange(n_tensor)[:, None, None]
@@ -243,9 +236,7 @@
             result = jnp.where(came, blocks[d][None], result)
         return jnp.broadcast_to(result, (n_tensor, pos, own_cols))
 
-    key_out, value_blocks = lax.optimization_barrier(
-        (by_page(gathered(key_held)), gathered(value_held))
-    )
+    key_out, value_blocks = lax.optimization_barrier((by_page(gathered(0)), gathered(1)))
     return key_out, by_page(value_blocks)
 
 

time: 39.8 us -> 39.2 us (0.985)
  Pallas kernels: 12 us -> 9.68 us
  waiting for transfers between devices: 10.6 us -> 12.4 us
    pallas_call x6, Pallas kernels: 12 us -> 9.68 us  [the longest x1 4.39 us: local(): call(functools.partial(stage_kernel, rounds), [jax.ShapeDtypeStruct((rows...]
    ppermute x6, waiting for transfers between devices: 5.83 us -> 6.76 us  [exchanged(): return lax.ppermute(block, axis, pairs)]
    ppermute x3, waiting for transfers between devices: 4.8 us -> 5.61 us  [rotated(): lax.ppermute(block, axis, [(i, (i + distance) % devices) for i in range(d...]
  transfers between devices with their start and end apart: 9 -> 9, of which waited for: 5 -> 5; matrix products, arithmetic and copies ran while one was open for 4% -> 4% of each run, Pallas kernels for 20% -> 14%
where the time goes in v6:
time: 39.2 us; the launch traced here: 39.1 us
  starting transfers between devices  12.7 us (32%)
  waiting for transfers between devices  12.4 us (32%)
  Pallas kernels  9.68 us (25%)
  other arithmetic  2.38 us (6%)
  local copies, waits for them, and re-layouts  1.25 us (3%)
  between operations  0.72 us (2%)
    ppermute x6, waiting for transfers between devices, exchanged(): return lax.ppermute(block, axis, pairs)  6.76 us
    ppermute x6, starting transfers between devices, exchanged(): return lax.ppermute(block, axis, pairs)  6.53 us
    ppermute x3, starting transfers between devices, rotated(): lax.ppermute(block, axis, [(i, (i + distance) % devices) for i in range(d...  6.13 us
    ppermute x3, waiting for transfers between devices, rotated(): lax.ppermute(block, axis, [(i, (i + distance) % devices) for i in range(d...  5.61 us
    pallas_call x1, Pallas kernels, local(): call(functools.partial(stage_kernel, rounds), [jax.ShapeDtypeStruct((rows...  4.39 us
    pallas_call x1, Pallas kernels, local(): call(functools.partial(encode_kernel, blocks), [block] * len(blocks), 1,...  4.04 us
    select_n x2, other arithmetic, by_page(): result = jnp.where(came, blocks[d][None], result)  2.29 us
    pallas_call x4, Pallas kernels, selected(): call(functools.partial(select_kernel, n_seq, first), [jax.ShapeDtypeStruc...  1.25 us
  transfers between devices with their start and end apart: 9, of which 5 were waited for; matrix products, arithmetic and copies ran while one was open for 4% of the time, Pallas kernels for 14%

profile of v6, /device:TPU:0, one launch (start us, length us, event | category | flops | bytes accessed | tf_op | source)
XLA Modules:
  0.0 39.1 jit_solution(10208167604321795669)
XLA Ops:
  0.6 0.0 copy-start
  0.6 1.0 %slice_bitcast_fusion = bf16[126,1024]{1,0:T(8,128)(2,1)S(1)} fusion(bf16[1,147,1024]{2,1,0:T(8,128)(2,1)} %pages_hbm.1), kind=kLoop, calls=%fused_computation.2 | loop fusion | bytes 516096 | tf_op jit(solution)/shard_map/squeeze | solution.py:186
  1.7 3.1 %collective-permute-start = (bf16[126,1024]{1,0:T(8,128)(2,1)S(1)}, bf16[126,1024]{1,0:T(8,128)(2,1)S(1)}, u32[]{:S(2)}, u32[]{:S(2)}) collective-permute-start(bf16[126,1024]{1,0:T(8,128)(2,1)S(1)} %slice_bitcast_fusion), channel_id=1, source_target_pairs={{0,2},{2,4},{4,6},{6,0},{1,3},{3,5},{5,7},{7,1},{8,10},{10,12},{12... | collective-permute-start | bytes 774152 | tf_op jit(solution)/shard_map/ppermute | solution.py:26
  4.8 0.0 copy-done
  4.8 0.2 reshape.22.order_ref
  5.0 0.1 pad_add_fusion.place
  5.1 4.4 %shard_map.95 = (bf16[160,1024]{1,0:T(8,128)(2,1)S(1)}, bf16[160,126]{1,0:T(8,128)(2,1)S(1)}, s32[160,160]{1,0:T(8,128)S(1)}, bf16[2,4,294,147]{3,2,1,0:T(8,128)...) custom-call(s32[2]{0:T(128)S(1)} %pad_add_fusion.place, ...), custom_call_target="tpu_custom_call" | custom-call | flops 50000000 | bytes 8000000 | tf_op jit(solution)/shard_map/pallas_call | solution.py:193
  9.5 3.6 %collective-permute-done.halo_ref = bf16[126,1024]{1,0:T(8,128)(2,1)S(1)} collective-permute-done((bf16[126,1024]{1,0:T(8,128)(2,1)S(1)}, bf16[126,1024]{1,0:T(8,128)(2,1)S(1)}, u32[]{:S(2)}, u32[]{:S(2)}) %collective-permute-start) | collective-permute-done | bytes 258080 | tf_op jit(solution)/shard_map/ppermute | solution.py:26
  13.1 4.0 %shard_map.96 = (bf16[147,256]{1,0:T(8,128)(2,1)S(1)}, bf16[147,256]{1,0:T(8,128)(2,1)S(1)}, bf16[147,256]{1,0:T(8,128)(2,1)S(1)}, bf16[147,256]{1,0:T(8,128)(2,...) custom-call(s32[2]{0:T(128)S(1)} %pad_add_fusion.place, ...), custom_call_target="tpu_custom_call" | custom-call | flops 2000000000 | bytes 10000000 | tf_op jit(solution)/shard_map/pallas_call | solution.py:213
  17.1 0.8 %collective-permute-start.1 = (bf16[147,256]{1,0:T(8,128)(2,1)S(1)}, bf16[147,256]{1,0:T(8,128)(2,1)S(1)}, u32[]{:S(2)}, u32[]{:S(2)}) collective-permute-start(bf16[147,256]{1,0:T(8,128)(2,1)S(1)} %get-tuple-element.31), channel_id=1, source_target_pairs={{0,4},{2,6},{4,0},{6,2},{1,5},{3,7},{5,1},{7,3},{8,12},{10,14},{12... | collective-permute-start | bytes 225800 | tf_op jit(solution)/shard_map/ppermute | solution.py:44
  17.9 1.4 %collective-permute-start.2 = (bf16[147,256]{1,0:T(8,128)(2,1)S(1)}, bf16[147,256]{1,0:T(8,128)(2,1)S(1)}, u32[]{:S(2)}, u32[]{:S(2)}) collective-permute-start(bf16[147,256]{1,0:T(8,128)(2,1)S(1)} %get-tuple-element.32), channel_id=1, source_target_pairs={{0,6},{2,4},{4,2},{6,0},{1,7},{3,5},{5,3},{7,1},{8,14},{10,12},{12... | collective-permute-start | bytes 225800 | tf_op jit(solution)/shard_map/ppermute | solution.py:44
  19.3 1.4 %collective-permute-start.3 = (bf16[147,256]{1,0:T(8,128)(2,1)S(1)}, bf16[147,256]{1,0:T(8,128)(2,1)S(1)}, u32[]{:S(2)}, u32[]{:S(2)}) collective-permute-start(bf16[147,256]{1,0:T(8,128)(2,1)S(1)} %get-tuple-element.33), channel_id=1, source_target_pairs={{0,2},{2,0},{4,6},{6,4},{1,3},{3,1},{5,7},{7,5},{8,10},{10,8},{12,... | collective-permute-start | bytes 225800 | tf_op jit(solution)/shard_map/ppermute | solution.py:44
  20.7 1.6 %collective-permute-start.5 = (bf16[147,256]{1,0:T(8,128)(2,1)S(1)}, bf16[147,256]{1,0:T(8,128)(2,1)S(1)}, u32[]{:S(2)}, u32[]{:S(2)}) collective-permute-start(bf16[147,256]{1,0:T(8,128)(2,1)S(1)} %get-tuple-element.35), channel_id=1, source_target_pairs={{0,4},{2,6},{4,0},{6,2},{1,5},{3,7},{5,1},{7,3},{8,12},{10,14},{12... | collective-permute-start | bytes 225800 | tf_op jit(solution)/shard_map/ppermute | solution.py:44
  22.3 1.4 %collective-permute-start.6 = (bf16[147,256]{1,0:T(8,128)(2,1)S(1)}, bf16[147,256]{1,0:T(8,128)(2,1)S(1)}, u32[]{:S(2)}, u32[]{:S(2)}) collective-permute-start(bf16[147,256]{1,0:T(8,128)(2,1)S(1)} %get-tuple-element.36), channel_id=1, source_target_pairs={{0,6},{2,4},{4,2},{6,0},{1,7},{3,5},{5,3},{7,1},{8,14},{10,12},{12... | collective-permute-start | bytes 225800 | tf_op jit(solution)/shard_map/ppermute | solution.py:44
  23.7 4.0 %collective-permute-done.1.refs_0_ = bf16[147,256]{1,0:T(8,128)(2,1)S(1)} collective-permute-done((bf16[147,256]{1,0:T(8,128)(2,1)S(1)}, bf16[147,256]{1,0:T(8,128)(2,1)S(1)}, u32[]{:S(2)}, u32[]{:S(2)}) %collective-permute-start.1) | collective-permute-done | bytes 75296 | tf_op jit(solution)/shard_map/ppermute | solution.py:44
  27.6 0.0 collective-permute-start.7
  27.7 0.0 collective-permute-done.2.refs_1_
  27.7 0.0 collective-permute-done.3.refs_2_
  27.7 0.3 shard_map.97
  28.0 1.6 %collective-permute-start.4 = (bf16[294,256]{1,0:T(8,128)(2,1)S(1)}, bf16[294,256]{1,0:T(8,128)(2,1)S(1)}, u32[]{:S(2)}, u32[]{:S(2)}) collective-permute-start(bf16[294,256]{1,0:T(8,128)(2,1)S(1)} %shard_map.97), channel_id=1, source_target_pairs={{0,1},{1,0},{2,3},{3,2},{4,5},{5,4},{6,7},{7,6},{8,9},{9,8},{10,11... | collective-permute-start | bytes 451592 | tf_op jit(solution)/shard_map/ppermute | solution.py:26
  29.6 2.2 %collective-permute-done.5.refs_0_ = bf16[147,256]{1,0:T(8,128)(2,1)S(1)} collective-permute-done((bf16[147,256]{1,0:T(8,128)(2,1)S(1)}, bf16[147,256]{1,0:T(8,128)(2,1)S(1)}, u32[]{:S(2)}, u32[]{:S(2)}) %collective-permute-start.5) | collective-permute-done | bytes 75296 | tf_op jit(solution)/shard_map/ppermute | solution.py:44
  31.8 0.0 collective-permute-done.6.refs_1_
  31.8 0.6 %collective-permute-done.7.refs_2_ = bf16[147,256]{1,0:T(8,128)(2,1)S(1)} collective-permute-done((bf16[147,256]{1,0:T(8,128)(2,1)S(1)}, bf16[147,256]{1,0:T(8,128)(2,1)S(1)}, u32[]{:S(2)}, u32[]{:S(2)}) %collective-permute-start.7) | collective-permute-done | bytes 75296 | tf_op jit(solution)/shard_map/ppermute | solution.py:44
  32.4 0.3 shard_map.100
  32.7 1.5 %collective-permute-start.8 = (bf16[294,256]{1,0:T(8,128)(2,1)S(1)}, bf16[294,256]{1,0:T(8,128)(2,1)S(1)}, u32[]{:S(2)}, u32[]{:S(2)}) collective-permute-start(bf16[294,256]{1,0:T(8,128)(2,1)S(1)} %shard_map.100), channel_id=1, source_target_pairs={{0,1},{1,0},{2,3},{3,2},{4,5},{5,4},{6,7},{7,6},{8,9},{9,8},{10,11... | collective-permute-start | bytes 451592 | tf_op jit(solution)/shard_map/ppermute | solution.py:26
  34.1 0.3 shard_map.99
  34.5 0.3 shard_map.98
  34.8 0.0 collective-permute-done.4
  34.8 1.1 %broadcast_select_fusion.1 = bf16[2,294,256]{2,0,1:T(2,128)(2,1)} fusion(pred[2]{0:T(512)(128)(4,1)S(1)} %iota_compare_fusion, bf16[294,256]{1,0:T(8,128)(2,1)S(1)} %shard_map.98, bf16[294,256]{1,0:T(8,128)(2,1)S(1)} %collective-permute-done.4), kind=kLoop, calls=%fused_computation.1 | loop fusion | flops 150528 | bytes 602114 | tf_op jit(solution)/shard_map/jit(_where)/select_n | solution.py:236
  35.9 2.0 %collective-permute-done.8 = bf16[294,256]{1,0:T(8,128)(2,1)S(1)} collective-permute-done((bf16[294,256]{1,0:T(8,128)(2,1)S(1)}, bf16[294,256]{1,0:T(8,128)(2,1)S(1)}, u32[]{:S(2)}, u32[]{:S(2)}) %collective-permute-start.8) | collective-permute-done | bytes 150560 | tf_op jit(solution)/shard_map/ppermute | solution.py:26
  37.9 1.1 %broadcast_select_fusion = bf16[2,294,256]{2,0,1:T(2,128)(2,1)} fusion(pred[2]{0:T(512)(128)(4,1)S(1)} %iota_compare_fusion, bf16[294,256]{1,0:T(8,128)(2,1)S(1)} %shard_map.99, bf16[294,256]{1,0:T(8,128)(2,1)S(1)} %collective-permute-done.8), kind=kLoop, calls=%fused_computation | loop fusion | flops 150528 | bytes 602114 | tf_op jit(solution)/shard_map/jit(_where)/select_n | solution.py:236
  (2 shorter events, 0.0 us)
Async XLA Ops:
  0.6 4.1 %copy-start = (s32[2,588]{1,0:T(2,128)S(1)}, s32[2,588]{1,0:T(2,128)}, u32[]{:S(2)}) copy-start(s32[2,588]{1,0:T(2,128)} %param.15) | copy-start | bytes 14116
  1.7 11.4 %collective-permute-start = (bf16[126,1024]{1,0:T(8,128)(2,1)S(1)}, bf16[126,1024]{1,0:T(8,128)(2,1)S(1)}, u32[]{:S(2)}, u32[]{:S(2)}) collective-permute-start(bf16[126,1024]{1,0:T(8,128)(2,1)S(1)} %slice_bitcast_fusion), channel_id=1, source_target_pairs={{0,2},{2,4},{4,6},{6,0},{1,3},{3,5},{5,7},{7,1},{8,10},{10,12},{12... | collective-permute-start | bytes 774152 | tf_op jit(solution)/shard_map/ppermute | solution.py:26
  17.1 10.5 %collective-permute-start.1 = (bf16[147,256]{1,0:T(8,128)(2,1)S(1)}, bf16[147,256]{1,0:T(8,128)(2,1)S(1)}, u32[]{:S(2)}, u32[]{:S(2)}) collective-permute-start(bf16[147,256]{1,0:T(8,128)(2,1)S(1)} %get-tuple-element.31), channel_id=1, source_target_pairs={{0,4},{2,6},{4,0},{6,2},{1,5},{3,7},{5,1},{7,3},{8,12},{10,14},{12... | collective-permute-start | bytes 225800 | tf_op jit(solution)/shard_map/ppermute | solution.py:44
  17.9 9.7 %collective-permute-start.2 = (bf16[147,256]{1,0:T(8,128)(2,1)S(1)}, bf16[147,256]{1,0:T(8,128)(2,1)S(1)}, u32[]{:S(2)}, u32[]{:S(2)}) collective-permute-start(bf16[147,256]{1,0:T(8,128)(2,1)S(1)} %get-tuple-element.32), channel_id=1, source_target_pairs={{0,6},{2,4},{4,2},{6,0},{1,7},{3,5},{5,3},{7,1},{8,14},{10,12},{12... | collective-permute-start | bytes 225800 | tf_op jit(solution)/shard_map/ppermute | solution.py:44
  19.3 8.4 %collective-permute-start.3 = (bf16[147,256]{1,0:T(8,128)(2,1)S(1)}, bf16[147,256]{1,0:T(8,128)(2,1)S(1)}, u32[]{:S(2)}, u32[]{:S(2)}) collective-permute-start(bf16[147,256]{1,0:T(8,128)(2,1)S(1)} %get-tuple-element.33), channel_id=1, source_target_pairs={{0,2},{2,0},{4,6},{6,4},{1,3},{3,1},{5,7},{7,5},{8,10},{10,8},{12,... | collective-permute-start | bytes 225800 | tf_op jit(solution)/shard_map/ppermute | solution.py:44
  20.7 11.1 %collective-permute-start.5 = (bf16[147,256]{1,0:T(8,128)(2,1)S(1)}, bf16[147,256]{1,0:T(8,128)(2,1)S(1)}, u32[]{:S(2)}, u32[]{:S(2)}) collective-permute-start(bf16[147,256]{1,0:T(8,128)(2,1)S(1)} %get-tuple-element.35), channel_id=1, source_target_pairs={{0,4},{2,6},{4,0},{6,2},{1,5},{3,7},{5,1},{7,3},{8,12},{10,14},{12... | collective-permute-start | bytes 225800 | tf_op jit(solution)/shard_map/ppermute | solution.py:44
  22.3 9.4 %collective-permute-start.6 = (bf16[147,256]{1,0:T(8,128)(2,1)S(1)}, bf16[147,256]{1,0:T(8,128)(2,1)S(1)}, u32[]{:S(2)}, u32[]{:S(2)}) collective-permute-start(bf16[147,256]{1,0:T(8,128)(2,1)S(1)} %get-tuple-element.36), channel_id=1, source_target_pairs={{0,6},{2,4},{4,2},{6,0},{1,7},{3,5},{5,3},{7,1},{8,14},{10,12},{12... | collective-permute-start | bytes 225800 | tf_op jit(solution)/shard_map/ppermute | solution.py:44
  27.6 4.7 %collective-permute-start.7 = (bf16[147,256]{1,0:T(8,128)(2,1)S(1)}, bf16[147,256]{1,0:T(8,128)(2,1)S(1)}, u32[]{:S(2)}, u32[]{:S(2)}) collective-permute-start(bf16[147,256]{1,0:T(8,128)(2,1)S(1)} %get-tuple-element.37), channel_id=1, source_target_pairs={{0,2},{2,0},{4,6},{6,4},{1,3},{3,1},{5,7},{7,5},{8,10},{10,8},{12,... | collective-permute-start | bytes 225800 | tf_op jit(solution)/shard_map/ppermute | solution.py:44
  28.0 6.8 %collective-permute-start.4 = (bf16[294,256]{1,0:T(8,128)(2,1)S(1)}, bf16[294,256]{1,0:T(8,128)(2,1)S(1)}, u32[]{:S(2)}, u32[]{:S(2)}) collective-permute-start(bf16[294,256]{1,0:T(8,128)(2,1)S(1)} %shard_map.97), channel_id=1, source_target_pairs={{0,1},{1,0},{2,3},{3,2},{4,5},{5,4},{6,7},{7,6},{8,9},{9,8},{10,11... | collective-permute-start | bytes 451592 | tf_op jit(solution)/shard_map/ppermute | solution.py:26
  32.7 5.3 %collective-permute-start.8 = (bf16[294,256]{1,0:T(8,128)(2,1)S(1)}, bf16[294,256]{1,0:T(8,128)(2,1)S(1)}, u32[]{:S(2)}, u32[]{:S(2)}) collective-permute-start(bf16[294,256]{1,0:T(8,128)(2,1)S(1)} %shard_map.100), channel_id=1, source_target_pairs={{0,1},{1,0},{2,3},{3,2},{4,5},{5,4},{6,7},{7,6},{8,9},{9,8},{10,11... | collective-permute-start | bytes 451592 | tf_op jit(solution)/shard_map/ppermute | solution.py:26

commit v7 on v6

--- a/solution.py
+++ b/solution.py
@@ -30,18 +30,32 @@
     return n & (n - 1) == 0
 
 
-def target(place, d, n):
-    return place ^ d if paired(n) else lax.rem(place + d, n)
-
-
-def origin(place, d, n):
-    return place ^ d if paired(n) else lax.rem(place - d + n, n)
-
-
-def exchanged(block, axis, d):
-    n = lax.axis_size(axis)
-    pairs = [(i, i ^ d if paired(n) else (i + d) % n) for i in range(n)]
-    return lax.ppermute(block, axis, pairs)
+def rounds_of(n):
+    return [(0, 0)] + list(zip([1, *range(2, n)], [*range(2, n), 1]))
+
+
+def distance(place, r, n):
+    even, odd = rounds_of(n)[r]
+    return jnp.where(lax.rem(place[2], 2) == 0, even, odd)
+
+
+def target(place, r, n):
+    d = distance(place, r, n)
+    return place[0] ^ d if paired(n) else lax.rem(place[0] + d, n)
+
+
+def origin(place, r, n):
+    d = distance(place, r, n)
+    return place[0] ^ d if paired(n) else lax.rem(place[0] - d + n, n)
+
+
+def exchanged(block, r):
+    n = lax.axis_size("seq")
+    pairs = []
+    for i in range(lax.axis_size("dp")):
+        d = rounds_of(n)[r][i % 2]
+        pairs += [(i * n + j, i * n + (j ^ d if paired(n) else (j + d) % n)) for j in range(n)]
+    return lax.ppermute(block, ("dp", "seq"), pairs)
 
 
 def band_of(seq, n_seq):
@@ -56,7 +70,7 @@
     return jnp.where(cond, 1.0, 0.0).astype(jnp.bfloat16)
 
 
-def stage_kernel(rounds, place, order_ref, shifts_hbm, pages_hbm, gain_hbm, *refs):
+def stage_kernel(place, order_ref, shifts_hbm, pages_hbm, gain_hbm, *refs):
     weights, refs = refs[:4], refs[4:]
     rolled_ref, take_ref, same_ref, picks_ref, gain_ref, *staged = refs[:9]
     shifts, own, arrived = refs[9:]
@@ -67,12 +81,11 @@
         copy.start()
     band_rows = own.shape[0]
     rows, halo_rows = take_ref.shape
-    n_seq = len(rounds)
-    n_tensor, pos, _ = order_ref.shape
+    n_tensor, n_seq, pos, _ = picks_ref.shape
     for i in range(n_tensor):
         order = order_ref[lax.rem(place[1] + i, n_tensor)]
-        for r, d in enumerate(rounds):
-            local = order - band_of(origin(place[0], d, n_seq), n_seq) * band_rows
+        for r in range(n_seq):
+            local = order - band_of(origin(place, r, n_seq), n_seq) * band_rows
             picks_ref[i, r] = one_hot(
                 local == lax.broadcasted_iota(jnp.int32, (pos, band_rows), 1)
             )
@@ -147,8 +160,8 @@
     attended = jnp.concatenate(parts, axis=1)
     memory = (rolled + dot(attended, out_ref[...])).astype(jnp.bfloat16)
     own_cols = sent[0].shape[1]
-    for (is_value, d), block_ref in zip(blocks, sent):
-        at = target(place[0], d, key_ref.shape[1] // own_cols) * own_cols
+    for (is_value, r), block_ref in zip(blocks, sent):
+        at = target(place, r, key_ref.shape[1] // own_cols) * own_cols
         weight_ref = value_ref if is_value else key_ref
         block = dot(memory, weight_ref[:, pl.ds(pl.multiple_of(at, own_cols), own_cols)])
         block_ref[...] = block[: block_ref.shape[0]].astype(jnp.bfloat16)
@@ -182,16 +195,15 @@
     own_cols = key_weight.shape[1] // n_seq
     pos = row_order.shape[1] // n_tensor
     rows = -(-band_rows // 16) * 16
-    place = jnp.stack([lax.axis_index("seq"), lax.axis_index("tensor")]).astype(jnp.int32)
+    place = jnp.stack([lax.axis_index(axis) for axis in ("seq", "tensor", "dp")]).astype(jnp.int32)
     halo = rotated(memory_in[0, GRID_W :], "seq", 1)
     order = lax.dynamic_index_in_dim(row_order, lax.axis_index("tensor"), 0, False)
     order = order.reshape(n_tensor, pos, 1)
 
-    rounds = [*range(2, n_seq), 1, 0]
     weights = [qkv_weight, out_weight, key_weight, value_weight]
     off_chip = [shift_offsets, memory_in, norm_gain.reshape(1, emb), *weights]
     rolled_own, take, same, picks, gain, qkv_chip, out_chip, key_chip, value_chip = call(
-        functools.partial(stage_kernel, rounds),
+        stage_kernel,
         [
             jax.ShapeDtypeStruct((rows, emb), jnp.bfloat16),
             jax.ShapeDtypeStruct((rows, halo.shape[0]), jnp.bfloat16),
@@ -209,12 +221,12 @@
     )(place, order, *(pltpu.with_memory_space_constraint(x, pltpu.HBM) for x in off_chip))
 
     block = jax.ShapeDtypeStruct((band_rows, own_cols), jnp.bfloat16)
-    blocks = [(is_value, d) for is_value in (False, True) for d in rounds]
+    blocks = [(is_value, r) for is_value in (False, True) for r in range(n_seq)]
     sent = call(
         functools.partial(encode_kernel, blocks), [block] * len(blocks),
         1, 9, 2_000_000_000, 10_000_000,
     )(place, rolled_own, halo, take, same, gain, qkv_chip, out_chip, key_chip, value_chip)
-    held = [exchanged(b, "seq", d) if d else b for (_, d), b in zip(blocks, sent)]
+    held = [exchanged(b, r) if r else b for (_, r), b in zip(blocks, sent)]
 
     def selected(group, first, count):
         return call(

time: 39.2 us -> 38.6 us (0.985)
  waiting for transfers between devices: 12.4 us -> 10.4 us
  starting transfers between devices: 12.7 us -> 13.9 us
    ppermute x6, waiting for transfers between devices: 6.76 us -> 4.7 us  [exchanged(): return lax.ppermute(block, ('dp', 'seq'), pairs)]
    ppermute x6, starting transfers between devices: 6.53 us -> 8.34 us  [exchanged(): return lax.ppermute(block, ('dp', 'seq'), pairs)]
    ppermute x3, starting transfers between devices: 6.13 us -> 5.6 us  [rotated(): lax.ppermute(block, axis, [(i, (i + distance) % devices) for i in range(d...]
  transfers between devices with their start and end apart: 9 -> 9, of which waited for: 5 -> 5; matrix products, arithmetic and copies ran while one was open for 4% -> 4% of each run, Pallas kernels for 14% -> 15%
where the time goes in v7:
time: 38.6 us; the launch traced here: 38.4 us
  starting transfers between devices  13.9 us (36%)
  waiting for transfers between devices  10.4 us (27%)
  Pallas kernels  9.76 us (25%)
  other arithmetic  2.38 us (6%)
  local copies, waits for them, and re-layouts  1.25 us (3%)
  between operations  0.72 us (2%)
    ppermute x6, starting transfers between devices, exchanged(): return lax.ppermute(block, ('dp', 'seq'), pairs)  8.34 us
    ppermute x3, waiting for transfers between devices, rotated(): lax.ppermute(block, axis, [(i, (i + distance) % devices) for i in range(d...  5.67 us
    ppermute x3, starting transfers between devices, rotated(): lax.ppermute(block, axis, [(i, (i + distance) % devices) for i in range(d...  5.6 us
    ppermute x6, waiting for transfers between devices, exchanged(): return lax.ppermute(block, ('dp', 'seq'), pairs)  4.7 us
    pallas_call x1, Pallas kernels, local(): call(stage_kernel, [jax.ShapeDtypeStruct((rows, emb), jnp.bfloat16), jax....  4.46 us
    pallas_call x1, Pallas kernels, local(): call(functools.partial(encode_kernel, blocks), [block] * len(blocks), 1,...  4.04 us
    select_n x2, other arithmetic, by_page(): result = jnp.where(came, blocks[d][None], result)  2.29 us
    pallas_call x4, Pallas kernels, selected(): call(functools.partial(select_kernel, n_seq, first), [jax.ShapeDtypeStruc...  1.26 us
  transfers between devices with their start and end apart: 9, of which 5 were waited for; matrix products, arithmetic and copies ran while one was open for 4% of the time, Pallas kernels for 15%

profile of v7, /device:TPU:0, one launch (start us, length us, event | category | flops | bytes accessed | tf_op | source)
XLA Modules:
  0.0 38.4 jit_solution(2167660397754576950)
XLA Ops:
  0.6 0.0 copy-start
  0.6 1.0 %slice_bitcast_fusion = bf16[126,1024]{1,0:T(8,128)(2,1)S(1)} fusion(bf16[1,147,1024]{2,1,0:T(8,128)(2,1)} %pages_hbm.1), kind=kLoop, calls=%fused_computation.2 | loop fusion | bytes 516096 | tf_op jit(solution)/shard_map/squeeze | solution.py:199
  1.7 3.1 %collective-permute-start = (bf16[126,1024]{1,0:T(8,128)(2,1)S(1)}, bf16[126,1024]{1,0:T(8,128)(2,1)S(1)}, u32[]{:S(2)}, u32[]{:S(2)}) collective-permute-start(bf16[126,1024]{1,0:T(8,128)(2,1)S(1)} %slice_bitcast_fusion), channel_id=1, source_target_pairs={{0,2},{2,4},{4,6},{6,0},{1,3},{3,5},{5,7},{7,1},{8,10},{10,12},{12... | collective-permute-start | bytes 774152 | tf_op jit(solution)/shard_map/ppermute | solution.py:26
  4.8 0.0 copy-done
  4.8 0.2 reshape.22.order_ref
  5.0 0.1 pad_add_fusion.place
  5.1 4.5 %shard_map.95 = (bf16[160,1024]{1,0:T(8,128)(2,1)S(1)}, bf16[160,126]{1,0:T(8,128)(2,1)S(1)}, s32[160,160]{1,0:T(8,128)S(1)}, bf16[2,4,294,147]{3,2,1,0:T(8,128)...) custom-call(s32[3]{0:T(128)S(1)} %pad_add_fusion.place, ...), custom_call_target="tpu_custom_call" | custom-call | flops 50000000 | bytes 8000000 | tf_op jit(solution)/shard_map/pallas_call | solution.py:205
  9.5 3.6 %collective-permute-done.halo_ref = bf16[126,1024]{1,0:T(8,128)(2,1)S(1)} collective-permute-done((bf16[126,1024]{1,0:T(8,128)(2,1)S(1)}, bf16[126,1024]{1,0:T(8,128)(2,1)S(1)}, u32[]{:S(2)}, u32[]{:S(2)}) %collective-permute-start) | collective-permute-done | bytes 258080 | tf_op jit(solution)/shard_map/ppermute | solution.py:26
  13.1 4.0 %shard_map.96 = (bf16[147,256]{1,0:T(8,128)(2,1)S(1)}, bf16[147,256]{1,0:T(8,128)(2,1)S(1)}, bf16[147,256]{1,0:T(8,128)(2,1)S(1)}, bf16[147,256]{1,0:T(8,128)(2,...) custom-call(s32[3]{0:T(128)S(1)} %pad_add_fusion.place, ...), custom_call_target="tpu_custom_call" | custom-call | flops 2000000000 | bytes 10000000 | tf_op jit(solution)/shard_map/pallas_call | solution.py:225
  17.1 0.1 collective-permute-start.1
  17.2 2.3 %collective-permute-start.2 = (bf16[147,256]{1,0:T(8,128)(2,1)S(1)}, bf16[147,256]{1,0:T(8,128)(2,1)S(1)}, u32[]{:S(2)}, u32[]{:S(2)}) collective-permute-start(bf16[147,256]{1,0:T(8,128)(2,1)S(1)} %get-tuple-element.33), channel_id=1, source_target_pairs={{0,4},{2,6},{4,0},{6,2},{8,14},{10,12},{12,10},{14,8},{16,20},{18,... | collective-permute-start | bytes 225800 | tf_op jit(solution)/shard_map/ppermute | solution.py:58
  19.5 2.1 %collective-permute-start.3 = (bf16[147,256]{1,0:T(8,128)(2,1)S(1)}, bf16[147,256]{1,0:T(8,128)(2,1)S(1)}, u32[]{:S(2)}, u32[]{:S(2)}) collective-permute-start(bf16[147,256]{1,0:T(8,128)(2,1)S(1)} %get-tuple-element.34), channel_id=1, source_target_pairs={{0,6},{2,4},{4,2},{6,0},{8,10},{10,8},{12,14},{14,12},{16,22},{18,... | collective-permute-start | bytes 225800 | tf_op jit(solution)/shard_map/ppermute | solution.py:58
  21.6 0.0 collective-permute-start.5
  21.6 2.3 %collective-permute-start.6 = (bf16[147,256]{1,0:T(8,128)(2,1)S(1)}, bf16[147,256]{1,0:T(8,128)(2,1)S(1)}, u32[]{:S(2)}, u32[]{:S(2)}) collective-permute-start(bf16[147,256]{1,0:T(8,128)(2,1)S(1)} %get-tuple-element.37), channel_id=1, source_target_pairs={{0,4},{2,6},{4,0},{6,2},{8,14},{10,12},{12,10},{14,8},{16,20},{18,... | collective-permute-start | bytes 225800 | tf_op jit(solution)/shard_map/ppermute | solution.py:58
  23.9 0.5 %collective-permute-done.1.refs_1_ = bf16[147,256]{1,0:T(8,128)(2,1)S(1)} collective-permute-done((bf16[147,256]{1,0:T(8,128)(2,1)S(1)}, bf16[147,256]{1,0:T(8,128)(2,1)S(1)}, u32[]{:S(2)}, u32[]{:S(2)}) %collective-permute-start.1) | collective-permute-done | bytes 75296 | tf_op jit(solution)/shard_map/ppermute | solution.py:58
  24.4 1.6 %collective-permute-start.7 = (bf16[147,256]{1,0:T(8,128)(2,1)S(1)}, bf16[147,256]{1,0:T(8,128)(2,1)S(1)}, u32[]{:S(2)}, u32[]{:S(2)}) collective-permute-start(bf16[147,256]{1,0:T(8,128)(2,1)S(1)} %get-tuple-element.38), channel_id=1, source_target_pairs={{0,6},{2,4},{4,2},{6,0},{8,10},{10,8},{12,14},{14,12},{16,22},{18,... | collective-permute-start | bytes 225800 | tf_op jit(solution)/shard_map/ppermute | solution.py:58
  26.0 1.4 %collective-permute-done.2.refs_2_ = bf16[147,256]{1,0:T(8,128)(2,1)S(1)} collective-permute-done((bf16[147,256]{1,0:T(8,128)(2,1)S(1)}, bf16[147,256]{1,0:T(8,128)(2,1)S(1)}, u32[]{:S(2)}, u32[]{:S(2)}) %collective-permute-start.2) | collective-permute-done | bytes 75296 | tf_op jit(solution)/shard_map/ppermute | solution.py:58
  27.4 0.0 collective-permute-done.3.refs_3_
  27.4 0.3 shard_map.97
  27.7 1.2 %collective-permute-start.4 = (bf16[294,256]{1,0:T(8,128)(2,1)S(1)}, bf16[294,256]{1,0:T(8,128)(2,1)S(1)}, u32[]{:S(2)}, u32[]{:S(2)}) collective-permute-start(bf16[294,256]{1,0:T(8,128)(2,1)S(1)} %shard_map.97), channel_id=1, source_target_pairs={{0,1},{1,0},{2,3},{3,2},{4,5},{5,4},{6,7},{7,6},{8,9},{9,8},{10,11... | collective-permute-start | bytes 451592 | tf_op jit(solution)/shard_map/ppermute | solution.py:26
  28.9 0.0 collective-permute-done.5.refs_1_
  28.9 2.8 %collective-permute-done.6.refs_2_ = bf16[147,256]{1,0:T(8,128)(2,1)S(1)} collective-permute-done((bf16[147,256]{1,0:T(8,128)(2,1)S(1)}, bf16[147,256]{1,0:T(8,128)(2,1)S(1)}, u32[]{:S(2)}, u32[]{:S(2)}) %collective-permute-start.6) | collective-permute-done | bytes 75296 | tf_op jit(solution)/shard_map/ppermute | solution.py:58
  31.7 0.0 collective-permute-done.7.refs_3_
  31.7 0.3 shard_map.100
  32.0 1.3 %collective-permute-start.8 = (bf16[294,256]{1,0:T(8,128)(2,1)S(1)}, bf16[294,256]{1,0:T(8,128)(2,1)S(1)}, u32[]{:S(2)}, u32[]{:S(2)}) collective-permute-start(bf16[294,256]{1,0:T(8,128)(2,1)S(1)} %shard_map.100), channel_id=1, source_target_pairs={{0,1},{1,0},{2,3},{3,2},{4,5},{5,4},{6,7},{7,6},{8,9},{9,8},{10,11... | collective-permute-start | bytes 451592 | tf_op jit(solution)/shard_map/ppermute | solution.py:26
  33.4 0.3 shard_map.99
  33.7 0.3 shard_map.98
  34.0 0.0 collective-permute-done.4
  34.0 1.1 %broadcast_select_fusion.1 = bf16[2,294,256]{2,0,1:T(2,128)(2,1)} fusion(pred[2]{0:T(512)(128)(4,1)S(1)} %iota_compare_fusion, bf16[294,256]{1,0:T(8,128)(2,1)S(1)} %shard_map.98, bf16[294,256]{1,0:T(8,128)(2,1)S(1)} %collective-permute-done.4), kind=kLoop, calls=%fused_computation.1 | loop fusion | flops 150528 | bytes 602114 | tf_op jit(solution)/shard_map/jit(_where)/select_n | solution.py:248
  35.2 2.1 %collective-permute-done.8 = bf16[294,256]{1,0:T(8,128)(2,1)S(1)} collective-permute-done((bf16[294,256]{1,0:T(8,128)(2,1)S(1)}, bf16[294,256]{1,0:T(8,128)(2,1)S(1)}, u32[]{:S(2)}, u32[]{:S(2)}) %collective-permute-start.8) | collective-permute-done | bytes 150560 | tf_op jit(solution)/shard_map/ppermute | solution.py:26
  37.3 1.1 %broadcast_select_fusion = bf16[2,294,256]{2,0,1:T(2,128)(2,1)} fusion(pred[2]{0:T(512)(128)(4,1)S(1)} %iota_compare_fusion, bf16[294,256]{1,0:T(8,128)(2,1)S(1)} %shard_map.99, bf16[294,256]{1,0:T(8,128)(2,1)S(1)} %collective-permute-done.8), kind=kLoop, calls=%fused_computation | loop fusion | flops 150528 | bytes 602114 | tf_op jit(solution)/shard_map/jit(_where)/select_n | solution.py:248
  (2 shorter events, 0.0 us)
Async XLA Ops:
  0.6 4.1 %copy-start = (s32[2,588]{1,0:T(2,128)S(1)}, s32[2,588]{1,0:T(2,128)}, u32[]{:S(2)}) copy-start(s32[2,588]{1,0:T(2,128)} %param.15) | copy-start | bytes 14116
  1.7 11.4 %collective-permute-start = (bf16[126,1024]{1,0:T(8,128)(2,1)S(1)}, bf16[126,1024]{1,0:T(8,128)(2,1)S(1)}, u32[]{:S(2)}, u32[]{:S(2)}) collective-permute-start(bf16[126,1024]{1,0:T(8,128)(2,1)S(1)} %slice_bitcast_fusion), channel_id=1, source_target_pairs={{0,2},{2,4},{4,6},{6,0},{1,3},{3,5},{5,7},{7,1},{8,10},{10,12},{12... | collective-permute-start | bytes 774152 | tf_op jit(solution)/shard_map/ppermute | solution.py:26
  17.1 7.3 %collective-permute-start.1 = (bf16[147,256]{1,0:T(8,128)(2,1)S(1)}, bf16[147,256]{1,0:T(8,128)(2,1)S(1)}, u32[]{:S(2)}, u32[]{:S(2)}) collective-permute-start(bf16[147,256]{1,0:T(8,128)(2,1)S(1)} %get-tuple-element.32), channel_id=1, source_target_pairs={{0,2},{2,0},{4,6},{6,4},{8,12},{10,14},{12,8},{14,10},{16,18},{18,... | collective-permute-start | bytes 225800 | tf_op jit(solution)/shard_map/ppermute | solution.py:58
  17.2 10.1 %collective-permute-start.2 = (bf16[147,256]{1,0:T(8,128)(2,1)S(1)}, bf16[147,256]{1,0:T(8,128)(2,1)S(1)}, u32[]{:S(2)}, u32[]{:S(2)}) collective-permute-start(bf16[147,256]{1,0:T(8,128)(2,1)S(1)} %get-tuple-element.33), channel_id=1, source_target_pairs={{0,4},{2,6},{4,0},{6,2},{8,14},{10,12},{12,10},{14,8},{16,20},{18,... | collective-permute-start | bytes 225800 | tf_op jit(solution)/shard_map/ppermute | solution.py:58
  19.5 7.9 %collective-permute-start.3 = (bf16[147,256]{1,0:T(8,128)(2,1)S(1)}, bf16[147,256]{1,0:T(8,128)(2,1)S(1)}, u32[]{:S(2)}, u32[]{:S(2)}) collective-permute-start(bf16[147,256]{1,0:T(8,128)(2,1)S(1)} %get-tuple-element.34), channel_id=1, source_target_pairs={{0,6},{2,4},{4,2},{6,0},{8,10},{10,8},{12,14},{14,12},{16,22},{18,... | collective-permute-start | bytes 225800 | tf_op jit(solution)/shard_map/ppermute | solution.py:58
  21.6 7.3 %collective-permute-start.5 = (bf16[147,256]{1,0:T(8,128)(2,1)S(1)}, bf16[147,256]{1,0:T(8,128)(2,1)S(1)}, u32[]{:S(2)}, u32[]{:S(2)}) collective-permute-start(bf16[147,256]{1,0:T(8,128)(2,1)S(1)} %get-tuple-element.36), channel_id=1, source_target_pairs={{0,2},{2,0},{4,6},{6,4},{8,12},{10,14},{12,8},{14,10},{16,18},{18,... | collective-permute-start | bytes 225800 | tf_op jit(solution)/shard_map/ppermute | solution.py:58
  21.6 10.1 %collective-permute-start.6 = (bf16[147,256]{1,0:T(8,128)(2,1)S(1)}, bf16[147,256]{1,0:T(8,128)(2,1)S(1)}, u32[]{:S(2)}, u32[]{:S(2)}) collective-permute-start(bf16[147,256]{1,0:T(8,128)(2,1)S(1)} %get-tuple-element.37), channel_id=1, source_target_pairs={{0,4},{2,6},{4,0},{6,2},{8,14},{10,12},{12,10},{14,8},{16,20},{18,... | collective-permute-start | bytes 225800 | tf_op jit(solution)/shard_map/ppermute | solution.py:58
  24.4 7.3 %collective-permute-start.7 = (bf16[147,256]{1,0:T(8,128)(2,1)S(1)}, bf16[147,256]{1,0:T(8,128)(2,1)S(1)}, u32[]{:S(2)}, u32[]{:S(2)}) collective-permute-start(bf16[147,256]{1,0:T(8,128)(2,1)S(1)} %get-tuple-element.38), channel_id=1, source_target_pairs={{0,6},{2,4},{4,2},{6,0},{8,10},{10,8},{12,14},{14,12},{16,22},{18,... | collective-permute-start | bytes 225800 | tf_op jit(solution)/shard_map/ppermute | solution.py:58
  27.7 6.3 %collective-permute-start.4 = (bf16[294,256]{1,0:T(8,128)(2,1)S(1)}, bf16[294,256]{1,0:T(8,128)(2,1)S(1)}, u32[]{:S(2)}, u32[]{:S(2)}) collective-permute-start(bf16[294,256]{1,0:T(8,128)(2,1)S(1)} %shard_map.97), channel_id=1, source_target_pairs={{0,1},{1,0},{2,3},{3,2},{4,5},{5,4},{6,7},{7,6},{8,9},{9,8},{10,11... | collective-permute-start | bytes 451592 | tf_op jit(solution)/shard_map/ppermute | solution.py:26
  32.0 5.3 %collective-permute-start.8 = (bf16[294,256]{1,0:T(8,128)(2,1)S(1)}, bf16[294,256]{1,0:T(8,128)(2,1)S(1)}, u32[]{:S(2)}, u32[]{:S(2)}) collective-permute-start(bf16[294,256]{1,0:T(8,128)(2,1)S(1)} %shard_map.100), channel_id=1, source_target_pairs={{0,1},{1,0},{2,3},{3,2},{4,5},{5,4},{6,7},{7,6},{8,9},{9,8},{10,11... | collective-permute-start | bytes 451592 | tf_op jit(solution)/shard_map/ppermute | solution.py:26

commit v8 on v7

--- a/solution.py
+++ b/solution.py
@@ -14,6 +14,7 @@
 WIN = 7
 
 GROUP = 8
+SLAB = (56, 64)
 VMEM_LIMIT = 24 * 1024 * 1024
 
 SMEM = pl.BlockSpec(memory_space=pltpu.SMEM)
@@ -68,6 +69,17 @@
 
 def one_hot(cond):
     return jnp.where(cond, 1.0, 0.0).astype(jnp.bfloat16)
+
+
+def cells(index, band_rows):
+    window = index // (WIN * WIN)
+    inside = index - window * (WIN * WIN)
+    row = inside // WIN
+    return row, window * WIN + inside - row * WIN
+
+
+def slab(window):
+    return window * WIN * WIN // 8 * 8
 
 
 def stage_kernel(place, order_ref, shifts_hbm, pages_hbm, gain_hbm, *refs):
@@ -84,17 +96,21 @@
     n_tensor, n_seq, pos, _ = picks_ref.shape
     for i in range(n_tensor):
         order = order_ref[lax.rem(place[1] + i, n_tensor)]
+        order_band = order // band_rows
+        row = (order - order_band * band_rows) // GRID_W
+        col = order - order_band * band_rows - row * GRID_W
+        window = col // WIN
+        cell_at = (window * WIN + row) * WIN + col - window * WIN
         for r in range(n_seq):
-            local = order - band_of(origin(place, r, n_seq), n_seq) * band_rows
-            picks_ref[i, r] = one_hot(
-                local == lax.broadcasted_iota(jnp.int32, (pos, band_rows), 1)
-            )
+            band = band_of(origin(place, r, n_seq), n_seq)
+            at = jnp.where(order_band == band, cell_at, -1)
+            picks_ref[i, r] = one_hot(at == lax.broadcasted_iota(jnp.int32, (1, band_rows), 1))
     copies[0].wait()
     row_shift, col_shift = shifts[0, 0], shifts[0, 1]
 
     cell = lax.broadcasted_iota(jnp.int32, (rows, 1), 0)
-    cell_row = cell // GRID_W
-    from_col = cell - cell_row * GRID_W + col_shift
+    cell_row, cell_col = cells(cell, band_rows)
+    from_col = cell_col + col_shift
     from_col = jnp.where(from_col >= GRID_W, from_col - GRID_W, from_col)
     skipped = band_rows - halo_rows
     source = jnp.where(cell < band_rows, (cell_row + row_shift) * GRID_W + from_col - skipped, -1)
@@ -106,14 +122,16 @@
     band = band_of(place[0], n_seq)
 
     def marks(index):
-        row = index // GRID_W
-        col = index - row * GRID_W
+        row, col = cells(index, band_rows)
         wrap_row = (band * WIN + row >= GRID_H - row_shift).astype(jnp.int32)
         wrap_col = (col >= GRID_W - col_shift).astype(jnp.int32)
         return jnp.where(index < band_rows, (col // WIN) * 4 + 2 * wrap_row + wrap_col, -1)
 
-    same = marks(cell) == marks(lax.broadcasted_iota(jnp.int32, (1, rows), 1))
-    same_ref[...] = same.astype(jnp.int32)
+    windows, queries, keys = same_ref.shape
+    for w in range(windows):
+        query = slab(w) + lax.broadcasted_iota(jnp.int32, (queries, 1), 0)
+        key = slab(w) + lax.broadcasted_iota(jnp.int32, (1, keys), 1)
+        same_ref[w] = (marks(query) == marks(key)).astype(jnp.int32)
     copies[1].wait()
     rolled_ref[...] = dot(take_own, own[...]).astype(jnp.bfloat16)
     for copy in copies[2:]:
@@ -132,31 +150,56 @@
     centred = rolled - mean
     variance = jnp.mean(centred * centred, axis=-1, keepdims=True)
     normed = (centred * lax.rsqrt(variance + 1e-05) * gain_ref[...]).astype(jnp.bfloat16)
-    qkv = dot(normed, qkv_ref[...]).astype(jnp.bfloat16)
-    queries, keys, values = (qkv[:, i * attn : (i + 1) * attn] for i in range(3))
-
-    same = jnp.concatenate([same_ref[...]] * GROUP, axis=0) != 0
+    qkv = dot(normed, qkv_ref[...])
+
+    windows, queries, keys = same_ref.shape
     width = GROUP * HEAD_DIM
     lane_head = lax.broadcasted_iota(jnp.int32, (1, width), 1) // HEAD_DIM
-    parts = []
-    for g in range(HEADS // GROUP):
-        at = g * width
-        q, k, v = (part[:, at : at + width] for part in (queries, keys, values))
+    units = [(w, g) for w in range(windows) for g in range(HEADS // GROUP)]
+
+    def taken(w, g, kind, count):
+        at = kind * attn + g * width
+        return qkv[slab(w) : slab(w) + count, at : at + width].astype(jnp.bfloat16)
+
+    scores = []
+    for w, g in units:
+        q, k = taken(w, g, 0, queries), taken(w, g, 1, keys)
         stacked = jnp.concatenate(
             [jnp.where(lane_head == h, q, jnp.zeros_like(q)) for h in range(GROUP)], axis=0
         )
-        scores = lax.dot_general(
-            stacked, k, (((1,), (1,)), ((), ())), preferred_element_type=jnp.float32
+        scores.append(
+            lax.dot_general(
+                stacked, k, (((1,), (1,)), ((), ())), preferred_element_type=jnp.float32
+            )
         )
-        scores = jnp.where(same, scores * HEAD_DIM ** (-0.5), -1000000000.0)
-        scores = jnp.exp(scores - jnp.max(scores, axis=-1, keepdims=True))
-        total = jnp.sum(scores, axis=-1, keepdims=True)
-        weights = (scores * (1.0 / total)).astype(jnp.bfloat16)
-        mixed = dot(weights, v)
-        part = jnp.zeros((rows, width), jnp.float32)
-        for h in range(GROUP):
-            part = jnp.where(lane_head == h, mixed[h * rows : (h + 1) * rows], part)
-        parts.append(part.astype(jnp.bfloat16))
+    weights = []
+    for (w, _), score in zip(units, scores):
+        same = jnp.concatenate([same_ref[w]] * GROUP, axis=0) != 0
+        score = jnp.where(same, score * HEAD_DIM ** (-0.5), -1000000000.0)
+        score = jnp.exp(score - jnp.max(score, axis=-1, keepdims=True))
+        total = jnp.sum(score, axis=-1, keepdims=True)
+        weights.append((score * (1.0 / total)).astype(jnp.bfloat16))
+    parts = [[] for _ in range(HEADS // GROUP)]
+    for (w, g), weight in zip(units, weights):
+        mixed = dot(weight, taken(w, g, 2, keys))
+        mine = mixed[:queries]
+        for h in range(1, GROUP):
+            mine = jnp.where(lane_head == h, mixed[h * queries : (h + 1) * queries], mine)
+        part = parts[g]
+        if w == 0:
+            part.append(mine)
+            continue
+        overlap = slab(w - 1) + queries - slab(w)
+        row = slab(w) + lax.broadcasted_iota(jnp.int32, (overlap, 1), 0)
+        last = part.pop()
+        part.append(last[:-overlap])
+        part.append(jnp.where(row < w * WIN * WIN, last[-overlap:], mine[:overlap]))
+        part.append(mine[overlap:])
+    pad = rows - slab(windows - 1) - queries
+    parts = [
+        jnp.concatenate([*part, jnp.zeros((pad, width), jnp.float32)], axis=0).astype(jnp.bfloat16)
+        for part in parts
+    ]
     attended = jnp.concatenate(parts, axis=1)
     memory = (rolled + dot(attended, out_ref[...])).astype(jnp.bfloat16)
     own_cols = sent[0].shape[1]
@@ -207,7 +250,7 @@
         [
             jax.ShapeDtypeStruct((rows, emb), jnp.bfloat16),
             jax.ShapeDtypeStruct((rows, halo.shape[0]), jnp.bfloat16),
-            jax.ShapeDtypeStruct((rows, rows), jnp.int32),
+            jax.ShapeDtypeStruct((GRID_W // WIN, *SLAB), jnp.int32),
             jax.ShapeDtypeStruct((n_tensor, n_seq, pos, band_rows), jnp.bfloat16),
             jax.ShapeDtypeStruct((1, emb), jnp.float32),
         ]

time: 38.6 us -> 38.1 us (0.987)
  waiting for transfers between devices: 10.4 us -> 9.65 us
    ppermute x3, waiting for transfers between devices: 5.67 us -> 4.98 us  [rotated(): lax.ppermute(block, axis, [(i, (i + distance) % devices) for i in range(d...]
    pallas_call x1, Pallas kernels: 4.46 us -> 5.15 us  [local(): call(stage_kernel, [jax.ShapeDtypeStruct((rows, emb), jnp.bfloat16), jax....]
    pallas_call x1, Pallas kernels: 4.04 us -> 3.55 us  [local(): call(functools.partial(encode_kernel, blocks), [block] * len(blocks), 1,...]
  transfers between devices with their start and end apart: 9 -> 9, of which waited for: 5 -> 5; matrix products, arithmetic and copies ran while one was open for 4% -> 4% of each run, Pallas kernels for 15% -> 17%
where the time goes in v8:
time: 38.1 us; the launch traced here: 37.9 us
  starting transfers between devices  14 us (37%)
  Pallas kernels  9.96 us (26%)
  waiting for transfers between devices  9.65 us (25%)
  other arithmetic  2.38 us (6%)
  local copies, waits for them, and re-layouts  1.25 us (3%)
  between operations  0.72 us (2%)
    ppermute x6, starting transfers between devices, exchanged(): return lax.ppermute(block, ('dp', 'seq'), pairs)  8.35 us
    ppermute x3, starting transfers between devices, rotated(): lax.ppermute(block, axis, [(i, (i + distance) % devices) for i in range(d...  5.62 us
    pallas_call x1, Pallas kernels, local(): call(stage_kernel, [jax.ShapeDtypeStruct((rows, emb), jnp.bfloat16), jax....  5.15 us
    ppermute x3, waiting for transfers between devices, rotated(): lax.ppermute(block, axis, [(i, (i + distance) % devices) for i in range(d...  4.98 us
    ppermute x6, waiting for transfers between devices, exchanged(): return lax.ppermute(block, ('dp', 'seq'), pairs)  4.67 us
    pallas_call x1, Pallas kernels, local(): call(functools.partial(encode_kernel, blocks), [block] * len(blocks), 1,...  3.55 us
    select_n x2, other arithmetic, by_page(): result = jnp.where(came, blocks[d][None], result)  2.29 us
    pallas_call x4, Pallas kernels, selected(): call(functools.partial(select_kernel, n_seq, first), [jax.ShapeDtypeStruc...  1.26 us
  transfers between devices with their start and end apart: 9, of which 5 were waited for; matrix products, arithmetic and copies ran while one was open for 4% of the time, Pallas kernels for 17%

profile of v8, /device:TPU:0, one launch (start us, length us, event | category | flops | bytes accessed | tf_op | source)
XLA Modules:
  0.0 37.9 jit_solution(10596821149423670871)
XLA Ops:
  0.6 0.0 copy-start
  0.6 1.0 %slice_bitcast_fusion = bf16[126,1024]{1,0:T(8,128)(2,1)S(1)} fusion(bf16[1,147,1024]{2,1,0:T(8,128)(2,1)} %pages_hbm.1), kind=kLoop, calls=%fused_computation.2 | loop fusion | bytes 516096 | tf_op jit(solution)/shard_map/squeeze | solution.py:242
  1.7 3.1 %collective-permute-start = (bf16[126,1024]{1,0:T(8,128)(2,1)S(1)}, bf16[126,1024]{1,0:T(8,128)(2,1)S(1)}, u32[]{:S(2)}, u32[]{:S(2)}) collective-permute-start(bf16[126,1024]{1,0:T(8,128)(2,1)S(1)} %slice_bitcast_fusion), channel_id=1, source_target_pairs={{0,2},{2,4},{4,6},{6,0},{1,3},{3,5},{5,7},{7,1},{8,10},{10,12},{12... | collective-permute-start | bytes 774152 | tf_op jit(solution)/shard_map/ppermute | solution.py:27
  4.8 0.0 copy-done
  4.8 0.2 reshape.22.order_ref
  5.0 0.1 pad_add_fusion.place
  5.1 5.1 %shard_map.95 = (bf16[160,1024]{1,0:T(8,128)(2,1)S(1)}, bf16[160,126]{1,0:T(8,128)(2,1)S(1)}, s32[3,56,64]{2,1,0:T(8,128)S(1)}, bf16[2,4,294,147]{3,2,1,0:T(8,12...) custom-call(s32[3]{0:T(128)S(1)} %pad_add_fusion.place, ...), custom_call_target="tpu_custom_call" | custom-call | flops 50000000 | bytes 8000000 | tf_op jit(solution)/shard_map/pallas_call | solution.py:248
  10.2 2.9 %collective-permute-done.halo_ref = bf16[126,1024]{1,0:T(8,128)(2,1)S(1)} collective-permute-done((bf16[126,1024]{1,0:T(8,128)(2,1)S(1)}, bf16[126,1024]{1,0:T(8,128)(2,1)S(1)}, u32[]{:S(2)}, u32[]{:S(2)}) %collective-permute-start) | collective-permute-done | bytes 258080 | tf_op jit(solution)/shard_map/ppermute | solution.py:27
  13.1 3.6 %shard_map.96 = (bf16[147,256]{1,0:T(8,128)(2,1)S(1)}, bf16[147,256]{1,0:T(8,128)(2,1)S(1)}, bf16[147,256]{1,0:T(8,128)(2,1)S(1)}, bf16[147,256]{1,0:T(8,128)(2,...) custom-call(s32[3]{0:T(128)S(1)} %pad_add_fusion.place, ...), custom_call_target="tpu_custom_call" | custom-call | flops 2000000000 | bytes 10000000 | tf_op jit(solution)/shard_map/pallas_call | solution.py:268
  16.6 0.1 collective-permute-start.1
  16.7 2.3 %collective-permute-start.2 = (bf16[147,256]{1,0:T(8,128)(2,1)S(1)}, bf16[147,256]{1,0:T(8,128)(2,1)S(1)}, u32[]{:S(2)}, u32[]{:S(2)}) collective-permute-start(bf16[147,256]{1,0:T(8,128)(2,1)S(1)} %get-tuple-element.33), channel_id=1, source_target_pairs={{0,4},{2,6},{4,0},{6,2},{8,14},{10,12},{12,10},{14,8},{16,20},{18,... | collective-permute-start | bytes 225800 | tf_op jit(solution)/shard_map/ppermute | solution.py:59
  19.0 2.1 %collective-permute-start.3 = (bf16[147,256]{1,0:T(8,128)(2,1)S(1)}, bf16[147,256]{1,0:T(8,128)(2,1)S(1)}, u32[]{:S(2)}, u32[]{:S(2)}) collective-permute-start(bf16[147,256]{1,0:T(8,128)(2,1)S(1)} %get-tuple-element.34), channel_id=1, source_target_pairs={{0,6},{2,4},{4,2},{6,0},{8,10},{10,8},{12,14},{14,12},{16,22},{18,... | collective-permute-start | bytes 225800 | tf_op jit(solution)/shard_map/ppermute | solution.py:59
  21.1 0.0 collective-permute-start.5
  21.1 2.3 %collective-permute-start.6 = (bf16[147,256]{1,0:T(8,128)(2,1)S(1)}, bf16[147,256]{1,0:T(8,128)(2,1)S(1)}, u32[]{:S(2)}, u32[]{:S(2)}) collective-permute-start(bf16[147,256]{1,0:T(8,128)(2,1)S(1)} %get-tuple-element.37), channel_id=1, source_target_pairs={{0,4},{2,6},{4,0},{6,2},{8,14},{10,12},{12,10},{14,8},{16,20},{18,... | collective-permute-start | bytes 225800 | tf_op jit(solution)/shard_map/ppermute | solution.py:59
  23.4 0.5 %collective-permute-done.1.refs_1_ = bf16[147,256]{1,0:T(8,128)(2,1)S(1)} collective-permute-done((bf16[147,256]{1,0:T(8,128)(2,1)S(1)}, bf16[147,256]{1,0:T(8,128)(2,1)S(1)}, u32[]{:S(2)}, u32[]{:S(2)}) %collective-permute-start.1) | collective-permute-done | bytes 75296 | tf_op jit(solution)/shard_map/ppermute | solution.py:59
  23.9 1.6 %collective-permute-start.7 = (bf16[147,256]{1,0:T(8,128)(2,1)S(1)}, bf16[147,256]{1,0:T(8,128)(2,1)S(1)}, u32[]{:S(2)}, u32[]{:S(2)}) collective-permute-start(bf16[147,256]{1,0:T(8,128)(2,1)S(1)} %get-tuple-element.38), channel_id=1, source_target_pairs={{0,6},{2,4},{4,2},{6,0},{8,10},{10,8},{12,14},{14,12},{16,22},{18,... | collective-permute-start | bytes 225800 | tf_op jit(solution)/shard_map/ppermute | solution.py:59
  25.5 1.4 %collective-permute-done.2.refs_2_ = bf16[147,256]{1,0:T(8,128)(2,1)S(1)} collective-permute-done((bf16[147,256]{1,0:T(8,128)(2,1)S(1)}, bf16[147,256]{1,0:T(8,128)(2,1)S(1)}, u32[]{:S(2)}, u32[]{:S(2)}) %collective-permute-start.2) | collective-permute-done | bytes 75296 | tf_op jit(solution)/shard_map/ppermute | solution.py:59
  26.9 0.0 collective-permute-done.3.refs_3_
  26.9 0.3 shard_map.97
  27.2 1.2 %collective-permute-start.4 = (bf16[294,256]{1,0:T(8,128)(2,1)S(1)}, bf16[294,256]{1,0:T(8,128)(2,1)S(1)}, u32[]{:S(2)}, u32[]{:S(2)}) collective-permute-start(bf16[294,256]{1,0:T(8,128)(2,1)S(1)} %shard_map.97), channel_id=1, source_target_pairs={{0,1},{1,0},{2,3},{3,2},{4,5},{5,4},{6,7},{7,6},{8,9},{9,8},{10,11... | collective-permute-start | bytes 451592 | tf_op jit(solution)/shard_map/ppermute | solution.py:27
  28.4 0.0 collective-permute-done.5.refs_1_
  28.4 2.8 %collective-permute-done.6.refs_2_ = bf16[147,256]{1,0:T(8,128)(2,1)S(1)} collective-permute-done((bf16[147,256]{1,0:T(8,128)(2,1)S(1)}, bf16[147,256]{1,0:T(8,128)(2,1)S(1)}, u32[]{:S(2)}, u32[]{:S(2)}) %collective-permute-start.6) | collective-permute-done | bytes 75296 | tf_op jit(solution)/shard_map/ppermute | solution.py:59
  31.2 0.0 collective-permute-done.7.refs_3_
  31.2 0.3 shard_map.100
  31.5 1.3 %collective-permute-start.8 = (bf16[294,256]{1,0:T(8,128)(2,1)S(1)}, bf16[294,256]{1,0:T(8,128)(2,1)S(1)}, u32[]{:S(2)}, u32[]{:S(2)}) collective-permute-start(bf16[294,256]{1,0:T(8,128)(2,1)S(1)} %shard_map.100), channel_id=1, source_target_pairs={{0,1},{1,0},{2,3},{3,2},{4,5},{5,4},{6,7},{7,6},{8,9},{9,8},{10,11... | collective-permute-start | bytes 451592 | tf_op jit(solution)/shard_map/ppermute | solution.py:27
  32.9 0.3 shard_map.99
  33.2 0.3 shard_map.98
  33.5 0.0 collective-permute-done.4
  33.5 1.1 %broadcast_select_fusion.1 = bf16[2,294,256]{2,0,1:T(2,128)(2,1)} fusion(pred[2]{0:T(512)(128)(4,1)S(1)} %iota_compare_fusion, bf16[294,256]{1,0:T(8,128)(2,1)S(1)} %shard_map.98, bf16[294,256]{1,0:T(8,128)(2,1)S(1)} %collective-permute-done.4), kind=kLoop, calls=%fused_computation.1 | loop fusion | flops 150528 | bytes 602114 | tf_op jit(solution)/shard_map/jit(_where)/select_n | solution.py:291
  34.7 2.1 %collective-permute-done.8 = bf16[294,256]{1,0:T(8,128)(2,1)S(1)} collective-permute-done((bf16[294,256]{1,0:T(8,128)(2,1)S(1)}, bf16[294,256]{1,0:T(8,128)(2,1)S(1)}, u32[]{:S(2)}, u32[]{:S(2)}) %collective-permute-start.8) | collective-permute-done | bytes 150560 | tf_op jit(solution)/shard_map/ppermute | solution.py:27
  36.8 1.1 %broadcast_select_fusion = bf16[2,294,256]{2,0,1:T(2,128)(2,1)} fusion(pred[2]{0:T(512)(128)(4,1)S(1)} %iota_compare_fusion, bf16[294,256]{1,0:T(8,128)(2,1)S(1)} %shard_map.99, bf16[294,256]{1,0:T(8,128)(2,1)S(1)} %collective-permute-done.8), kind=kLoop, calls=%fused_computation | loop fusion | flops 150528 | bytes 602114 | tf_op jit(solution)/shard_map/jit(_where)/select_n | solution.py:291
  (2 shorter events, 0.0 us)
Async XLA Ops:
  0.6 4.1 %copy-start = (s32[2,588]{1,0:T(2,128)S(1)}, s32[2,588]{1,0:T(2,128)}, u32[]{:S(2)}) copy-start(s32[2,588]{1,0:T(2,128)} %param.15) | copy-start | bytes 14116
  1.7 11.4 %collective-permute-start = (bf16[126,1024]{1,0:T(8,128)(2,1)S(1)}, bf16[126,1024]{1,0:T(8,128)(2,1)S(1)}, u32[]{:S(2)}, u32[]{:S(2)}) collective-permute-start(bf16[126,1024]{1,0:T(8,128)(2,1)S(1)} %slice_bitcast_fusion), channel_id=1, source_target_pairs={{0,2},{2,4},{4,6},{6,0},{1,3},{3,5},{5,7},{7,1},{8,10},{10,12},{12... | collective-permute-start | bytes 774152 | tf_op jit(solution)/shard_map/ppermute | solution.py:27
  16.6 7.3 %collective-permute-start.1 = (bf16[147,256]{1,0:T(8,128)(2,1)S(1)}, bf16[147,256]{1,0:T(8,128)(2,1)S(1)}, u32[]{:S(2)}, u32[]{:S(2)}) collective-permute-start(bf16[147,256]{1,0:T(8,128)(2,1)S(1)} %get-tuple-element.32), channel_id=1, source_target_pairs={{0,2},{2,0},{4,6},{6,4},{8,12},{10,14},{12,8},{14,10},{16,18},{18,... | collective-permute-start | bytes 225800 | tf_op jit(solution)/shard_map/ppermute | solution.py:59
  16.7 10.2 %collective-permute-start.2 = (bf16[147,256]{1,0:T(8,128)(2,1)S(1)}, bf16[147,256]{1,0:T(8,128)(2,1)S(1)}, u32[]{:S(2)}, u32[]{:S(2)}) collective-permute-start(bf16[147,256]{1,0:T(8,128)(2,1)S(1)} %get-tuple-element.33), channel_id=1, source_target_pairs={{0,4},{2,6},{4,0},{6,2},{8,14},{10,12},{12,10},{14,8},{16,20},{18,... | collective-permute-start | bytes 225800 | tf_op jit(solution)/shard_map/ppermute | solution.py:59
  19.0 7.9 %collective-permute-start.3 = (bf16[147,256]{1,0:T(8,128)(2,1)S(1)}, bf16[147,256]{1,0:T(8,128)(2,1)S(1)}, u32[]{:S(2)}, u32[]{:S(2)}) collective-permute-start(bf16[147,256]{1,0:T(8,128)(2,1)S(1)} %get-tuple-element.34), channel_id=1, source_target_pairs={{0,6},{2,4},{4,2},{6,0},{8,10},{10,8},{12,14},{14,12},{16,22},{18,... | collective-permute-start | bytes 225800 | tf_op jit(solution)/shard_map/ppermute | solution.py:59
  21.1 7.3 %collective-permute-start.5 = (bf16[147,256]{1,0:T(8,128)(2,1)S(1)}, bf16[147,256]{1,0:T(8,128)(2,1)S(1)}, u32[]{:S(2)}, u32[]{:S(2)}) collective-permute-start(bf16[147,256]{1,0:T(8,128)(2,1)S(1)} %get-tuple-element.36), channel_id=1, source_target_pairs={{0,2},{2,0},{4,6},{6,4},{8,12},{10,14},{12,8},{14,10},{16,18},{18,... | collective-permute-start | bytes 225800 | tf_op jit(solution)/shard_map/ppermute | solution.py:59
  21.1 10.1 %collective-permute-start.6 = (bf16[147,256]{1,0:T(8,128)(2,1)S(1)}, bf16[147,256]{1,0:T(8,128)(2,1)S(1)}, u32[]{:S(2)}, u32[]{:S(2)}) collective-permute-start(bf16[147,256]{1,0:T(8,128)(2,1)S(1)} %get-tuple-element.37), channel_id=1, source_target_pairs={{0,4},{2,6},{4,0},{6,2},{8,14},{10,12},{12,10},{14,8},{16,20},{18,... | collective-permute-start | bytes 225800 | tf_op jit(solution)/shard_map/ppermute | solution.py:59
  23.9 7.3 %collective-permute-start.7 = (bf16[147,256]{1,0:T(8,128)(2,1)S(1)}, bf16[147,256]{1,0:T(8,128)(2,1)S(1)}, u32[]{:S(2)}, u32[]{:S(2)}) collective-permute-start(bf16[147,256]{1,0:T(8,128)(2,1)S(1)} %get-tuple-element.38), channel_id=1, source_target_pairs={{0,6},{2,4},{4,2},{6,0},{8,10},{10,8},{12,14},{14,12},{16,22},{18,... | collective-permute-start | bytes 225800 | tf_op jit(solution)/shard_map/ppermute | solution.py:59
  27.2 6.3 %collective-permute-start.4 = (bf16[294,256]{1,0:T(8,128)(2,1)S(1)}, bf16[294,256]{1,0:T(8,128)(2,1)S(1)}, u32[]{:S(2)}, u32[]{:S(2)}) collective-permute-start(bf16[294,256]{1,0:T(8,128)(2,1)S(1)} %shard_map.97), channel_id=1, source_target_pairs={{0,1},{1,0},{2,3},{3,2},{4,5},{5,4},{6,7},{7,6},{8,9},{9,8},{10,11... | collective-permute-start | bytes 451592 | tf_op jit(solution)/shard_map/ppermute | solution.py:27
  31.5 5.3 %collective-permute-start.8 = (bf16[294,256]{1,0:T(8,128)(2,1)S(1)}, bf16[294,256]{1,0:T(8,128)(2,1)S(1)}, u32[]{:S(2)}, u32[]{:S(2)}) collective-permute-start(bf16[294,256]{1,0:T(8,128)(2,1)S(1)} %shard_map.100), channel_id=1, source_target_pairs={{0,1},{1,0},{2,3},{3,2},{4,5},{5,4},{6,7},{7,6},{8,9},{9,8},{10,11... | collective-permute-start | bytes 451592 | tf_op jit(solution)/shard_map/ppermute | solution.py:27

commit v9 on v8

--- a/solution.py
+++ b/solution.py
@@ -32,7 +32,9 @@
 
 
 def rounds_of(n):
-    return [(0, 0)] + list(zip([1, *range(2, n)], [*range(2, n), 1]))
+    even = [*range(1, n)]
+    odd = [*even[1:2], *even[:1], *even[2:]]
+    return [(0, 0), *zip(even, odd)]
 
 
 def distance(place, r, n):
@@ -202,18 +204,24 @@
     ]
     attended = jnp.concatenate(parts, axis=1)
     memory = (rolled + dot(attended, out_ref[...])).astype(jnp.bfloat16)
-    own_cols = sent[0].shape[1]
-    for (is_value, r), block_ref in zip(blocks, sent):
-        at = target(place, r, key_ref.shape[1] // own_cols) * own_cols
-        weight_ref = value_ref if is_value else key_ref
-        block = dot(memory, weight_ref[:, pl.ds(pl.multiple_of(at, own_cols), own_cols)])
-        block_ref[...] = block[: block_ref.shape[0]].astype(jnp.bfloat16)
-
-
-def select_kernel(n_seq, first, picks_ref, *refs):
-    held, outs = refs[:n_seq], refs[n_seq:]
+    n_seq = 1 + max(r for _, r in blocks)
+    own_cols = key_ref.shape[1] // n_seq
+    for (kinds, r), block_ref in zip(blocks, sent):
+        at = pl.multiple_of(target(place, r, n_seq) * own_cols, own_cols)
+        for i, kind in enumerate(kinds):
+            block = dot(memory, (key_ref, value_ref)[kind][:, pl.ds(at, own_cols)])
+            cols = slice(i * own_cols, (i + 1) * own_cols)
+            block_ref[:, cols] = block[: block_ref.shape[0]].astype(jnp.bfloat16)
+
+
+def select_kernel(rounds, first, picks_ref, *refs):
+    held, outs = refs[: len(rounds)], refs[len(rounds) :]
     for i, out in enumerate(outs):
-        terms = [dot(picks_ref[first + i, r], held[r][...]) for r in range(n_seq)]
+        width = out.shape[1]
+        terms = [
+            dot(picks_ref[first + i, r], ref[:, at * width : (at + 1) * width])
+            for (r, at), ref in zip(rounds, held)
+        ]
         out[...] = sum(terms[1:], terms[0]).astype(jnp.bfloat16)
 
 
@@ -263,20 +271,25 @@
         ],
     )(place, order, *(pltpu.with_memory_space_constraint(x, pltpu.HBM) for x in off_chip))
 
-    block = jax.ShapeDtypeStruct((band_rows, own_cols), jnp.bfloat16)
-    blocks = [(is_value, r) for is_value in (False, True) for r in range(n_seq)]
+    apart = [0, *range(2, n_seq)]
+    blocks = [((0,), r) for r in apart] + [((0, 1), 1)] + [((1,), r) for r in apart]
     sent = call(
-        functools.partial(encode_kernel, blocks), [block] * len(blocks),
+        functools.partial(encode_kernel, blocks),
+        [
+            jax.ShapeDtypeStruct((band_rows, len(kinds) * own_cols), jnp.bfloat16)
+            for kinds, _ in blocks
+        ],
         1, 9, 2_000_000_000, 10_000_000,
     )(place, rolled_own, halo, take, same, gain, qkv_chip, out_chip, key_chip, value_chip)
     held = [exchanged(b, r) if r else b for (_, r), b in zip(blocks, sent)]
 
-    def selected(group, first, count):
+    def selected(kind, first, count):
+        mine = [(r, kinds.index(kind), b) for (kinds, r), b in zip(blocks, held) if kind in kinds]
         return call(
-            functools.partial(select_kernel, n_seq, first),
+            functools.partial(select_kernel, [(r, at) for r, at, _ in mine], first),
             [jax.ShapeDtypeStruct((pos, own_cols), jnp.bfloat16)] * count,
             0, 1 + n_seq, 300_000_000, 1_000_000,
-        )(picks, *held[group * n_seq : (group + 1) * n_seq])
+        )(picks, *(b for *_, b in mine))
 
     def gathered(group):
         away = selected(group, 1, n_tensor - 1)

time: 38.1 us -> 37.7 us (0.990)
  starting transfers between devices: 14 us -> 12.4 us
  waiting for transfers between devices: 9.65 us -> 10.9 us
    ppermute x6 -> x5, starting transfers between devices: 8.35 us -> 6.19 us  [exchanged(): return lax.ppermute(block, ('dp', 'seq'), pairs)]
    ppermute x6 -> x5, waiting for transfers between devices: 4.67 us -> 6.08 us  [exchanged(): return lax.ppermute(block, ('dp', 'seq'), pairs)]
    ppermute x3, starting transfers between devices: 5.62 us -> 6.24 us  [rotated(): lax.ppermute(block, axis, [(i, (i + distance) % devices) for i in range(d...]
  transfers between devices with their start and end apart: 9 -> 8, of which waited for: 5 -> 6; matrix products, arithmetic and copies ran while one was open for 4% -> 4% of each run, Pallas kernels for 17% -> 17%
where the time goes in v9:
time: 37.7 us; the launch traced here: 37.6 us
  starting transfers between devices  12.4 us (33%)
  waiting for transfers between devices  10.9 us (29%)
  Pallas kernels  9.91 us (26%)
  other arithmetic  2.38 us (6%)
  local copies, waits for them, and re-layouts  1.25 us (3%)
  between operations  0.71 us (2%)
    ppermute x3, starting transfers between devices, rotated(): lax.ppermute(block, axis, [(i, (i + distance) % devices) for i in range(d...  6.24 us
    ppermute x5, starting transfers between devices, exchanged(): return lax.ppermute(block, ('dp', 'seq'), pairs)  6.19 us
    ppermute x5, waiting for transfers between devices, exchanged(): return lax.ppermute(block, ('dp', 'seq'), pairs)  6.08 us
    pallas_call x1, Pallas kernels, local(): call(stage_kernel, [jax.ShapeDtypeStruct((rows, emb), jnp.bfloat16), jax....  5.09 us
    ppermute x3, waiting for transfers between devices, rotated(): lax.ppermute(block, axis, [(i, (i + distance) % devices) for i in range(d...  4.8 us
    pallas_call x1, Pallas kernels, local(): call(functools.partial(encode_kernel, blocks), [jax.ShapeDtypeStruct((ban...  3.55 us
    select_n x2, other arithmetic, by_page(): result = jnp.where(came, blocks[d][None], result)  2.29 us
    pallas_call x4, Pallas kernels, selected(): call(functools.partial(select_kernel, [(r, at) for r, at, _ in mine], fir...  1.26 us
  transfers between devices with their start and end apart: 8, of which 6 were waited for; matrix products, arithmetic and copies ran while one was open for 4% of the time, Pallas kernels for 17%

profile of v9, /device:TPU:0, one launch (start us, length us, event | category | flops | bytes accessed | tf_op | source)
XLA Modules:
  0.0 37.6 jit_solution(6433638114543472233)
XLA Ops:
  0.6 0.0 copy-start
  0.6 1.0 %slice_bitcast_fusion = bf16[126,1024]{1,0:T(8,128)(2,1)S(1)} fusion(bf16[1,147,1024]{2,1,0:T(8,128)(2,1)} %pages_hbm.1), kind=kLoop, calls=%fused_computation.2 | loop fusion | bytes 516096 | tf_op jit(solution)/shard_map/squeeze | solution.py:250
  1.7 3.1 %collective-permute-start = (bf16[126,1024]{1,0:T(8,128)(2,1)S(1)}, bf16[126,1024]{1,0:T(8,128)(2,1)S(1)}, u32[]{:S(2)}, u32[]{:S(2)}) collective-permute-start(bf16[126,1024]{1,0:T(8,128)(2,1)S(1)} %slice_bitcast_fusion), channel_id=1, source_target_pairs={{0,2},{2,4},{4,6},{6,0},{1,3},{3,5},{5,7},{7,1},{8,10},{10,12},{12... | collective-permute-start | bytes 774152 | tf_op jit(solution)/shard_map/ppermute | solution.py:27
  4.8 0.0 copy-done
  4.8 0.2 reshape.22.order_ref
  5.0 0.1 pad_add_fusion.place
  5.1 5.1 %shard_map.95 = (bf16[160,1024]{1,0:T(8,128)(2,1)S(1)}, bf16[160,126]{1,0:T(8,128)(2,1)S(1)}, s32[3,56,64]{2,1,0:T(8,128)S(1)}, bf16[2,4,294,147]{3,2,1,0:T(8,12...) custom-call(s32[3]{0:T(128)S(1)} %pad_add_fusion.place, ...), custom_call_target="tpu_custom_call" | custom-call | flops 50000000 | bytes 8000000 | tf_op jit(solution)/shard_map/pallas_call | solution.py:256
  10.2 2.9 %collective-permute-done.halo_ref = bf16[126,1024]{1,0:T(8,128)(2,1)S(1)} collective-permute-done((bf16[126,1024]{1,0:T(8,128)(2,1)S(1)}, bf16[126,1024]{1,0:T(8,128)(2,1)S(1)}, u32[]{:S(2)}, u32[]{:S(2)}) %collective-permute-start) | collective-permute-done | bytes 258080 | tf_op jit(solution)/shard_map/ppermute | solution.py:27
  13.1 3.6 %shard_map.96 = (bf16[147,256]{1,0:T(8,128)(2,1)S(1)}, bf16[147,256]{1,0:T(8,128)(2,1)S(1)}, bf16[147,256]{1,0:T(8,128)(2,1)S(1)}, bf16[147,512]{1,0:T(8,128)(2,...) custom-call(s32[3]{0:T(128)S(1)} %pad_add_fusion.place, ...), custom_call_target="tpu_custom_call" | custom-call | flops 2000000000 | bytes 10000000 | tf_op jit(solution)/shard_map/pallas_call | solution.py:276
  16.6 0.1 collective-permute-start.3
  16.7 2.3 %collective-permute-start.1 = (bf16[147,256]{1,0:T(8,128)(2,1)S(1)}, bf16[147,256]{1,0:T(8,128)(2,1)S(1)}, u32[]{:S(2)}, u32[]{:S(2)}) collective-permute-start(bf16[147,256]{1,0:T(8,128)(2,1)S(1)} %get-tuple-element.31), channel_id=1, source_target_pairs={{0,4},{2,6},{4,0},{6,2},{8,10},{10,8},{12,14},{14,12},{16,20},{18,... | collective-permute-start | bytes 225800 | tf_op jit(solution)/shard_map/ppermute | solution.py:61
  19.0 2.1 %collective-permute-start.2 = (bf16[147,256]{1,0:T(8,128)(2,1)S(1)}, bf16[147,256]{1,0:T(8,128)(2,1)S(1)}, u32[]{:S(2)}, u32[]{:S(2)}) collective-permute-start(bf16[147,256]{1,0:T(8,128)(2,1)S(1)} %get-tuple-element.32), channel_id=1, source_target_pairs={{0,6},{2,4},{4,2},{6,0},{8,14},{10,12},{12,10},{14,8},{16,22},{18,... | collective-permute-start | bytes 225800 | tf_op jit(solution)/shard_map/ppermute | solution.py:61
  21.1 0.0 collective-permute-start.5
  21.1 1.7 %collective-permute-start.6 = (bf16[147,256]{1,0:T(8,128)(2,1)S(1)}, bf16[147,256]{1,0:T(8,128)(2,1)S(1)}, u32[]{:S(2)}, u32[]{:S(2)}) collective-permute-start(bf16[147,256]{1,0:T(8,128)(2,1)S(1)} %get-tuple-element.36), channel_id=1, source_target_pairs={{0,6},{2,4},{4,2},{6,0},{8,14},{10,12},{12,10},{14,8},{16,22},{18,... | collective-permute-start | bytes 225800 | tf_op jit(solution)/shard_map/ppermute | solution.py:61
  22.8 0.8 %collective-permute-done.1.refs_1_ = bf16[147,256]{1,0:T(8,128)(2,1)S(1)} collective-permute-done((bf16[147,256]{1,0:T(8,128)(2,1)S(1)}, bf16[147,256]{1,0:T(8,128)(2,1)S(1)}, u32[]{:S(2)}, u32[]{:S(2)}) %collective-permute-start.1) | collective-permute-done | bytes 75296 | tf_op jit(solution)/shard_map/ppermute | solution.py:61
  23.6 3.4 %collective-permute-done.2.refs_2_ = bf16[147,256]{1,0:T(8,128)(2,1)S(1)} collective-permute-done((bf16[147,256]{1,0:T(8,128)(2,1)S(1)}, bf16[147,256]{1,0:T(8,128)(2,1)S(1)}, u32[]{:S(2)}, u32[]{:S(2)}) %collective-permute-start.2) | collective-permute-done | bytes 75296 | tf_op jit(solution)/shard_map/ppermute | solution.py:61
  27.0 0.5 %collective-permute-done.3.refs_3_.refs_0_ = bf16[147,512]{1,0:T(8,128)(2,1)S(1)} collective-permute-done((bf16[147,512]{1,0:T(8,128)(2,1)S(1)}, bf16[147,512]{1,0:T(8,128)(2,1)S(1)}, u32[]{:S(2)}, u32[]{:S(2)}) %collective-permute-start.3) | collective-permute-done | bytes 150560 | tf_op jit(solution)/shard_map/ppermute | solution.py:61
  27.5 0.3 shard_map.97
  27.8 1.6 %collective-permute-start.4 = (bf16[294,256]{1,0:T(8,128)(2,1)S(1)}, bf16[294,256]{1,0:T(8,128)(2,1)S(1)}, u32[]{:S(2)}, u32[]{:S(2)}) collective-permute-start(bf16[294,256]{1,0:T(8,128)(2,1)S(1)} %shard_map.97), channel_id=1, source_target_pairs={{0,1},{1,0},{2,3},{3,2},{4,5},{5,4},{6,7},{7,6},{8,9},{9,8},{10,11... | collective-permute-start | bytes 451592 | tf_op jit(solution)/shard_map/ppermute | solution.py:27
  29.4 1.4 %collective-permute-done.5.refs_2_ = bf16[147,256]{1,0:T(8,128)(2,1)S(1)} collective-permute-done((bf16[147,256]{1,0:T(8,128)(2,1)S(1)}, bf16[147,256]{1,0:T(8,128)(2,1)S(1)}, u32[]{:S(2)}, u32[]{:S(2)}) %collective-permute-start.5) | collective-permute-done | bytes 75296 | tf_op jit(solution)/shard_map/ppermute | solution.py:61
  30.8 0.0 collective-permute-done.6.refs_3_
  30.8 0.3 shard_map.100
  31.2 1.6 %collective-permute-start.7 = (bf16[294,256]{1,0:T(8,128)(2,1)S(1)}, bf16[294,256]{1,0:T(8,128)(2,1)S(1)}, u32[]{:S(2)}, u32[]{:S(2)}) collective-permute-start(bf16[294,256]{1,0:T(8,128)(2,1)S(1)} %shard_map.100), channel_id=1, source_target_pairs={{0,1},{1,0},{2,3},{3,2},{4,5},{5,4},{6,7},{7,6},{8,9},{9,8},{10,11... | collective-permute-start | bytes 451592 | tf_op jit(solution)/shard_map/ppermute | solution.py:27
  32.7 0.3 shard_map.99
  33.1 0.3 shard_map.98
  33.4 0.0 collective-permute-done.4
  33.4 1.1 %broadcast_select_fusion.1 = bf16[2,294,256]{2,0,1:T(2,128)(2,1)} fusion(pred[2]{0:T(512)(128)(4,1)S(1)} %iota_compare_fusion, bf16[294,256]{1,0:T(8,128)(2,1)S(1)} %shard_map.98, bf16[294,256]{1,0:T(8,128)(2,1)S(1)} %collective-permute-done.4), kind=kLoop, calls=%fused_computation.1 | loop fusion | flops 150528 | bytes 602114 | tf_op jit(solution)/shard_map/jit(_where)/select_n | solution.py:304
  34.6 1.8 %collective-permute-done.7 = bf16[294,256]{1,0:T(8,128)(2,1)S(1)} collective-permute-done((bf16[294,256]{1,0:T(8,128)(2,1)S(1)}, bf16[294,256]{1,0:T(8,128)(2,1)S(1)}, u32[]{:S(2)}, u32[]{:S(2)}) %collective-permute-start.7) | collective-permute-done | bytes 150560 | tf_op jit(solution)/shard_map/ppermute | solution.py:27
  36.4 1.1 %broadcast_select_fusion = bf16[2,294,256]{2,0,1:T(2,128)(2,1)} fusion(pred[2]{0:T(512)(128)(4,1)S(1)} %iota_compare_fusion, bf16[294,256]{1,0:T(8,128)(2,1)S(1)} %shard_map.99, bf16[294,256]{1,0:T(8,128)(2,1)S(1)} %collective-permute-done.7), kind=kLoop, calls=%fused_computation | loop fusion | flops 150528 | bytes 602114 | tf_op jit(solution)/shard_map/jit(_where)/select_n | solution.py:304
  (2 shorter events, 0.0 us)
Async XLA Ops:
  0.6 4.1 %copy-start = (s32[2,588]{1,0:T(2,128)S(1)}, s32[2,588]{1,0:T(2,128)}, u32[]{:S(2)}) copy-start(s32[2,588]{1,0:T(2,128)} %param.15) | copy-start | bytes 14116
  1.7 11.4 %collective-permute-start = (bf16[126,1024]{1,0:T(8,128)(2,1)S(1)}, bf16[126,1024]{1,0:T(8,128)(2,1)S(1)}, u32[]{:S(2)}, u32[]{:S(2)}) collective-permute-start(bf16[126,1024]{1,0:T(8,128)(2,1)S(1)} %slice_bitcast_fusion), channel_id=1, source_target_pairs={{0,2},{2,4},{4,6},{6,0},{1,3},{3,5},{5,7},{7,1},{8,10},{10,12},{12... | collective-permute-start | bytes 774152 | tf_op jit(solution)/shard_map/ppermute | solution.py:27
  16.6 10.8 %collective-permute-start.3 = (bf16[147,512]{1,0:T(8,128)(2,1)S(1)}, bf16[147,512]{1,0:T(8,128)(2,1)S(1)}, u32[]{:S(2)}, u32[]{:S(2)}) collective-permute-start(bf16[147,512]{1,0:T(8,128)(2,1)S(1)} %get-tuple-element.33), channel_id=1, source_target_pairs={{0,2},{2,0},{4,6},{6,4},{8,12},{10,14},{12,8},{14,10},{16,18},{18,... | collective-permute-start | bytes 451592 | tf_op jit(solution)/shard_map/ppermute | solution.py:61
  16.7 6.9 %collective-permute-start.1 = (bf16[147,256]{1,0:T(8,128)(2,1)S(1)}, bf16[147,256]{1,0:T(8,128)(2,1)S(1)}, u32[]{:S(2)}, u32[]{:S(2)}) collective-permute-start(bf16[147,256]{1,0:T(8,128)(2,1)S(1)} %get-tuple-element.31), channel_id=1, source_target_pairs={{0,4},{2,6},{4,0},{6,2},{8,10},{10,8},{12,14},{14,12},{16,20},{18,... | collective-permute-start | bytes 225800 | tf_op jit(solution)/shard_map/ppermute | solution.py:61
  19.0 7.9 %collective-permute-start.2 = (bf16[147,256]{1,0:T(8,128)(2,1)S(1)}, bf16[147,256]{1,0:T(8,128)(2,1)S(1)}, u32[]{:S(2)}, u32[]{:S(2)}) collective-permute-start(bf16[147,256]{1,0:T(8,128)(2,1)S(1)} %get-tuple-element.32), channel_id=1, source_target_pairs={{0,6},{2,4},{4,2},{6,0},{8,14},{10,12},{12,10},{14,8},{16,22},{18,... | collective-permute-start | bytes 225800 | tf_op jit(solution)/shard_map/ppermute | solution.py:61
  21.1 9.7 %collective-permute-start.5 = (bf16[147,256]{1,0:T(8,128)(2,1)S(1)}, bf16[147,256]{1,0:T(8,128)(2,1)S(1)}, u32[]{:S(2)}, u32[]{:S(2)}) collective-permute-start(bf16[147,256]{1,0:T(8,128)(2,1)S(1)} %get-tuple-element.35), channel_id=1, source_target_pairs={{0,4},{2,6},{4,0},{6,2},{8,10},{10,8},{12,14},{14,12},{16,20},{18,... | collective-permute-start | bytes 225800 | tf_op jit(solution)/shard_map/ppermute | solution.py:61
  21.1 9.7 %collective-permute-start.6 = (bf16[147,256]{1,0:T(8,128)(2,1)S(1)}, bf16[147,256]{1,0:T(8,128)(2,1)S(1)}, u32[]{:S(2)}, u32[]{:S(2)}) collective-permute-start(bf16[147,256]{1,0:T(8,128)(2,1)S(1)} %get-tuple-element.36), channel_id=1, source_target_pairs={{0,6},{2,4},{4,2},{6,0},{8,14},{10,12},{12,10},{14,8},{16,22},{18,... | collective-permute-start | bytes 225800 | tf_op jit(solution)/shard_map/ppermute | solution.py:61
  27.8 5.6 %collective-permute-start.4 = (bf16[294,256]{1,0:T(8,128)(2,1)S(1)}, bf16[294,256]{1,0:T(8,128)(2,1)S(1)}, u32[]{:S(2)}, u32[]{:S(2)}) collective-permute-start(bf16[294,256]{1,0:T(8,128)(2,1)S(1)} %shard_map.97), channel_id=1, source_target_pairs={{0,1},{1,0},{2,3},{3,2},{4,5},{5,4},{6,7},{7,6},{8,9},{9,8},{10,11... | collective-permute-start | bytes 451592 | tf_op jit(solution)/shard_map/ppermute | solution.py:27
  31.2 5.3 %collective-permute-start.7 = (bf16[294,256]{1,0:T(8,128)(2,1)S(1)}, bf16[294,256]{1,0:T(8,128)(2,1)S(1)}, u32[]{:S(2)}, u32[]{:S(2)}) collective-permute-start(bf16[294,256]{1,0:T(8,128)(2,1)S(1)} %shard_map.100), channel_id=1, source_target_pairs={{0,1},{1,0},{2,3},{3,2},{4,5},{5,4},{6,7},{7,6},{8,9},{9,8},{10,11... | collective-permute-start | bytes 451592 | tf_op jit(solution)/shard_map/ppermute | solution.py:27

commit v10 on v9

--- a/solution.py
+++ b/solution.py
@@ -141,7 +141,7 @@
 
 
 def encode_kernel(
-    blocks, place, rolled_ref, halo_ref, take_ref, same_ref, gain_ref, qkv_ref, out_ref, key_ref,
+    blocks, band_rows, place, rolled_ref, halo_ref, take_ref, same_ref, gain_ref, qkv_ref, out_ref, key_ref,
     value_ref, *sent
 ):
     rows = rolled_ref.shape[0]
@@ -206,22 +206,48 @@
     memory = (rolled + dot(attended, out_ref[...])).astype(jnp.bfloat16)
     n_seq = 1 + max(r for _, r in blocks)
     own_cols = key_ref.shape[1] // n_seq
+
+    def block(kind, r):
+        at = pl.multiple_of(target(place, r, n_seq) * own_cols, own_cols)
+        return dot(memory, (key_ref, value_ref)[kind][:, pl.ds(at, own_cols)])
+
+    apart = {r for kinds, r in blocks if kinds == (0,)}
+    values = {r: block(1, r) for r in apart}
     for (kinds, r), block_ref in zip(blocks, sent):
-        at = pl.multiple_of(target(place, r, n_seq) * own_cols, own_cols)
-        for i, kind in enumerate(kinds):
-            block = dot(memory, (key_ref, value_ref)[kind][:, pl.ds(at, own_cols)])
-            cols = slice(i * own_cols, (i + 1) * own_cols)
-            block_ref[:, cols] = block[: block_ref.shape[0]].astype(jnp.bfloat16)
+        count = block_ref.shape[0]
+        if kinds == (1,):
+            block_ref[...] = values[r][:count].astype(jnp.bfloat16)
+        elif kinds == (0,):
+            keys = block(0, r)
+            whole = count // 8 * 8
+            extra = count - band_rows
+            spot = lax.broadcasted_iota(jnp.int32, (8, 1), 0)
+            moved = pltpu.roll(values[r][whole : whole + 8], extra, 0)
+            tail = jnp.where(spot < band_rows - whole, keys[whole : whole + 8], moved)
+            both = jnp.concatenate([keys[:whole], tail], axis=0)
+            block_ref[...] = both[:count].astype(jnp.bfloat16)
+        else:
+            for i, kind in enumerate(kinds):
+                cols = slice(i * own_cols, (i + 1) * own_cols)
+                block_ref[:, cols] = block(kind, r)[:count].astype(jnp.bfloat16)
 
 
 def select_kernel(rounds, first, picks_ref, *refs):
-    held, outs = refs[: len(rounds)], refs[len(rounds) :]
+    outs = refs[sum(1 + rest for *_, rest in rounds) :]
+    refs = iter(refs)
+    band_rows = picks_ref.shape[-1]
+    width = outs[0].shape[1]
+    blocks = []
+    for r, at, rest in rounds:
+        block = next(refs)[:, at * width : (at + 1) * width]
+        if rest:
+            whole = block.shape[0]
+            last = next(refs)[whole:, :].astype(jnp.float32)
+            last = last[band_rows - whole :].astype(jnp.bfloat16)
+            block = jnp.concatenate([block, last], axis=0)
+        blocks.append((r, block[:band_rows]))
     for i, out in enumerate(outs):
-        width = out.shape[1]
-        terms = [
-            dot(picks_ref[first + i, r], ref[:, at * width : (at + 1) * width])
-            for (r, at), ref in zip(rounds, held)
-        ]
+        terms = [dot(picks_ref[first + i, r], block) for r, block in blocks]
         out[...] = sum(terms[1:], terms[0]).astype(jnp.bfloat16)
 
 
@@ -273,10 +299,12 @@
 
     apart = [0, *range(2, n_seq)]
     blocks = [((0,), r) for r in apart] + [((0, 1), 1)] + [((1,), r) for r in apart]
+    whole = band_rows // 16 * 16
+    counts = {(0,): 2 * band_rows - whole, (0, 1): band_rows, (1,): whole}
     sent = call(
-        functools.partial(encode_kernel, blocks),
+        functools.partial(encode_kernel, blocks, band_rows),
         [
-            jax.ShapeDtypeStruct((band_rows, len(kinds) * own_cols), jnp.bfloat16)
+            jax.ShapeDtypeStruct((counts[kinds], len(kinds) * own_cols), jnp.bfloat16)
             for kinds, _ in blocks
         ],
         1, 9, 2_000_000_000, 10_000_000,
@@ -284,12 +312,17 @@
     held = [exchanged(b, r) if r else b for (_, r), b in zip(blocks, sent)]
 
     def selected(kind, first, count):
-        mine = [(r, kinds.index(kind), b) for (kinds, r), b in zip(blocks, held) if kind in kinds]
+        mine, operands = [], []
+        for (kinds, r), b in zip(blocks, held):
+            if kind in kinds:
+                rest = kinds == (1,)
+                mine.append((r, kinds.index(kind), int(rest)))
+                operands += [b, held[blocks.index(((0,), r))]] if rest else [b]
         return call(
-            functools.partial(select_kernel, [(r, at) for r, at, _ in mine], first),
+            functools.partial(select_kernel, mine, first),
             [jax.ShapeDtypeStruct((pos, own_cols), jnp.bfloat16)] * count,
-            0, 1 + n_seq, 300_000_000, 1_000_000,
-        )(picks, *(b for *_, b in mine))
+            0, 1 + len(operands), 300_000_000, 1_000_000,
+        )(picks, *operands)
 
     def gathered(group):
         away = selected(group, 1, n_tensor - 1)

time: 37.7 us -> 37.5 us (level)
  transfers between devices with their start and end apart: 8 -> 8, of which waited for: 6 -> 7; matrix products, arithmetic and copies ran while one was open for 4% -> 4% of each run, Pallas kernels for 17% -> 17%
where the time goes in v10:
time: 37.5 us; the launch traced here: 37.3 us
  starting transfers between devices  12.4 us (33%)
  waiting for transfers between devices  10.7 us (29%)
  Pallas kernels  9.89 us (26%)
  other arithmetic  2.38 us (6%)
  local copies, waits for them, and re-layouts  1.25 us (3%)
  between operations  0.71 us (2%)
    ppermute x3, starting transfers between devices, rotated(): lax.ppermute(block, axis, [(i, (i + distance) % devices) for i in range(d...  6.24 us
    ppermute x5, starting transfers between devices, exchanged(): return lax.ppermute(block, ('dp', 'seq'), pairs)  6.18 us
    ppermute x5, waiting for transfers between devices, exchanged(): return lax.ppermute(block, ('dp', 'seq'), pairs)  5.88 us
    pallas_call x1, Pallas kernels, local(): call(stage_kernel, [jax.ShapeDtypeStruct((rows, emb), jnp.bfloat16), jax....  5.09 us
    ppermute x3, waiting for transfers between devices, rotated(): lax.ppermute(block, axis, [(i, (i + distance) % devices) for i in range(d...  4.8 us
    pallas_call x1, Pallas kernels, local(): call(functools.partial(encode_kernel, blocks, band_rows), [jax.ShapeDtype...  3.55 us
    select_n x2, other arithmetic, by_page(): result = jnp.where(came, blocks[d][None], result)  2.29 us
    pallas_call x4, Pallas kernels, selected(): call(functools.partial(select_kernel, mine, first), [jax.ShapeDtypeStruct...  1.25 us
  transfers between devices with their start and end apart: 8, of which 7 were waited for; matrix products, arithmetic and copies ran while one was open for 4% of the time, Pallas kernels for 17%

profile of v10, /device:TPU:0, one launch (start us, length us, event | category | flops | bytes accessed | tf_op | source)
XLA Modules:
  0.0 37.3 jit_solution(16123601656242145299)
XLA Ops:
  0.6 0.0 copy-start
  0.6 1.0 %slice_bitcast_fusion = bf16[126,1024]{1,0:T(8,128)(2,1)S(1)} fusion(bf16[1,147,1024]{2,1,0:T(8,128)(2,1)} %pages_hbm.1), kind=kLoop, calls=%fused_computation.2 | loop fusion | bytes 516096 | tf_op jit(solution)/shard_map/squeeze | solution.py:276
  1.7 3.1 %collective-permute-start = (bf16[126,1024]{1,0:T(8,128)(2,1)S(1)}, bf16[126,1024]{1,0:T(8,128)(2,1)S(1)}, u32[]{:S(2)}, u32[]{:S(2)}) collective-permute-start(bf16[126,1024]{1,0:T(8,128)(2,1)S(1)} %slice_bitcast_fusion), channel_id=1, source_target_pairs={{0,2},{2,4},{4,6},{6,0},{1,3},{3,5},{5,7},{7,1},{8,10},{10,12},{12... | collective-permute-start | bytes 774152 | tf_op jit(solution)/shard_map/ppermute | solution.py:27
  4.8 0.0 copy-done
  4.8 0.2 reshape.22.order_ref
  5.0 0.1 pad_add_fusion.place
  5.1 5.1 %shard_map.95 = (bf16[160,1024]{1,0:T(8,128)(2,1)S(1)}, bf16[160,126]{1,0:T(8,128)(2,1)S(1)}, s32[3,56,64]{2,1,0:T(8,128)S(1)}, bf16[2,4,294,147]{3,2,1,0:T(8,12...) custom-call(s32[3]{0:T(128)S(1)} %pad_add_fusion.place, ...), custom_call_target="tpu_custom_call" | custom-call | flops 50000000 | bytes 8000000 | tf_op jit(solution)/shard_map/pallas_call | solution.py:282
  10.2 2.9 %collective-permute-done.halo_ref = bf16[126,1024]{1,0:T(8,128)(2,1)S(1)} collective-permute-done((bf16[126,1024]{1,0:T(8,128)(2,1)S(1)}, bf16[126,1024]{1,0:T(8,128)(2,1)S(1)}, u32[]{:S(2)}, u32[]{:S(2)}) %collective-permute-start) | collective-permute-done | bytes 258080 | tf_op jit(solution)/shard_map/ppermute | solution.py:27
  13.1 3.5 %shard_map.96 = (bf16[150,256]{1,0:T(8,128)(2,1)S(1)}, bf16[150,256]{1,0:T(8,128)(2,1)S(1)}, bf16[150,256]{1,0:T(8,128)(2,1)S(1)}, bf16[147,512]{1,0:T(8,128)(2,...) custom-call(s32[3]{0:T(128)S(1)} %pad_add_fusion.place, ...), custom_call_target="tpu_custom_call" | custom-call | flops 2000000000 | bytes 10000000 | tf_op jit(solution)/shard_map/pallas_call | solution.py:304
  16.6 0.1 collective-permute-start.3
  16.7 2.3 %collective-permute-start.1 = (bf16[150,256]{1,0:T(8,128)(2,1)S(1)}, bf16[150,256]{1,0:T(8,128)(2,1)S(1)}, u32[]{:S(2)}, u32[]{:S(2)}) collective-permute-start(bf16[150,256]{1,0:T(8,128)(2,1)S(1)} %get-tuple-element.31), channel_id=1, source_target_pairs={{0,4},{2,6},{4,0},{6,2},{8,10},{10,8},{12,14},{14,12},{16,20},{18,... | collective-permute-start | bytes 230408 | tf_op jit(solution)/shard_map/ppermute | solution.py:61
  19.0 2.1 %collective-permute-start.2 = (bf16[150,256]{1,0:T(8,128)(2,1)S(1)}, bf16[150,256]{1,0:T(8,128)(2,1)S(1)}, u32[]{:S(2)}, u32[]{:S(2)}) collective-permute-start(bf16[150,256]{1,0:T(8,128)(2,1)S(1)} %get-tuple-element.32), channel_id=1, source_target_pairs={{0,6},{2,4},{4,2},{6,0},{8,14},{10,12},{12,10},{14,8},{16,22},{18,... | collective-permute-start | bytes 230408 | tf_op jit(solution)/shard_map/ppermute | solution.py:61
  21.1 0.0 collective-permute-start.5
  21.1 1.7 %collective-permute-start.6 = (bf16[144,256]{1,0:T(8,128)(2,1)S(1)}, bf16[144,256]{1,0:T(8,128)(2,1)S(1)}, u32[]{:S(2)}, u32[]{:S(2)}) collective-permute-start(bf16[144,256]{1,0:T(8,128)(2,1)S(1)} %get-tuple-element.36), channel_id=1, source_target_pairs={{0,6},{2,4},{4,2},{6,0},{8,14},{10,12},{12,10},{14,8},{16,22},{18,... | collective-permute-start | bytes 221192 | tf_op jit(solution)/shard_map/ppermute | solution.py:61
  22.8 0.8 %collective-permute-done.1.refs_1_.refs_4_ = bf16[150,256]{1,0:T(8,128)(2,1)S(1)} collective-permute-done((bf16[150,256]{1,0:T(8,128)(2,1)S(1)}, bf16[150,256]{1,0:T(8,128)(2,1)S(1)}, u32[]{:S(2)}, u32[]{:S(2)}) %collective-permute-start.1) | collective-permute-done | bytes 76832 | tf_op jit(solution)/shard_map/ppermute | solution.py:61
  23.6 3.4 %collective-permute-done.2.refs_2_.refs_6_ = bf16[150,256]{1,0:T(8,128)(2,1)S(1)} collective-permute-done((bf16[150,256]{1,0:T(8,128)(2,1)S(1)}, bf16[150,256]{1,0:T(8,128)(2,1)S(1)}, u32[]{:S(2)}, u32[]{:S(2)}) %collective-permute-start.2) | collective-permute-done | bytes 76832 | tf_op jit(solution)/shard_map/ppermute | solution.py:61
  27.0 0.4 %collective-permute-done.3.refs_3_.refs_0_ = bf16[147,512]{1,0:T(8,128)(2,1)S(1)} collective-permute-done((bf16[147,512]{1,0:T(8,128)(2,1)S(1)}, bf16[147,512]{1,0:T(8,128)(2,1)S(1)}, u32[]{:S(2)}, u32[]{:S(2)}) %collective-permute-start.3) | collective-permute-done | bytes 150560 | tf_op jit(solution)/shard_map/ppermute | solution.py:61
  27.4 0.3 shard_map.97
  27.7 1.6 %collective-permute-start.4 = (bf16[294,256]{1,0:T(8,128)(2,1)S(1)}, bf16[294,256]{1,0:T(8,128)(2,1)S(1)}, u32[]{:S(2)}, u32[]{:S(2)}) collective-permute-start(bf16[294,256]{1,0:T(8,128)(2,1)S(1)} %shard_map.97), channel_id=1, source_target_pairs={{0,1},{1,0},{2,3},{3,2},{4,5},{5,4},{6,7},{7,6},{8,9},{9,8},{10,11... | collective-permute-start | bytes 451592 | tf_op jit(solution)/shard_map/ppermute | solution.py:27
  29.3 1.3 %collective-permute-done.5.refs_3_ = bf16[144,256]{1,0:T(8,128)(2,1)S(1)} collective-permute-done((bf16[144,256]{1,0:T(8,128)(2,1)S(1)}, bf16[144,256]{1,0:T(8,128)(2,1)S(1)}, u32[]{:S(2)}, u32[]{:S(2)}) %collective-permute-start.5) | collective-permute-done | bytes 73760 | tf_op jit(solution)/shard_map/ppermute | solution.py:61
  30.6 0.0 collective-permute-done.6.refs_5_
  30.6 0.3 shard_map.100
  30.9 1.6 %collective-permute-start.7 = (bf16[294,256]{1,0:T(8,128)(2,1)S(1)}, bf16[294,256]{1,0:T(8,128)(2,1)S(1)}, u32[]{:S(2)}, u32[]{:S(2)}) collective-permute-start(bf16[294,256]{1,0:T(8,128)(2,1)S(1)} %shard_map.100), channel_id=1, source_target_pairs={{0,1},{1,0},{2,3},{3,2},{4,5},{5,4},{6,7},{7,6},{8,9},{9,8},{10,11... | collective-permute-start | bytes 451592 | tf_op jit(solution)/shard_map/ppermute | solution.py:27
  32.5 0.3 shard_map.99
  32.9 0.3 shard_map.98
  33.2 0.1 collective-permute-done.4
  33.3 1.1 %broadcast_select_fusion.1 = bf16[2,294,256]{2,0,1:T(2,128)(2,1)} fusion(pred[2]{0:T(512)(128)(4,1)S(1)} %iota_compare_fusion, bf16[294,256]{1,0:T(8,128)(2,1)S(1)} %shard_map.98, bf16[294,256]{1,0:T(8,128)(2,1)S(1)} %collective-permute-done.4), kind=kLoop, calls=%fused_computation.1 | loop fusion | flops 150528 | bytes 602114 | tf_op jit(solution)/shard_map/jit(_where)/select_n | solution.py:337
  34.4 1.8 %collective-permute-done.7 = bf16[294,256]{1,0:T(8,128)(2,1)S(1)} collective-permute-done((bf16[294,256]{1,0:T(8,128)(2,1)S(1)}, bf16[294,256]{1,0:T(8,128)(2,1)S(1)}, u32[]{:S(2)}, u32[]{:S(2)}) %collective-permute-start.7) | collective-permute-done | bytes 150560 | tf_op jit(solution)/shard_map/ppermute | solution.py:27
  36.2 1.1 %broadcast_select_fusion = bf16[2,294,256]{2,0,1:T(2,128)(2,1)} fusion(pred[2]{0:T(512)(128)(4,1)S(1)} %iota_compare_fusion, bf16[294,256]{1,0:T(8,128)(2,1)S(1)} %shard_map.99, bf16[294,256]{1,0:T(8,128)(2,1)S(1)} %collective-permute-done.7), kind=kLoop, calls=%fused_computation | loop fusion | flops 150528 | bytes 602114 | tf_op jit(solution)/shard_map/jit(_where)/select_n | solution.py:337
  (2 shorter events, 0.0 us)
Async XLA Ops:
  0.6 4.1 %copy-start = (s32[2,588]{1,0:T(2,128)S(1)}, s32[2,588]{1,0:T(2,128)}, u32[]{:S(2)}) copy-start(s32[2,588]{1,0:T(2,128)} %param.15) | copy-start | bytes 14116
  1.7 11.4 %collective-permute-start = (bf16[126,1024]{1,0:T(8,128)(2,1)S(1)}, bf16[126,1024]{1,0:T(8,128)(2,1)S(1)}, u32[]{:S(2)}, u32[]{:S(2)}) collective-permute-start(bf16[126,1024]{1,0:T(8,128)(2,1)S(1)} %slice_bitcast_fusion), channel_id=1, source_target_pairs={{0,2},{2,4},{4,6},{6,0},{1,3},{3,5},{5,7},{7,1},{8,10},{10,12},{12... | collective-permute-start | bytes 774152 | tf_op jit(solution)/shard_map/ppermute | solution.py:27
  16.6 10.8 %collective-permute-start.3 = (bf16[147,512]{1,0:T(8,128)(2,1)S(1)}, bf16[147,512]{1,0:T(8,128)(2,1)S(1)}, u32[]{:S(2)}, u32[]{:S(2)}) collective-permute-start(bf16[147,512]{1,0:T(8,128)(2,1)S(1)} %get-tuple-element.33), channel_id=1, source_target_pairs={{0,2},{2,0},{4,6},{6,4},{8,12},{10,14},{12,8},{14,10},{16,18},{18,... | collective-permute-start | bytes 451592 | tf_op jit(solution)/shard_map/ppermute | solution.py:61
  16.7 6.9 %collective-permute-start.1 = (bf16[150,256]{1,0:T(8,128)(2,1)S(1)}, bf16[150,256]{1,0:T(8,128)(2,1)S(1)}, u32[]{:S(2)}, u32[]{:S(2)}) collective-permute-start(bf16[150,256]{1,0:T(8,128)(2,1)S(1)} %get-tuple-element.31), channel_id=1, source_target_pairs={{0,4},{2,6},{4,0},{6,2},{8,10},{10,8},{12,14},{14,12},{16,20},{18,... | collective-permute-start | bytes 230408 | tf_op jit(solution)/shard_map/ppermute | solution.py:61
  19.0 8.0 %collective-permute-start.2 = (bf16[150,256]{1,0:T(8,128)(2,1)S(1)}, bf16[150,256]{1,0:T(8,128)(2,1)S(1)}, u32[]{:S(2)}, u32[]{:S(2)}) collective-permute-start(bf16[150,256]{1,0:T(8,128)(2,1)S(1)} %get-tuple-element.32), channel_id=1, source_target_pairs={{0,6},{2,4},{4,2},{6,0},{8,14},{10,12},{12,10},{14,8},{16,22},{18,... | collective-permute-start | bytes 230408 | tf_op jit(solution)/shard_map/ppermute | solution.py:61
  21.1 9.5 %collective-permute-start.5 = (bf16[144,256]{1,0:T(8,128)(2,1)S(1)}, bf16[144,256]{1,0:T(8,128)(2,1)S(1)}, u32[]{:S(2)}, u32[]{:S(2)}) collective-permute-start(bf16[144,256]{1,0:T(8,128)(2,1)S(1)} %get-tuple-element.35), channel_id=1, source_target_pairs={{0,4},{2,6},{4,0},{6,2},{8,10},{10,8},{12,14},{14,12},{16,20},{18,... | collective-permute-start | bytes 221192 | tf_op jit(solution)/shard_map/ppermute | solution.py:61
  21.1 9.5 %collective-permute-start.6 = (bf16[144,256]{1,0:T(8,128)(2,1)S(1)}, bf16[144,256]{1,0:T(8,128)(2,1)S(1)}, u32[]{:S(2)}, u32[]{:S(2)}) collective-permute-start(bf16[144,256]{1,0:T(8,128)(2,1)S(1)} %get-tuple-element.36), channel_id=1, source_target_pairs={{0,6},{2,4},{4,2},{6,0},{8,14},{10,12},{12,10},{14,8},{16,22},{18,... | collective-permute-start | bytes 221192 | tf_op jit(solution)/shard_map/ppermute | solution.py:61
  27.7 5.5 %collective-permute-start.4 = (bf16[294,256]{1,0:T(8,128)(2,1)S(1)}, bf16[294,256]{1,0:T(8,128)(2,1)S(1)}, u32[]{:S(2)}, u32[]{:S(2)}) collective-permute-start(bf16[294,256]{1,0:T(8,128)(2,1)S(1)} %shard_map.97), channel_id=1, source_target_pairs={{0,1},{1,0},{2,3},{3,2},{4,5},{5,4},{6,7},{7,6},{8,9},{9,8},{10,11... | collective-permute-start | bytes 451592 | tf_op jit(solution)/shard_map/ppermute | solution.py:27
  30.9 5.3 %collective-permute-start.7 = (bf16[294,256]{1,0:T(8,128)(2,1)S(1)}, bf16[294,256]{1,0:T(8,128)(2,1)S(1)}, u32[]{:S(2)}, u32[]{:S(2)}) collective-permute-start(bf16[294,256]{1,0:T(8,128)(2,1)S(1)} %shard_map.100), channel_id=1, source_target_pairs={{0,1},{1,0},{2,3},{3,2},{4,5},{5,4},{6,7},{7,6},{8,9},{9,8},{10,11... | collective-permute-start | bytes 451592 | tf_op jit(solution)/shard_map/ppermute | solution.py:27

commit v11 on v10

--- a/solution.py
+++ b/solution.py
@@ -13,7 +13,7 @@
 GRID_W = 21
 WIN = 7
 
-GROUP = 8
+GROUP = 4
 SLAB = (56, 64)
 VMEM_LIMIT = 24 * 1024 * 1024
 
@@ -180,10 +180,10 @@
         score = jnp.where(same, score * HEAD_DIM ** (-0.5), -1000000000.0)
         score = jnp.exp(score - jnp.max(score, axis=-1, keepdims=True))
         total = jnp.sum(score, axis=-1, keepdims=True)
-        weights.append((score * (1.0 / total)).astype(jnp.bfloat16))
+        weights.append((score.astype(jnp.bfloat16), 1.0 / total))
     parts = [[] for _ in range(HEADS // GROUP)]
     for (w, g), weight in zip(units, weights):
-        mixed = dot(weight, taken(w, g, 2, keys))
+        mixed = dot(weight[0], taken(w, g, 2, keys)) * weight[1]
         mine = mixed[:queries]
         for h in range(1, GROUP):
             mine = jnp.where(lane_head == h, mixed[h * queries : (h + 1) * queries], mine)

time: 37.5 us -> 37.4 us (level)
  no operation moved by 1% of the time
where the time goes in v11:
time: 37.4 us; the launch traced here: 37.2 us
  starting transfers between devices  12.4 us (33%)
  waiting for transfers between devices  10.7 us (29%)
  Pallas kernels  9.75 us (26%)
  other arithmetic  2.38 us (6%)
  local copies, waits for them, and re-layouts  1.25 us (3%)
  between operations  0.71 us (2%)
    ppermute x3, starting transfers between devices, rotated(): lax.ppermute(block, axis, [(i, (i + distance) % devices) for i in range(d...  6.24 us
    ppermute x5, starting transfers between devices, exchanged(): return lax.ppermute(block, ('dp', 'seq'), pairs)  6.18 us
    ppermute x5, waiting for transfers between devices, exchanged(): return lax.ppermute(block, ('dp', 'seq'), pairs)  5.89 us
    pallas_call x1, Pallas kernels, local(): call(stage_kernel, [jax.ShapeDtypeStruct((rows, emb), jnp.bfloat16), jax....  5.09 us
    ppermute x3, waiting for transfers between devices, rotated(): lax.ppermute(block, axis, [(i, (i + distance) % devices) for i in range(d...  4.8 us
    pallas_call x1, Pallas kernels, local(): call(functools.partial(encode_kernel, blocks, band_rows), [jax.ShapeDtype...  3.41 us
    select_n x2, other arithmetic, by_page(): result = jnp.where(came, blocks[d][None], result)  2.29 us
    pallas_call x4, Pallas kernels, selected(): call(functools.partial(select_kernel, mine, first), [jax.ShapeDtypeStruct...  1.25 us
  transfers between devices with their start and end apart: 8, of which 7 were waited for; matrix products, arithmetic and copies ran while one was open for 4% of the time, Pallas kernels for 17%

profile of v11, /device:TPU:0, one launch (start us, length us, event | category | flops | bytes accessed | tf_op | source)
XLA Modules:
  0.0 37.2 jit_solution(13400798191790948402)
XLA Ops:
  0.6 0.0 copy-start
  0.6 1.0 %slice_bitcast_fusion = bf16[126,1024]{1,0:T(8,128)(2,1)S(1)} fusion(bf16[1,147,1024]{2,1,0:T(8,128)(2,1)} %pages_hbm.1), kind=kLoop, calls=%fused_computation.2 | loop fusion | bytes 516096 | tf_op jit(solution)/shard_map/squeeze | solution.py:276
  1.7 3.1 %collective-permute-start = (bf16[126,1024]{1,0:T(8,128)(2,1)S(1)}, bf16[126,1024]{1,0:T(8,128)(2,1)S(1)}, u32[]{:S(2)}, u32[]{:S(2)}) collective-permute-start(bf16[126,1024]{1,0:T(8,128)(2,1)S(1)} %slice_bitcast_fusion), channel_id=1, source_target_pairs={{0,2},{2,4},{4,6},{6,0},{1,3},{3,5},{5,7},{7,1},{8,10},{10,12},{12... | collective-permute-start | bytes 774152 | tf_op jit(solution)/shard_map/ppermute | solution.py:27
  4.8 0.0 copy-done
  4.8 0.2 reshape.22.order_ref
  5.0 0.1 pad_add_fusion.place
  5.1 5.1 %shard_map.95 = (bf16[160,1024]{1,0:T(8,128)(2,1)S(1)}, bf16[160,126]{1,0:T(8,128)(2,1)S(1)}, s32[3,56,64]{2,1,0:T(8,128)S(1)}, bf16[2,4,294,147]{3,2,1,0:T(8,12...) custom-call(s32[3]{0:T(128)S(1)} %pad_add_fusion.place, ...), custom_call_target="tpu_custom_call" | custom-call | flops 50000000 | bytes 8000000 | tf_op jit(solution)/shard_map/pallas_call | solution.py:282
  10.2 2.9 %collective-permute-done.halo_ref = bf16[126,1024]{1,0:T(8,128)(2,1)S(1)} collective-permute-done((bf16[126,1024]{1,0:T(8,128)(2,1)S(1)}, bf16[126,1024]{1,0:T(8,128)(2,1)S(1)}, u32[]{:S(2)}, u32[]{:S(2)}) %collective-permute-start) | collective-permute-done | bytes 258080 | tf_op jit(solution)/shard_map/ppermute | solution.py:27
  13.1 3.4 %shard_map.96 = (bf16[150,256]{1,0:T(8,128)(2,1)S(1)}, bf16[150,256]{1,0:T(8,128)(2,1)S(1)}, bf16[150,256]{1,0:T(8,128)(2,1)S(1)}, bf16[147,512]{1,0:T(8,128)(2,...) custom-call(s32[3]{0:T(128)S(1)} %pad_add_fusion.place, ...), custom_call_target="tpu_custom_call" | custom-call | flops 2000000000 | bytes 10000000 | tf_op jit(solution)/shard_map/pallas_call | solution.py:304
  16.5 0.1 collective-permute-start.3
  16.6 2.3 %collective-permute-start.1 = (bf16[150,256]{1,0:T(8,128)(2,1)S(1)}, bf16[150,256]{1,0:T(8,128)(2,1)S(1)}, u32[]{:S(2)}, u32[]{:S(2)}) collective-permute-start(bf16[150,256]{1,0:T(8,128)(2,1)S(1)} %get-tuple-element.31), channel_id=1, source_target_pairs={{0,4},{2,6},{4,0},{6,2},{8,10},{10,8},{12,14},{14,12},{16,20},{18,... | collective-permute-start | bytes 230408 | tf_op jit(solution)/shard_map/ppermute | solution.py:61
  18.9 2.1 %collective-permute-start.2 = (bf16[150,256]{1,0:T(8,128)(2,1)S(1)}, bf16[150,256]{1,0:T(8,128)(2,1)S(1)}, u32[]{:S(2)}, u32[]{:S(2)}) collective-permute-start(bf16[150,256]{1,0:T(8,128)(2,1)S(1)} %get-tuple-element.32), channel_id=1, source_target_pairs={{0,6},{2,4},{4,2},{6,0},{8,14},{10,12},{12,10},{14,8},{16,22},{18,... | collective-permute-start | bytes 230408 | tf_op jit(solution)/shard_map/ppermute | solution.py:61
  21.0 0.0 collective-permute-start.5
  21.0 1.7 %collective-permute-start.6 = (bf16[144,256]{1,0:T(8,128)(2,1)S(1)}, bf16[144,256]{1,0:T(8,128)(2,1)S(1)}, u32[]{:S(2)}, u32[]{:S(2)}) collective-permute-start(bf16[144,256]{1,0:T(8,128)(2,1)S(1)} %get-tuple-element.36), channel_id=1, source_target_pairs={{0,6},{2,4},{4,2},{6,0},{8,14},{10,12},{12,10},{14,8},{16,22},{18,... | collective-permute-start | bytes 221192 | tf_op jit(solution)/shard_map/ppermute | solution.py:61
  22.7 0.8 %collective-permute-done.1.refs_1_.refs_4_ = bf16[150,256]{1,0:T(8,128)(2,1)S(1)} collective-permute-done((bf16[150,256]{1,0:T(8,128)(2,1)S(1)}, bf16[150,256]{1,0:T(8,128)(2,1)S(1)}, u32[]{:S(2)}, u32[]{:S(2)}) %collective-permute-start.1) | collective-permute-done | bytes 76832 | tf_op jit(solution)/shard_map/ppermute | solution.py:61
  23.5 3.4 %collective-permute-done.2.refs_2_.refs_6_ = bf16[150,256]{1,0:T(8,128)(2,1)S(1)} collective-permute-done((bf16[150,256]{1,0:T(8,128)(2,1)S(1)}, bf16[150,256]{1,0:T(8,128)(2,1)S(1)}, u32[]{:S(2)}, u32[]{:S(2)}) %collective-permute-start.2) | collective-permute-done | bytes 76832 | tf_op jit(solution)/shard_map/ppermute | solution.py:61
  26.9 0.4 %collective-permute-done.3.refs_3_.refs_0_ = bf16[147,512]{1,0:T(8,128)(2,1)S(1)} collective-permute-done((bf16[147,512]{1,0:T(8,128)(2,1)S(1)}, bf16[147,512]{1,0:T(8,128)(2,1)S(1)}, u32[]{:S(2)}, u32[]{:S(2)}) %collective-permute-start.3) | collective-permute-done | bytes 150560 | tf_op jit(solution)/shard_map/ppermute | solution.py:61
  27.3 0.3 shard_map.97
  27.6 1.6 %collective-permute-start.4 = (bf16[294,256]{1,0:T(8,128)(2,1)S(1)}, bf16[294,256]{1,0:T(8,128)(2,1)S(1)}, u32[]{:S(2)}, u32[]{:S(2)}) collective-permute-start(bf16[294,256]{1,0:T(8,128)(2,1)S(1)} %shard_map.97), channel_id=1, source_target_pairs={{0,1},{1,0},{2,3},{3,2},{4,5},{5,4},{6,7},{7,6},{8,9},{9,8},{10,11... | collective-permute-start | bytes 451592 | tf_op jit(solution)/shard_map/ppermute | solution.py:27
  29.2 1.3 %collective-permute-done.5.refs_3_ = bf16[144,256]{1,0:T(8,128)(2,1)S(1)} collective-permute-done((bf16[144,256]{1,0:T(8,128)(2,1)S(1)}, bf16[144,256]{1,0:T(8,128)(2,1)S(1)}, u32[]{:S(2)}, u32[]{:S(2)}) %collective-permute-start.5) | collective-permute-done | bytes 73760 | tf_op jit(solution)/shard_map/ppermute | solution.py:61
  30.5 0.0 collective-permute-done.6.refs_5_
  30.5 0.3 shard_map.100
  30.8 1.6 %collective-permute-start.7 = (bf16[294,256]{1,0:T(8,128)(2,1)S(1)}, bf16[294,256]{1,0:T(8,128)(2,1)S(1)}, u32[]{:S(2)}, u32[]{:S(2)}) collective-permute-start(bf16[294,256]{1,0:T(8,128)(2,1)S(1)} %shard_map.100), channel_id=1, source_target_pairs={{0,1},{1,0},{2,3},{3,2},{4,5},{5,4},{6,7},{7,6},{8,9},{9,8},{10,11... | collective-permute-start | bytes 451592 | tf_op jit(solution)/shard_map/ppermute | solution.py:27
  32.4 0.3 shard_map.99
  32.7 0.3 shard_map.98
  33.0 0.1 collective-permute-done.4
  33.1 1.1 %broadcast_select_fusion.1 = bf16[2,294,256]{2,0,1:T(2,128)(2,1)} fusion(pred[2]{0:T(512)(128)(4,1)S(1)} %iota_compare_fusion, bf16[294,256]{1,0:T(8,128)(2,1)S(1)} %shard_map.98, bf16[294,256]{1,0:T(8,128)(2,1)S(1)} %collective-permute-done.4), kind=kLoop, calls=%fused_computation.1 | loop fusion | flops 150528 | bytes 602114 | tf_op jit(solution)/shard_map/jit(_where)/select_n | solution.py:337
  34.3 1.8 %collective-permute-done.7 = bf16[294,256]{1,0:T(8,128)(2,1)S(1)} collective-permute-done((bf16[294,256]{1,0:T(8,128)(2,1)S(1)}, bf16[294,256]{1,0:T(8,128)(2,1)S(1)}, u32[]{:S(2)}, u32[]{:S(2)}) %collective-permute-start.7) | collective-permute-done | bytes 150560 | tf_op jit(solution)/shard_map/ppermute | solution.py:27
  36.1 1.1 %broadcast_select_fusion = bf16[2,294,256]{2,0,1:T(2,128)(2,1)} fusion(pred[2]{0:T(512)(128)(4,1)S(1)} %iota_compare_fusion, bf16[294,256]{1,0:T(8,128)(2,1)S(1)} %shard_map.99, bf16[294,256]{1,0:T(8,128)(2,1)S(1)} %collective-permute-done.7), kind=kLoop, calls=%fused_computation | loop fusion | flops 150528 | bytes 602114 | tf_op jit(solution)/shard_map/jit(_where)/select_n | solution.py:337
  (2 shorter events, 0.0 us)
Async XLA Ops:
  0.6 4.1 %copy-start = (s32[2,588]{1,0:T(2,128)S(1)}, s32[2,588]{1,0:T(2,128)}, u32[]{:S(2)}) copy-start(s32[2,588]{1,0:T(2,128)} %param.15) | copy-start | bytes 14116
  1.7 11.4 %collective-permute-start = (bf16[126,1024]{1,0:T(8,128)(2,1)S(1)}, bf16[126,1024]{1,0:T(8,128)(2,1)S(1)}, u32[]{:S(2)}, u32[]{:S(2)}) collective-permute-start(bf16[126,1024]{1,0:T(8,128)(2,1)S(1)} %slice_bitcast_fusion), channel_id=1, source_target_pairs={{0,2},{2,4},{4,6},{6,0},{1,3},{3,5},{5,7},{7,1},{8,10},{10,12},{12... | collective-permute-start | bytes 774152 | tf_op jit(solution)/shard_map/ppermute | solution.py:27
  16.5 10.8 %collective-permute-start.3 = (bf16[147,512]{1,0:T(8,128)(2,1)S(1)}, bf16[147,512]{1,0:T(8,128)(2,1)S(1)}, u32[]{:S(2)}, u32[]{:S(2)}) collective-permute-start(bf16[147,512]{1,0:T(8,128)(2,1)S(1)} %get-tuple-element.33), channel_id=1, source_target_pairs={{0,2},{2,0},{4,6},{6,4},{8,12},{10,14},{12,8},{14,10},{16,18},{18,... | collective-permute-start | bytes 451592 | tf_op jit(solution)/shard_map/ppermute | solution.py:61
  16.6 6.9 %collective-permute-start.1 = (bf16[150,256]{1,0:T(8,128)(2,1)S(1)}, bf16[150,256]{1,0:T(8,128)(2,1)S(1)}, u32[]{:S(2)}, u32[]{:S(2)}) collective-permute-start(bf16[150,256]{1,0:T(8,128)(2,1)S(1)} %get-tuple-element.31), channel_id=1, source_target_pairs={{0,4},{2,6},{4,0},{6,2},{8,10},{10,8},{12,14},{14,12},{16,20},{18,... | collective-permute-start | bytes 230408 | tf_op jit(solution)/shard_map/ppermute | solution.py:61
  18.9 8.0 %collective-permute-start.2 = (bf16[150,256]{1,0:T(8,128)(2,1)S(1)}, bf16[150,256]{1,0:T(8,128)(2,1)S(1)}, u32[]{:S(2)}, u32[]{:S(2)}) collective-permute-start(bf16[150,256]{1,0:T(8,128)(2,1)S(1)} %get-tuple-element.32), channel_id=1, source_target_pairs={{0,6},{2,4},{4,2},{6,0},{8,14},{10,12},{12,10},{14,8},{16,22},{18,... | collective-permute-start | bytes 230408 | tf_op jit(solution)/shard_map/ppermute | solution.py:61
  21.0 9.5 %collective-permute-start.5 = (bf16[144,256]{1,0:T(8,128)(2,1)S(1)}, bf16[144,256]{1,0:T(8,128)(2,1)S(1)}, u32[]{:S(2)}, u32[]{:S(2)}) collective-permute-start(bf16[144,256]{1,0:T(8,128)(2,1)S(1)} %get-tuple-element.35), channel_id=1, source_target_pairs={{0,4},{2,6},{4,0},{6,2},{8,10},{10,8},{12,14},{14,12},{16,20},{18,... | collective-permute-start | bytes 221192 | tf_op jit(solution)/shard_map/ppermute | solution.py:61
  21.0 9.5 %collective-permute-start.6 = (bf16[144,256]{1,0:T(8,128)(2,1)S(1)}, bf16[144,256]{1,0:T(8,128)(2,1)S(1)}, u32[]{:S(2)}, u32[]{:S(2)}) collective-permute-start(bf16[144,256]{1,0:T(8,128)(2,1)S(1)} %get-tuple-element.36), channel_id=1, source_target_pairs={{0,6},{2,4},{4,2},{6,0},{8,14},{10,12},{12,10},{14,8},{16,22},{18,... | collective-permute-start | bytes 221192 | tf_op jit(solution)/shard_map/ppermute | solution.py:61
  27.6 5.5 %collective-permute-start.4 = (bf16[294,256]{1,0:T(8,128)(2,1)S(1)}, bf16[294,256]{1,0:T(8,128)(2,1)S(1)}, u32[]{:S(2)}, u32[]{:S(2)}) collective-permute-start(bf16[294,256]{1,0:T(8,128)(2,1)S(1)} %shard_map.97), channel_id=1, source_target_pairs={{0,1},{1,0},{2,3},{3,2},{4,5},{5,4},{6,7},{7,6},{8,9},{9,8},{10,11... | collective-permute-start | bytes 451592 | tf_op jit(solution)/shard_map/ppermute | solution.py:27
  30.8 5.3 %collective-permute-start.7 = (bf16[294,256]{1,0:T(8,128)(2,1)S(1)}, bf16[294,256]{1,0:T(8,128)(2,1)S(1)}, u32[]{:S(2)}, u32[]{:S(2)}) collective-permute-start(bf16[294,256]{1,0:T(8,128)(2,1)S(1)} %shard_map.100), channel_id=1, source_target_pairs={{0,1},{1,0},{2,3},{3,2},{4,5},{5,4},{6,7},{7,6},{8,9},{9,8},{10,11... | collective-permute-start | bytes 451592 | tf_op jit(solution)/shard_map/ppermute | solution.py:27

commit v12 on v11

--- a/solution.py
+++ b/solution.py
@@ -177,8 +177,9 @@
     weights = []
     for (w, _), score in zip(units, scores):
         same = jnp.concatenate([same_ref[w]] * GROUP, axis=0) != 0
-        score = jnp.where(same, score * HEAD_DIM ** (-0.5), -1000000000.0)
-        score = jnp.exp(score - jnp.max(score, axis=-1, keepdims=True))
+        score = jnp.where(same, score, -1000000000.0 * HEAD_DIM**0.5)
+        top = jnp.max(score, axis=-1, keepdims=True)
+        score = jnp.exp2((score - top) * (HEAD_DIM ** (-0.5) * 1.4426950408889634))
         total = jnp.sum(score, axis=-1, keepdims=True)
         weights.append((score.astype(jnp.bfloat16), 1.0 / total))
     parts = [[] for _ in range(HEADS // GROUP)]

time: 37.4 us -> 37.3 us (level)
  no operation moved by 1% of the time
where the time goes in v12:
time: 37.3 us; the launch traced here: 37.2 us
  starting transfers between devices  12.4 us (33%)
  waiting for transfers between devices  10.7 us (29%)
  Pallas kernels  9.73 us (26%)
  other arithmetic  2.38 us (6%)
  local copies, waits for them, and re-layouts  1.25 us (3%)
  between operations  0.71 us (2%)
    ppermute x3, starting transfers between devices, rotated(): lax.ppermute(block, axis, [(i, (i + distance) % devices) for i in range(d...  6.24 us
    ppermute x5, starting transfers between devices, exchanged(): return lax.ppermute(block, ('dp', 'seq'), pairs)  6.18 us
    ppermute x5, waiting for transfers between devices, exchanged(): return lax.ppermute(block, ('dp', 'seq'), pairs)  5.88 us
    pallas_call x1, Pallas kernels, local(): call(stage_kernel, [jax.ShapeDtypeStruct((rows, emb), jnp.bfloat16), jax....  5.09 us
    ppermute x3, waiting for transfers between devices, rotated(): lax.ppermute(block, axis, [(i, (i + distance) % devices) for i in range(d...  4.8 us
    pallas_call x1, Pallas kernels, local(): call(functools.partial(encode_kernel, blocks, band_rows), [jax.ShapeDtype...  3.39 us
    select_n x2, other arithmetic, by_page(): result = jnp.where(came, blocks[d][None], result)  2.29 us
    pallas_call x4, Pallas kernels, selected(): call(functools.partial(select_kernel, mine, first), [jax.ShapeDtypeStruct...  1.25 us
  transfers between devices with their start and end apart: 8, of which 7 were waited for; matrix products, arithmetic and copies ran while one was open for 4% of the time, Pallas kernels for 17%

profile of v12, /device:TPU:0, one launch (start us, length us, event | category | flops | bytes accessed | tf_op | source)
XLA Modules:
  0.0 37.2 jit_solution(6096477395019070404)
XLA Ops:
  0.6 0.0 copy-start
  0.6 1.0 %slice_bitcast_fusion = bf16[126,1024]{1,0:T(8,128)(2,1)S(1)} fusion(bf16[1,147,1024]{2,1,0:T(8,128)(2,1)} %pages_hbm.1), kind=kLoop, calls=%fused_computation.2 | loop fusion | bytes 516096 | tf_op jit(solution)/shard_map/squeeze | solution.py:277
  1.7 3.1 %collective-permute-start = (bf16[126,1024]{1,0:T(8,128)(2,1)S(1)}, bf16[126,1024]{1,0:T(8,128)(2,1)S(1)}, u32[]{:S(2)}, u32[]{:S(2)}) collective-permute-start(bf16[126,1024]{1,0:T(8,128)(2,1)S(1)} %slice_bitcast_fusion), channel_id=1, source_target_pairs={{0,2},{2,4},{4,6},{6,0},{1,3},{3,5},{5,7},{7,1},{8,10},{10,12},{12... | collective-permute-start | bytes 774152 | tf_op jit(solution)/shard_map/ppermute | solution.py:27
  4.8 0.0 copy-done
  4.8 0.2 reshape.22.order_ref
  5.0 0.1 pad_add_fusion.place
  5.1 5.1 %shard_map.95 = (bf16[160,1024]{1,0:T(8,128)(2,1)S(1)}, bf16[160,126]{1,0:T(8,128)(2,1)S(1)}, s32[3,56,64]{2,1,0:T(8,128)S(1)}, bf16[2,4,294,147]{3,2,1,0:T(8,12...) custom-call(s32[3]{0:T(128)S(1)} %pad_add_fusion.place, ...), custom_call_target="tpu_custom_call" | custom-call | flops 50000000 | bytes 8000000 | tf_op jit(solution)/shard_map/pallas_call | solution.py:283
  10.2 2.9 %collective-permute-done.halo_ref = bf16[126,1024]{1,0:T(8,128)(2,1)S(1)} collective-permute-done((bf16[126,1024]{1,0:T(8,128)(2,1)S(1)}, bf16[126,1024]{1,0:T(8,128)(2,1)S(1)}, u32[]{:S(2)}, u32[]{:S(2)}) %collective-permute-start) | collective-permute-done | bytes 258080 | tf_op jit(solution)/shard_map/ppermute | solution.py:27
  13.1 3.4 %shard_map.96 = (bf16[150,256]{1,0:T(8,128)(2,1)S(1)}, bf16[150,256]{1,0:T(8,128)(2,1)S(1)}, bf16[150,256]{1,0:T(8,128)(2,1)S(1)}, bf16[147,512]{1,0:T(8,128)(2,...) custom-call(s32[3]{0:T(128)S(1)} %pad_add_fusion.place, ...), custom_call_target="tpu_custom_call" | custom-call | flops 2000000000 | bytes 10000000 | tf_op jit(solution)/shard_map/pallas_call | solution.py:305
  16.5 0.1 collective-permute-start.3
  16.6 2.3 %collective-permute-start.1 = (bf16[150,256]{1,0:T(8,128)(2,1)S(1)}, bf16[150,256]{1,0:T(8,128)(2,1)S(1)}, u32[]{:S(2)}, u32[]{:S(2)}) collective-permute-start(bf16[150,256]{1,0:T(8,128)(2,1)S(1)} %get-tuple-element.31), channel_id=1, source_target_pairs={{0,4},{2,6},{4,0},{6,2},{8,10},{10,8},{12,14},{14,12},{16,20},{18,... | collective-permute-start | bytes 230408 | tf_op jit(solution)/shard_map/ppermute | solution.py:61
  18.8 2.1 %collective-permute-start.2 = (bf16[150,256]{1,0:T(8,128)(2,1)S(1)}, bf16[150,256]{1,0:T(8,128)(2,1)S(1)}, u32[]{:S(2)}, u32[]{:S(2)}) collective-permute-start(bf16[150,256]{1,0:T(8,128)(2,1)S(1)} %get-tuple-element.32), channel_id=1, source_target_pairs={{0,6},{2,4},{4,2},{6,0},{8,14},{10,12},{12,10},{14,8},{16,22},{18,... | collective-permute-start | bytes 230408 | tf_op jit(solution)/shard_map/ppermute | solution.py:61
  20.9 0.0 collective-permute-start.5
  20.9 1.7 %collective-permute-start.6 = (bf16[144,256]{1,0:T(8,128)(2,1)S(1)}, bf16[144,256]{1,0:T(8,128)(2,1)S(1)}, u32[]{:S(2)}, u32[]{:S(2)}) collective-permute-start(bf16[144,256]{1,0:T(8,128)(2,1)S(1)} %get-tuple-element.36), channel_id=1, source_target_pairs={{0,6},{2,4},{4,2},{6,0},{8,14},{10,12},{12,10},{14,8},{16,22},{18,... | collective-permute-start | bytes 221192 | tf_op jit(solution)/shard_map/ppermute | solution.py:61
  22.7 0.8 %collective-permute-done.1.refs_1_.refs_4_ = bf16[150,256]{1,0:T(8,128)(2,1)S(1)} collective-permute-done((bf16[150,256]{1,0:T(8,128)(2,1)S(1)}, bf16[150,256]{1,0:T(8,128)(2,1)S(1)}, u32[]{:S(2)}, u32[]{:S(2)}) %collective-permute-start.1) | collective-permute-done | bytes 76832 | tf_op jit(solution)/shard_map/ppermute | solution.py:61
  23.5 3.4 %collective-permute-done.2.refs_2_.refs_6_ = bf16[150,256]{1,0:T(8,128)(2,1)S(1)} collective-permute-done((bf16[150,256]{1,0:T(8,128)(2,1)S(1)}, bf16[150,256]{1,0:T(8,128)(2,1)S(1)}, u32[]{:S(2)}, u32[]{:S(2)}) %collective-permute-start.2) | collective-permute-done | bytes 76832 | tf_op jit(solution)/shard_map/ppermute | solution.py:61
  26.8 0.4 %collective-permute-done.3.refs_3_.refs_0_ = bf16[147,512]{1,0:T(8,128)(2,1)S(1)} collective-permute-done((bf16[147,512]{1,0:T(8,128)(2,1)S(1)}, bf16[147,512]{1,0:T(8,128)(2,1)S(1)}, u32[]{:S(2)}, u32[]{:S(2)}) %collective-permute-start.3) | collective-permute-done | bytes 150560 | tf_op jit(solution)/shard_map/ppermute | solution.py:61
  27.2 0.3 shard_map.97
  27.6 1.6 %collective-permute-start.4 = (bf16[294,256]{1,0:T(8,128)(2,1)S(1)}, bf16[294,256]{1,0:T(8,128)(2,1)S(1)}, u32[]{:S(2)}, u32[]{:S(2)}) collective-permute-start(bf16[294,256]{1,0:T(8,128)(2,1)S(1)} %shard_map.97), channel_id=1, source_target_pairs={{0,1},{1,0},{2,3},{3,2},{4,5},{5,4},{6,7},{7,6},{8,9},{9,8},{10,11... | collective-permute-start | bytes 451592 | tf_op jit(solution)/shard_map/ppermute | solution.py:27
  29.1 1.3 %collective-permute-done.5.refs_3_ = bf16[144,256]{1,0:T(8,128)(2,1)S(1)} collective-permute-done((bf16[144,256]{1,0:T(8,128)(2,1)S(1)}, bf16[144,256]{1,0:T(8,128)(2,1)S(1)}, u32[]{:S(2)}, u32[]{:S(2)}) %collective-permute-start.5) | collective-permute-done | bytes 73760 | tf_op jit(solution)/shard_map/ppermute | solution.py:61
  30.5 0.0 collective-permute-done.6.refs_5_
  30.5 0.3 shard_map.100
  30.8 1.6 %collective-permute-start.7 = (bf16[294,256]{1,0:T(8,128)(2,1)S(1)}, bf16[294,256]{1,0:T(8,128)(2,1)S(1)}, u32[]{:S(2)}, u32[]{:S(2)}) collective-permute-start(bf16[294,256]{1,0:T(8,128)(2,1)S(1)} %shard_map.100), channel_id=1, source_target_pairs={{0,1},{1,0},{2,3},{3,2},{4,5},{5,4},{6,7},{7,6},{8,9},{9,8},{10,11... | collective-permute-start | bytes 451592 | tf_op jit(solution)/shard_map/ppermute | solution.py:27
  32.4 0.3 shard_map.99
  32.7 0.3 shard_map.98
  33.0 0.1 collective-permute-done.4
  33.1 1.1 %broadcast_select_fusion.1 = bf16[2,294,256]{2,0,1:T(2,128)(2,1)} fusion(pred[2]{0:T(512)(128)(4,1)S(1)} %iota_compare_fusion, bf16[294,256]{1,0:T(8,128)(2,1)S(1)} %shard_map.98, bf16[294,256]{1,0:T(8,128)(2,1)S(1)} %collective-permute-done.4), kind=kLoop, calls=%fused_computation.1 | loop fusion | flops 150528 | bytes 602114 | tf_op jit(solution)/shard_map/jit(_where)/select_n | solution.py:338
  34.2 1.8 %collective-permute-done.7 = bf16[294,256]{1,0:T(8,128)(2,1)S(1)} collective-permute-done((bf16[294,256]{1,0:T(8,128)(2,1)S(1)}, bf16[294,256]{1,0:T(8,128)(2,1)S(1)}, u32[]{:S(2)}, u32[]{:S(2)}) %collective-permute-start.7) | collective-permute-done | bytes 150560 | tf_op jit(solution)/shard_map/ppermute | solution.py:27
  36.0 1.1 %broadcast_select_fusion = bf16[2,294,256]{2,0,1:T(2,128)(2,1)} fusion(pred[2]{0:T(512)(128)(4,1)S(1)} %iota_compare_fusion, bf16[294,256]{1,0:T(8,128)(2,1)S(1)} %shard_map.99, bf16[294,256]{1,0:T(8,128)(2,1)S(1)} %collective-permute-done.7), kind=kLoop, calls=%fused_computation | loop fusion | flops 150528 | bytes 602114 | tf_op jit(solution)/shard_map/jit(_where)/select_n | solution.py:338
  (2 shorter events, 0.0 us)
Async XLA Ops:
  0.6 4.1 %copy-start = (s32[2,588]{1,0:T(2,128)S(1)}, s32[2,588]{1,0:T(2,128)}, u32[]{:S(2)}) copy-start(s32[2,588]{1,0:T(2,128)} %param.15) | copy-start | bytes 14116
  1.7 11.4 %collective-permute-start = (bf16[126,1024]{1,0:T(8,128)(2,1)S(1)}, bf16[126,1024]{1,0:T(8,128)(2,1)S(1)}, u32[]{:S(2)}, u32[]{:S(2)}) collective-permute-start(bf16[126,1024]{1,0:T(8,128)(2,1)S(1)} %slice_bitcast_fusion), channel_id=1, source_target_pairs={{0,2},{2,4},{4,6},{6,0},{1,3},{3,5},{5,7},{7,1},{8,10},{10,12},{12... | collective-permute-start | bytes 774152 | tf_op jit(solution)/shard_map/ppermute | solution.py:27
  16.5 10.8 %collective-permute-start.3 = (bf16[147,512]{1,0:T(8,128)(2,1)S(1)}, bf16[147,512]{1,0:T(8,128)(2,1)S(1)}, u32[]{:S(2)}, u32[]{:S(2)}) collective-permute-start(bf16[147,512]{1,0:T(8,128)(2,1)S(1)} %get-tuple-element.33), channel_id=1, source_target_pairs={{0,2},{2,0},{4,6},{6,4},{8,12},{10,14},{12,8},{14,10},{16,18},{18,... | collective-permute-start | bytes 451592 | tf_op jit(solution)/shard_map/ppermute | solution.py:61
  16.6 6.9 %collective-permute-start.1 = (bf16[150,256]{1,0:T(8,128)(2,1)S(1)}, bf16[150,256]{1,0:T(8,128)(2,1)S(1)}, u32[]{:S(2)}, u32[]{:S(2)}) collective-permute-start(bf16[150,256]{1,0:T(8,128)(2,1)S(1)} %get-tuple-element.31), channel_id=1, source_target_pairs={{0,4},{2,6},{4,0},{6,2},{8,10},{10,8},{12,14},{14,12},{16,20},{18,... | collective-permute-start | bytes 230408 | tf_op jit(solution)/shard_map/ppermute | solution.py:61
  18.8 8.0 %collective-permute-start.2 = (bf16[150,256]{1,0:T(8,128)(2,1)S(1)}, bf16[150,256]{1,0:T(8,128)(2,1)S(1)}, u32[]{:S(2)}, u32[]{:S(2)}) collective-permute-start(bf16[150,256]{1,0:T(8,128)(2,1)S(1)} %get-tuple-element.32), channel_id=1, source_target_pairs={{0,6},{2,4},{4,2},{6,0},{8,14},{10,12},{12,10},{14,8},{16,22},{18,... | collective-permute-start | bytes 230408 | tf_op jit(solution)/shard_map/ppermute | solution.py:61
  20.9 9.5 %collective-permute-start.5 = (bf16[144,256]{1,0:T(8,128)(2,1)S(1)}, bf16[144,256]{1,0:T(8,128)(2,1)S(1)}, u32[]{:S(2)}, u32[]{:S(2)}) collective-permute-start(bf16[144,256]{1,0:T(8,128)(2,1)S(1)} %get-tuple-element.35), channel_id=1, source_target_pairs={{0,4},{2,6},{4,0},{6,2},{8,10},{10,8},{12,14},{14,12},{16,20},{18,... | collective-permute-start | bytes 221192 | tf_op jit(solution)/shard_map/ppermute | solution.py:61
  20.9 9.5 %collective-permute-start.6 = (bf16[144,256]{1,0:T(8,128)(2,1)S(1)}, bf16[144,256]{1,0:T(8,128)(2,1)S(1)}, u32[]{:S(2)}, u32[]{:S(2)}) collective-permute-start(bf16[144,256]{1,0:T(8,128)(2,1)S(1)} %get-tuple-element.36), channel_id=1, source_target_pairs={{0,6},{2,4},{4,2},{6,0},{8,14},{10,12},{12,10},{14,8},{16,22},{18,... | collective-permute-start | bytes 221192 | tf_op jit(solution)/shard_map/ppermute | solution.py:61
  27.6 5.5 %collective-permute-start.4 = (bf16[294,256]{1,0:T(8,128)(2,1)S(1)}, bf16[294,256]{1,0:T(8,128)(2,1)S(1)}, u32[]{:S(2)}, u32[]{:S(2)}) collective-permute-start(bf16[294,256]{1,0:T(8,128)(2,1)S(1)} %shard_map.97), channel_id=1, source_target_pairs={{0,1},{1,0},{2,3},{3,2},{4,5},{5,4},{6,7},{7,6},{8,9},{9,8},{10,11... | collective-permute-start | bytes 451592 | tf_op jit(solution)/shard_map/ppermute | solution.py:27
  30.8 5.3 %collective-permute-start.7 = (bf16[294,256]{1,0:T(8,128)(2,1)S(1)}, bf16[294,256]{1,0:T(8,128)(2,1)S(1)}, u32[]{:S(2)}, u32[]{:S(2)}) collective-permute-start(bf16[294,256]{1,0:T(8,128)(2,1)S(1)} %shard_map.100), channel_id=1, source_target_pairs={{0,1},{1,0},{2,3},{3,2},{4,5},{5,4},{6,7},{7,6},{8,9},{9,8},{10,11... | collective-permute-start | bytes 451592 | tf_op jit(solution)/shard_map/ppermute | solution.py:27
